TPU v7x, 512 devices: a whole 4x8x8 slice. The times are simulated.
512 devices in a mesh: row: 32 (over x_lo, z, core), blk: 16 (over x_hi, y).
Axes of the slice: x: 4 (x_hi: 2, x_lo: 2; x = x_hi * 2 + x_lo), y: 8, z: 8, core: 2. Of those that a mesh axis runs over, the one named last changes fastest.
Arguments:
- queries: bfloat16 [128, 2048, 128], P('row', 'blk'), may hold values from -6 to 6
- keys: bfloat16 [128, 2048, 128], P('row', 'blk'), may hold values from -6 to 6
- values: bfloat16 [128, 2048, 128], P('row', 'blk'), may hold values from -6 to 6
- bias: bfloat16 [4, 2048, 2048], P(None, 'blk'), may hold values from -6 to 6
- out_grad: bfloat16 [128, 2048, 128], P('row', 'blk'), may hold values from -48 to 48
- outputs: bfloat16 [128, 2048, 128], P('row', 'blk'), may hold values from -1.5 to 1.5
- logsumexp: float32 [128, 4, 2048], P('row', None, 'blk'), may hold values from 8 to 9.5
Outputs:
- query_grad: bfloat16 [128, 2048, 128], P('row', 'blk')
- key_grad: bfloat16 [128, 2048, 128], P('row', 'blk')
- value_grad: bfloat16 [128, 2048, 128], P('row', 'blk')
- bias_grad: float32 [4, 2048, 2048], P(None, 'blk', 'row')
All inputs are finite; a program needn't handle non-finite values.
Results may differ from a plain program's by a relative error of at most 0.0049.
Values may be sent and summed in bfloat16 or wider, within the bound.
No kernel may reach another device: no remote copies, remote signals or barrier semaphores. Data moves between devices by JAX's collectives and lax.ppermute only.
A program may use at most 64 MiB of HBM per device.

v0:
```python
import jax
import jax.numpy as jnp
from jax import lax
from jax.sharding import PartitionSpec as P


def passed_along(value, axis, steps):
    count = lax.axis_size(axis)
    pairs = [(source, (source + steps) % count) for source in range(count)]
    return lax.ppermute(value, axis, pairs)


def body(queries, keys, values, bias, out_grad, outputs, logsumexp):
    rows, nodes, width = queries.shape
    heads = bias.shape[0]
    head_dim = width // heads
    scale = head_dim ** (-0.5)
    blocks = lax.axis_size("blk")
    mine = lax.axis_index("blk")
    query_four = queries.reshape(rows, nodes, heads, head_dim)
    grad_four = out_grad.reshape(rows, nodes, heads, head_dim)
    output_four = outputs.reshape(rows, nodes, heads, head_dim)
    delta = jnp.sum(grad_four.astype(jnp.float32) * output_four.astype(jnp.float32), axis=-1)
    delta = jnp.transpose(delta, (0, 2, 1))

    def contribute(key_block, value_block, column):
        count = key_block.shape[1]
        key_four = key_block.reshape(rows, count, heads, head_dim)
        value_four = value_block.reshape(rows, count, heads, head_dim)
        bias_block = lax.dynamic_slice_in_dim(bias, column, count, 2).astype(jnp.float32)
        scores = (
            jnp.einsum("rjhd,rkhd->rhjk", query_four, key_four, preferred_element_type=jnp.float32)
            * scale
            + bias_block[None]
        )
        probs = jnp.exp(scores - logsumexp[:, :, :, None])
        probs_low = probs.astype(jnp.bfloat16)
        value_part = jnp.einsum(
            "rhjk,rjhd->rkhd", probs_low, grad_four, preferred_element_type=jnp.float32
        ).reshape(rows, count, width)
        prob_grad = jnp.einsum(
            "rjhd,rkhd->rhjk", grad_four, value_four, preferred_element_type=jnp.float32
        )
        score_grad = probs * (prob_grad - delta[:, :, :, None])
        score_low = score_grad.astype(jnp.bfloat16)
        query_part = (
            jnp.einsum("rhjk,rkhd->rjhd", score_low, key_four, preferred_element_type=jnp.float32)
            * scale
        )
        key_part = (
            jnp.einsum(
                "rhjk,rjhd->rkhd", score_low, query_four, preferred_element_type=jnp.float32
            ).reshape(rows, count, width)
            * scale
        )
        return (query_part, key_part, value_part, jnp.sum(score_grad, axis=0))

    def add_bias(table, part, column):
        current = lax.dynamic_slice_in_dim(table, column, part.shape[2], 2)
        return lax.dynamic_update_slice_in_dim(table, current + part, column, 2)

    query_start = jnp.zeros((rows, nodes, heads, head_dim), jnp.float32)
    table_start = jnp.zeros((heads, nodes, blocks * nodes), jnp.float32)

    def one_step(step, state):
        key_block, value_block, key_acc, value_acc, query_acc, table = state
        source = (mine - step) % blocks
        column = source * nodes
        query_part, key_part, value_part, bias_part = contribute(key_block, value_block, column)
        table = add_bias(table, bias_part, column)
        key_block, value_block = passed_along((key_block, value_block), "blk", 1)
        key_acc, value_acc = passed_along((key_acc + key_part, value_acc + value_part), "blk", 1)
        return (key_block, value_block, key_acc, value_acc, query_acc + query_part, table)

    zeros_grad = jnp.zeros((rows, nodes, width), jnp.float32)
    state = (keys, values, zeros_grad, zeros_grad, query_start, table_start)
    state = lax.fori_loop(0, blocks, one_step, state)
    key_total, value_total, query_total, table = (state[2], state[3], state[4], state[5])
    bias_grad = lax.psum_scatter(table, "row", scatter_dimension=2, tiled=True)
    query_grad = query_total.reshape(rows, nodes, width).astype(jnp.bfloat16)
    return (query_grad, key_total.astype(jnp.bfloat16), value_total.astype(jnp.bfloat16), bias_grad)


def solution(mesh):
    in_specs = (
        P("row", "blk", None),
        P("row", "blk", None),
        P("row", "blk", None),
        P(None, "blk", None),
        P("row", "blk", None),
        P("row", "blk", None),
        P("row", None, "blk"),
    )
    out_specs = (
        P("row", "blk", None),
        P("row", "blk", None),
        P("row", "blk", None),
        P(None, "blk", "row"),
    )
    return jax.shard_map(body, mesh=mesh, in_specs=in_specs, out_specs=out_specs, check_vma=False)
```

profile of v0, /device:TPU:1, one launch (start us, length us, event | category | flops | bytes accessed | tf_op | source)
XLA Modules:
  0.0 527.6 jit_solution(18206636449441322475)
XLA Ops:
  14.7 382.1 %while.26 = (s32[]{:T(128)}, bf16[4,128,128]{1,2,0:T(8,128)(2,1)S(1)}, bf16[4,128,128]{1,2,0:T(8,128)(2,1)S(1)}, f32[4,128,128]{1,2,0:T(8,128)S(1)}, f32[4,128,1...) while((s32[]{:T(128)}, ...), condition=%wide.region_3.4_spmd.clone, body=%wide.region_1.3_spmd.clone.sunk | while | flops 86442000 | bytes 15745546 | solution.py:77
  14.7 4.0 collective-permute-start
  28.0 4.4 collective-permute-start.3
  36.1 5.6 %collective-permute-done.3 = f32[4,128,128]{1,2,0:T(8,128)S(1)} collective-permute-done((f32[4,128,128]{1,2,0:T(8,128)S(1)}, f32[4,128,128]{1,2,0:T(8,128)S(1)}, u32[]{:S(2)}, u32[]{:S(2)}) %collective-permute-start.3) | collective-permute-done | bytes 262176 | tf_op jit(solution)/shard_map/while/body/eval_jaxpr/ppermute | solution.py:10
  59.8 5.6 %collective-permute-done.3 = f32[4,128,128]{1,2,0:T(8,128)S(1)} collective-permute-done((f32[4,128,128]{1,2,0:T(8,128)S(1)}, f32[4,128,128]{1,2,0:T(8,128)S(1)}, u32[]{:S(2)}, u32[]{:S(2)}) %collective-permute-start.3) | collective-permute-done | bytes 262176 | tf_op jit(solution)/shard_map/while/body/eval_jaxpr/ppermute | solution.py:10
  83.5 5.6 %collective-permute-done.3 = f32[4,128,128]{1,2,0:T(8,128)S(1)} collective-permute-done((f32[4,128,128]{1,2,0:T(8,128)S(1)}, f32[4,128,128]{1,2,0:T(8,128)S(1)}, u32[]{:S(2)}, u32[]{:S(2)}) %collective-permute-start.3) | collective-permute-done | bytes 262176 | tf_op jit(solution)/shard_map/while/body/eval_jaxpr/ppermute | solution.py:10
  102.6 4.6 collective-permute-done.2
  107.1 5.6 %collective-permute-done.3 = f32[4,128,128]{1,2,0:T(8,128)S(1)} collective-permute-done((f32[4,128,128]{1,2,0:T(8,128)S(1)}, f32[4,128,128]{1,2,0:T(8,128)S(1)}, u32[]{:S(2)}, u32[]{:S(2)}) %collective-permute-start.3) | collective-permute-done | bytes 262176 | tf_op jit(solution)/shard_map/while/body/eval_jaxpr/ppermute | solution.py:10
  130.8 5.6 %collective-permute-done.3 = f32[4,128,128]{1,2,0:T(8,128)S(1)} collective-permute-done((f32[4,128,128]{1,2,0:T(8,128)S(1)}, f32[4,128,128]{1,2,0:T(8,128)S(1)}, u32[]{:S(2)}, u32[]{:S(2)}) %collective-permute-start.3) | collective-permute-done | bytes 262176 | tf_op jit(solution)/shard_map/while/body/eval_jaxpr/ppermute | solution.py:10
  150.4 4.1 collective-permute-done.2
  154.5 5.6 %collective-permute-done.3 = f32[4,128,128]{1,2,0:T(8,128)S(1)} collective-permute-done((f32[4,128,128]{1,2,0:T(8,128)S(1)}, f32[4,128,128]{1,2,0:T(8,128)S(1)}, u32[]{:S(2)}, u32[]{:S(2)}) %collective-permute-start.3) | collective-permute-done | bytes 262176 | tf_op jit(solution)/shard_map/while/body/eval_jaxpr/ppermute | solution.py:10
  174.1 4.1 collective-permute-done.2
  178.2 5.6 %collective-permute-done.3 = f32[4,128,128]{1,2,0:T(8,128)S(1)} collective-permute-done((f32[4,128,128]{1,2,0:T(8,128)S(1)}, f32[4,128,128]{1,2,0:T(8,128)S(1)}, u32[]{:S(2)}, u32[]{:S(2)}) %collective-permute-start.3) | collective-permute-done | bytes 262176 | tf_op jit(solution)/shard_map/while/body/eval_jaxpr/ppermute | solution.py:10
  197.7 4.1 collective-permute-done.2
  201.8 5.6 %collective-permute-done.3 = f32[4,128,128]{1,2,0:T(8,128)S(1)} collective-permute-done((f32[4,128,128]{1,2,0:T(8,128)S(1)}, f32[4,128,128]{1,2,0:T(8,128)S(1)}, u32[]{:S(2)}, u32[]{:S(2)}) %collective-permute-start.3) | collective-permute-done | bytes 262176 | tf_op jit(solution)/shard_map/while/body/eval_jaxpr/ppermute | solution.py:10
  221.4 4.1 collective-permute-done.2
  225.5 5.6 %collective-permute-done.3 = f32[4,128,128]{1,2,0:T(8,128)S(1)} collective-permute-done((f32[4,128,128]{1,2,0:T(8,128)S(1)}, f32[4,128,128]{1,2,0:T(8,128)S(1)}, u32[]{:S(2)}, u32[]{:S(2)}) %collective-permute-start.3) | collective-permute-done | bytes 262176 | tf_op jit(solution)/shard_map/while/body/eval_jaxpr/ppermute | solution.py:10
  245.1 4.1 collective-permute-done.2
  249.2 5.6 %collective-permute-done.3 = f32[4,128,128]{1,2,0:T(8,128)S(1)} collective-permute-done((f32[4,128,128]{1,2,0:T(8,128)S(1)}, f32[4,128,128]{1,2,0:T(8,128)S(1)}, u32[]{:S(2)}, u32[]{:S(2)}) %collective-permute-start.3) | collective-permute-done | bytes 262176 | tf_op jit(solution)/shard_map/while/body/eval_jaxpr/ppermute | solution.py:10
  268.8 4.1 collective-permute-done.2
  272.8 5.6 %collective-permute-done.3 = f32[4,128,128]{1,2,0:T(8,128)S(1)} collective-permute-done((f32[4,128,128]{1,2,0:T(8,128)S(1)}, f32[4,128,128]{1,2,0:T(8,128)S(1)}, u32[]{:S(2)}, u32[]{:S(2)}) %collective-permute-start.3) | collective-permute-done | bytes 262176 | tf_op jit(solution)/shard_map/while/body/eval_jaxpr/ppermute | solution.py:10
  292.4 4.1 collective-permute-done.2
  296.5 5.6 %collective-permute-done.3 = f32[4,128,128]{1,2,0:T(8,128)S(1)} collective-permute-done((f32[4,128,128]{1,2,0:T(8,128)S(1)}, f32[4,128,128]{1,2,0:T(8,128)S(1)}, u32[]{:S(2)}, u32[]{:S(2)}) %collective-permute-start.3) | collective-permute-done | bytes 262176 | tf_op jit(solution)/shard_map/while/body/eval_jaxpr/ppermute | solution.py:10
  316.1 4.1 collective-permute-done.2
  320.2 5.6 %collective-permute-done.3 = f32[4,128,128]{1,2,0:T(8,128)S(1)} collective-permute-done((f32[4,128,128]{1,2,0:T(8,128)S(1)}, f32[4,128,128]{1,2,0:T(8,128)S(1)}, u32[]{:S(2)}, u32[]{:S(2)}) %collective-permute-start.3) | collective-permute-done | bytes 262176 | tf_op jit(solution)/shard_map/while/body/eval_jaxpr/ppermute | solution.py:10
  339.8 4.1 collective-permute-done.2
  343.9 5.6 %collective-permute-done.3 = f32[4,128,128]{1,2,0:T(8,128)S(1)} collective-permute-done((f32[4,128,128]{1,2,0:T(8,128)S(1)}, f32[4,128,128]{1,2,0:T(8,128)S(1)}, u32[]{:S(2)}, u32[]{:S(2)}) %collective-permute-start.3) | collective-permute-done | bytes 262176 | tf_op jit(solution)/shard_map/while/body/eval_jaxpr/ppermute | solution.py:10
  363.4 4.1 collective-permute-done.2
  367.5 5.6 %collective-permute-done.3 = f32[4,128,128]{1,2,0:T(8,128)S(1)} collective-permute-done((f32[4,128,128]{1,2,0:T(8,128)S(1)}, f32[4,128,128]{1,2,0:T(8,128)S(1)}, u32[]{:S(2)}, u32[]{:S(2)}) %collective-permute-start.3) | collective-permute-done | bytes 262176 | tf_op jit(solution)/shard_map/while/body/eval_jaxpr/ppermute | solution.py:10
  387.1 4.1 collective-permute-done.2
  391.2 5.6 %collective-permute-done.3 = f32[4,128,128]{1,2,0:T(8,128)S(1)} collective-permute-done((f32[4,128,128]{1,2,0:T(8,128)S(1)}, f32[4,128,128]{1,2,0:T(8,128)S(1)}, u32[]{:S(2)}, u32[]{:S(2)}) %collective-permute-start.3) | collective-permute-done | bytes 262176 | tf_op jit(solution)/shard_map/while/body/eval_jaxpr/ppermute | solution.py:10
  399.2 121.6 %reduce-scatter.2.cloned.1.call-done = f32[4,128,64]{1,2,0:T(8,128)} async-done(((f32[4,128,2048]{1,2,0:T(8,128)}), f32[4,128,64]{1,2,0:T(8,128)}) %reduce-scatter.2.cloned.1.call-update) | async-done | bytes 131088 | tf_op jit(solution)/shard_map/reduce_scatter | solution.py:79
  (356 shorter events, 241.6 us)
Async XLA Ops:
  7.2 513.6 %reduce-scatter.2.cloned.1.call-start = ((), (), s32[]{:S(2)}) async-start(), calls=%async_computation.1 | async-start | bytes 4325376 | tf_op jit(solution)/shard_map/reduce_scatter | solution.py:79
  14.7 20.1 %collective-permute-start = (bf16[4,128,128]{1,2,0:T(8,128)(2,1)S(1)}, bf16[4,128,128]{1,2,0:T(8,128)(2,1)S(1)}, u32[]{:S(2)}, u32[]{:S(2)}) collective-permute-start(bf16[4,128,128]{1,2,0:T(8,128)(2,1)S(1)} %copy.46), channel_id=1, source_target_pairs={{0,1},{1,2},{2,3},{3,4},{4,5},{5,6},{6,7},{7,8},{8,9},{9,10},{10,1... | collective-permute-start | bytes 393224 | tf_op jit(solution)/shard_map/while/body/eval_jaxpr/ppermute | solution.py:10
  18.8 16.0 %collective-permute-start.1 = (bf16[4,128,128]{1,2,0:T(8,128)(2,1)S(1)}, bf16[4,128,128]{1,2,0:T(8,128)(2,1)S(1)}, u32[]{:S(2)}, u32[]{:S(2)}) collective-permute-start(bf16[4,128,128]{1,2,0:T(8,128)(2,1)S(1)} %copy.47), channel_id=1, source_target_pairs={{0,1},{1,2},{2,3},{3,4},{4,5},{5,6},{6,7},{7,8},{8,9},{9,10},{10,1... | collective-permute-start | bytes 393224 | tf_op jit(solution)/shard_map/while/body/eval_jaxpr/ppermute | solution.py:10
  41.8 15.5 %collective-permute-start = (bf16[4,128,128]{1,2,0:T(8,128)(2,1)S(1)}, bf16[4,128,128]{1,2,0:T(8,128)(2,1)S(1)}, u32[]{:S(2)}, u32[]{:S(2)}) collective-permute-start(bf16[4,128,128]{1,2,0:T(8,128)(2,1)S(1)} %copy.46), channel_id=1, source_target_pairs={{0,1},{1,2},{2,3},{3,4},{4,5},{5,6},{6,7},{7,8},{8,9},{9,10},{10,1... | collective-permute-start | bytes 393224 | tf_op jit(solution)/shard_map/while/body/eval_jaxpr/ppermute | solution.py:10
  51.3 14.1 %collective-permute-start.3 = (f32[4,128,128]{1,2,0:T(8,128)S(1)}, f32[4,128,128]{1,2,0:T(8,128)S(1)}, u32[]{:S(2)}, u32[]{:S(2)}) collective-permute-start(f32[4,128,128]{1,2,0:T(8,128)S(1)} %bitcast_add_fusion.5), channel_id=1, source_target_pairs={{0,1},{1,2},{2,3},{3,4},{4,5},{5,6},{6,7},{7,8},{8,9},{9,10},{10,1... | collective-permute-start | bytes 786440 | tf_op jit(solution)/shard_map/while/body/eval_jaxpr/ppermute | solution.py:10
  65.5 14.2 %collective-permute-start = (bf16[4,128,128]{1,2,0:T(8,128)(2,1)S(1)}, bf16[4,128,128]{1,2,0:T(8,128)(2,1)S(1)}, u32[]{:S(2)}, u32[]{:S(2)}) collective-permute-start(bf16[4,128,128]{1,2,0:T(8,128)(2,1)S(1)} %copy.46), channel_id=1, source_target_pairs={{0,1},{1,2},{2,3},{3,4},{4,5},{5,6},{6,7},{7,8},{8,9},{9,10},{10,1... | collective-permute-start | bytes 393224 | tf_op jit(solution)/shard_map/while/body/eval_jaxpr/ppermute | solution.py:10
  74.0 15.1 %collective-permute-start.3 = (f32[4,128,128]{1,2,0:T(8,128)S(1)}, f32[4,128,128]{1,2,0:T(8,128)S(1)}, u32[]{:S(2)}, u32[]{:S(2)}) collective-permute-start(f32[4,128,128]{1,2,0:T(8,128)S(1)} %bitcast_add_fusion.5), channel_id=1, source_target_pairs={{0,1},{1,2},{2,3},{3,4},{4,5},{5,6},{6,7},{7,8},{8,9},{9,10},{10,1... | collective-permute-start | bytes 786440 | tf_op jit(solution)/shard_map/while/body/eval_jaxpr/ppermute | solution.py:10
  97.7 15.0 %collective-permute-start.3 = (f32[4,128,128]{1,2,0:T(8,128)S(1)}, f32[4,128,128]{1,2,0:T(8,128)S(1)}, u32[]{:S(2)}, u32[]{:S(2)}) collective-permute-start(f32[4,128,128]{1,2,0:T(8,128)S(1)} %bitcast_add_fusion.5), channel_id=1, source_target_pairs={{0,1},{1,2},{2,3},{3,4},{4,5},{5,6},{6,7},{7,8},{8,9},{9,10},{10,1... | collective-permute-start | bytes 786440 | tf_op jit(solution)/shard_map/while/body/eval_jaxpr/ppermute | solution.py:10
  112.8 14.1 %collective-permute-start = (bf16[4,128,128]{1,2,0:T(8,128)(2,1)S(1)}, bf16[4,128,128]{1,2,0:T(8,128)(2,1)S(1)}, u32[]{:S(2)}, u32[]{:S(2)}) collective-permute-start(bf16[4,128,128]{1,2,0:T(8,128)(2,1)S(1)} %copy.46), channel_id=1, source_target_pairs={{0,1},{1,2},{2,3},{3,4},{4,5},{5,6},{6,7},{7,8},{8,9},{9,10},{10,1... | collective-permute-start | bytes 393224 | tf_op jit(solution)/shard_map/while/body/eval_jaxpr/ppermute | solution.py:10
  121.4 15.1 %collective-permute-start.3 = (f32[4,128,128]{1,2,0:T(8,128)S(1)}, f32[4,128,128]{1,2,0:T(8,128)S(1)}, u32[]{:S(2)}, u32[]{:S(2)}) collective-permute-start(f32[4,128,128]{1,2,0:T(8,128)S(1)} %bitcast_add_fusion.5), channel_id=1, source_target_pairs={{0,1},{1,2},{2,3},{3,4},{4,5},{5,6},{6,7},{7,8},{8,9},{9,10},{10,1... | collective-permute-start | bytes 786440 | tf_op jit(solution)/shard_map/while/body/eval_jaxpr/ppermute | solution.py:10
  136.5 13.9 %collective-permute-start = (bf16[4,128,128]{1,2,0:T(8,128)(2,1)S(1)}, bf16[4,128,128]{1,2,0:T(8,128)(2,1)S(1)}, u32[]{:S(2)}, u32[]{:S(2)}) collective-permute-start(bf16[4,128,128]{1,2,0:T(8,128)(2,1)S(1)} %copy.46), channel_id=1, source_target_pairs={{0,1},{1,2},{2,3},{3,4},{4,5},{5,6},{6,7},{7,8},{8,9},{9,10},{10,1... | collective-permute-start | bytes 393224 | tf_op jit(solution)/shard_map/while/body/eval_jaxpr/ppermute | solution.py:10
  145.1 15.1 %collective-permute-start.3 = (f32[4,128,128]{1,2,0:T(8,128)S(1)}, f32[4,128,128]{1,2,0:T(8,128)S(1)}, u32[]{:S(2)}, u32[]{:S(2)}) collective-permute-start(f32[4,128,128]{1,2,0:T(8,128)S(1)} %bitcast_add_fusion.5), channel_id=1, source_target_pairs={{0,1},{1,2},{2,3},{3,4},{4,5},{5,6},{6,7},{7,8},{8,9},{9,10},{10,1... | collective-permute-start | bytes 786440 | tf_op jit(solution)/shard_map/while/body/eval_jaxpr/ppermute | solution.py:10
  160.1 13.9 %collective-permute-start = (bf16[4,128,128]{1,2,0:T(8,128)(2,1)S(1)}, bf16[4,128,128]{1,2,0:T(8,128)(2,1)S(1)}, u32[]{:S(2)}, u32[]{:S(2)}) collective-permute-start(bf16[4,128,128]{1,2,0:T(8,128)(2,1)S(1)} %copy.46), channel_id=1, source_target_pairs={{0,1},{1,2},{2,3},{3,4},{4,5},{5,6},{6,7},{7,8},{8,9},{9,10},{10,1... | collective-permute-start | bytes 393224 | tf_op jit(solution)/shard_map/while/body/eval_jaxpr/ppermute | solution.py:10
  168.7 15.1 %collective-permute-start.3 = (f32[4,128,128]{1,2,0:T(8,128)S(1)}, f32[4,128,128]{1,2,0:T(8,128)S(1)}, u32[]{:S(2)}, u32[]{:S(2)}) collective-permute-start(f32[4,128,128]{1,2,0:T(8,128)S(1)} %bitcast_add_fusion.5), channel_id=1, source_target_pairs={{0,1},{1,2},{2,3},{3,4},{4,5},{5,6},{6,7},{7,8},{8,9},{9,10},{10,1... | collective-permute-start | bytes 786440 | tf_op jit(solution)/shard_map/while/body/eval_jaxpr/ppermute | solution.py:10
  183.8 13.9 %collective-permute-start = (bf16[4,128,128]{1,2,0:T(8,128)(2,1)S(1)}, bf16[4,128,128]{1,2,0:T(8,128)(2,1)S(1)}, u32[]{:S(2)}, u32[]{:S(2)}) collective-permute-start(bf16[4,128,128]{1,2,0:T(8,128)(2,1)S(1)} %copy.46), channel_id=1, source_target_pairs={{0,1},{1,2},{2,3},{3,4},{4,5},{5,6},{6,7},{7,8},{8,9},{9,10},{10,1... | collective-permute-start | bytes 393224 | tf_op jit(solution)/shard_map/while/body/eval_jaxpr/ppermute | solution.py:10
  192.4 15.1 %collective-permute-start.3 = (f32[4,128,128]{1,2,0:T(8,128)S(1)}, f32[4,128,128]{1,2,0:T(8,128)S(1)}, u32[]{:S(2)}, u32[]{:S(2)}) collective-permute-start(f32[4,128,128]{1,2,0:T(8,128)S(1)} %bitcast_add_fusion.5), channel_id=1, source_target_pairs={{0,1},{1,2},{2,3},{3,4},{4,5},{5,6},{6,7},{7,8},{8,9},{9,10},{10,1... | collective-permute-start | bytes 786440 | tf_op jit(solution)/shard_map/while/body/eval_jaxpr/ppermute | solution.py:10
  207.5 13.9 %collective-permute-start = (bf16[4,128,128]{1,2,0:T(8,128)(2,1)S(1)}, bf16[4,128,128]{1,2,0:T(8,128)(2,1)S(1)}, u32[]{:S(2)}, u32[]{:S(2)}) collective-permute-start(bf16[4,128,128]{1,2,0:T(8,128)(2,1)S(1)} %copy.46), channel_id=1, source_target_pairs={{0,1},{1,2},{2,3},{3,4},{4,5},{5,6},{6,7},{7,8},{8,9},{9,10},{10,1... | collective-permute-start | bytes 393224 | tf_op jit(solution)/shard_map/while/body/eval_jaxpr/ppermute | solution.py:10
  216.1 15.1 %collective-permute-start.3 = (f32[4,128,128]{1,2,0:T(8,128)S(1)}, f32[4,128,128]{1,2,0:T(8,128)S(1)}, u32[]{:S(2)}, u32[]{:S(2)}) collective-permute-start(f32[4,128,128]{1,2,0:T(8,128)S(1)} %bitcast_add_fusion.5), channel_id=1, source_target_pairs={{0,1},{1,2},{2,3},{3,4},{4,5},{5,6},{6,7},{7,8},{8,9},{9,10},{10,1... | collective-permute-start | bytes 786440 | tf_op jit(solution)/shard_map/while/body/eval_jaxpr/ppermute | solution.py:10
  231.1 13.9 %collective-permute-start = (bf16[4,128,128]{1,2,0:T(8,128)(2,1)S(1)}, bf16[4,128,128]{1,2,0:T(8,128)(2,1)S(1)}, u32[]{:S(2)}, u32[]{:S(2)}) collective-permute-start(bf16[4,128,128]{1,2,0:T(8,128)(2,1)S(1)} %copy.46), channel_id=1, source_target_pairs={{0,1},{1,2},{2,3},{3,4},{4,5},{5,6},{6,7},{7,8},{8,9},{9,10},{10,1... | collective-permute-start | bytes 393224 | tf_op jit(solution)/shard_map/while/body/eval_jaxpr/ppermute | solution.py:10
  239.7 15.1 %collective-permute-start.3 = (f32[4,128,128]{1,2,0:T(8,128)S(1)}, f32[4,128,128]{1,2,0:T(8,128)S(1)}, u32[]{:S(2)}, u32[]{:S(2)}) collective-permute-start(f32[4,128,128]{1,2,0:T(8,128)S(1)} %bitcast_add_fusion.5), channel_id=1, source_target_pairs={{0,1},{1,2},{2,3},{3,4},{4,5},{5,6},{6,7},{7,8},{8,9},{9,10},{10,1... | collective-permute-start | bytes 786440 | tf_op jit(solution)/shard_map/while/body/eval_jaxpr/ppermute | solution.py:10
  254.8 13.9 %collective-permute-start = (bf16[4,128,128]{1,2,0:T(8,128)(2,1)S(1)}, bf16[4,128,128]{1,2,0:T(8,128)(2,1)S(1)}, u32[]{:S(2)}, u32[]{:S(2)}) collective-permute-start(bf16[4,128,128]{1,2,0:T(8,128)(2,1)S(1)} %copy.46), channel_id=1, source_target_pairs={{0,1},{1,2},{2,3},{3,4},{4,5},{5,6},{6,7},{7,8},{8,9},{9,10},{10,1... | collective-permute-start | bytes 393224 | tf_op jit(solution)/shard_map/while/body/eval_jaxpr/ppermute | solution.py:10
  263.4 15.1 %collective-permute-start.3 = (f32[4,128,128]{1,2,0:T(8,128)S(1)}, f32[4,128,128]{1,2,0:T(8,128)S(1)}, u32[]{:S(2)}, u32[]{:S(2)}) collective-permute-start(f32[4,128,128]{1,2,0:T(8,128)S(1)} %bitcast_add_fusion.5), channel_id=1, source_target_pairs={{0,1},{1,2},{2,3},{3,4},{4,5},{5,6},{6,7},{7,8},{8,9},{9,10},{10,1... | collective-permute-start | bytes 786440 | tf_op jit(solution)/shard_map/while/body/eval_jaxpr/ppermute | solution.py:10
  278.5 13.9 %collective-permute-start = (bf16[4,128,128]{1,2,0:T(8,128)(2,1)S(1)}, bf16[4,128,128]{1,2,0:T(8,128)(2,1)S(1)}, u32[]{:S(2)}, u32[]{:S(2)}) collective-permute-start(bf16[4,128,128]{1,2,0:T(8,128)(2,1)S(1)} %copy.46), channel_id=1, source_target_pairs={{0,1},{1,2},{2,3},{3,4},{4,5},{5,6},{6,7},{7,8},{8,9},{9,10},{10,1... | collective-permute-start | bytes 393224 | tf_op jit(solution)/shard_map/while/body/eval_jaxpr/ppermute | solution.py:10
  287.1 15.1 %collective-permute-start.3 = (f32[4,128,128]{1,2,0:T(8,128)S(1)}, f32[4,128,128]{1,2,0:T(8,128)S(1)}, u32[]{:S(2)}, u32[]{:S(2)}) collective-permute-start(f32[4,128,128]{1,2,0:T(8,128)S(1)} %bitcast_add_fusion.5), channel_id=1, source_target_pairs={{0,1},{1,2},{2,3},{3,4},{4,5},{5,6},{6,7},{7,8},{8,9},{9,10},{10,1... | collective-permute-start | bytes 786440 | tf_op jit(solution)/shard_map/while/body/eval_jaxpr/ppermute | solution.py:10
  302.2 13.9 %collective-permute-start = (bf16[4,128,128]{1,2,0:T(8,128)(2,1)S(1)}, bf16[4,128,128]{1,2,0:T(8,128)(2,1)S(1)}, u32[]{:S(2)}, u32[]{:S(2)}) collective-permute-start(bf16[4,128,128]{1,2,0:T(8,128)(2,1)S(1)} %copy.46), channel_id=1, source_target_pairs={{0,1},{1,2},{2,3},{3,4},{4,5},{5,6},{6,7},{7,8},{8,9},{9,10},{10,1... | collective-permute-start | bytes 393224 | tf_op jit(solution)/shard_map/while/body/eval_jaxpr/ppermute | solution.py:10
  310.8 15.1 %collective-permute-start.3 = (f32[4,128,128]{1,2,0:T(8,128)S(1)}, f32[4,128,128]{1,2,0:T(8,128)S(1)}, u32[]{:S(2)}, u32[]{:S(2)}) collective-permute-start(f32[4,128,128]{1,2,0:T(8,128)S(1)} %bitcast_add_fusion.5), channel_id=1, source_target_pairs={{0,1},{1,2},{2,3},{3,4},{4,5},{5,6},{6,7},{7,8},{8,9},{9,10},{10,1... | collective-permute-start | bytes 786440 | tf_op jit(solution)/shard_map/while/body/eval_jaxpr/ppermute | solution.py:10
  325.8 13.9 %collective-permute-start = (bf16[4,128,128]{1,2,0:T(8,128)(2,1)S(1)}, bf16[4,128,128]{1,2,0:T(8,128)(2,1)S(1)}, u32[]{:S(2)}, u32[]{:S(2)}) collective-permute-start(bf16[4,128,128]{1,2,0:T(8,128)(2,1)S(1)} %copy.46), channel_id=1, source_target_pairs={{0,1},{1,2},{2,3},{3,4},{4,5},{5,6},{6,7},{7,8},{8,9},{9,10},{10,1... | collective-permute-start | bytes 393224 | tf_op jit(solution)/shard_map/while/body/eval_jaxpr/ppermute | solution.py:10
  334.4 15.1 %collective-permute-start.3 = (f32[4,128,128]{1,2,0:T(8,128)S(1)}, f32[4,128,128]{1,2,0:T(8,128)S(1)}, u32[]{:S(2)}, u32[]{:S(2)}) collective-permute-start(f32[4,128,128]{1,2,0:T(8,128)S(1)} %bitcast_add_fusion.5), channel_id=1, source_target_pairs={{0,1},{1,2},{2,3},{3,4},{4,5},{5,6},{6,7},{7,8},{8,9},{9,10},{10,1... | collective-permute-start | bytes 786440 | tf_op jit(solution)/shard_map/while/body/eval_jaxpr/ppermute | solution.py:10
  349.5 13.9 %collective-permute-start = (bf16[4,128,128]{1,2,0:T(8,128)(2,1)S(1)}, bf16[4,128,128]{1,2,0:T(8,128)(2,1)S(1)}, u32[]{:S(2)}, u32[]{:S(2)}) collective-permute-start(bf16[4,128,128]{1,2,0:T(8,128)(2,1)S(1)} %copy.46), channel_id=1, source_target_pairs={{0,1},{1,2},{2,3},{3,4},{4,5},{5,6},{6,7},{7,8},{8,9},{9,10},{10,1... | collective-permute-start | bytes 393224 | tf_op jit(solution)/shard_map/while/body/eval_jaxpr/ppermute | solution.py:10
  358.1 15.1 %collective-permute-start.3 = (f32[4,128,128]{1,2,0:T(8,128)S(1)}, f32[4,128,128]{1,2,0:T(8,128)S(1)}, u32[]{:S(2)}, u32[]{:S(2)}) collective-permute-start(f32[4,128,128]{1,2,0:T(8,128)S(1)} %bitcast_add_fusion.5), channel_id=1, source_target_pairs={{0,1},{1,2},{2,3},{3,4},{4,5},{5,6},{6,7},{7,8},{8,9},{9,10},{10,1... | collective-permute-start | bytes 786440 | tf_op jit(solution)/shard_map/while/body/eval_jaxpr/ppermute | solution.py:10
  373.2 13.9 %collective-permute-start = (bf16[4,128,128]{1,2,0:T(8,128)(2,1)S(1)}, bf16[4,128,128]{1,2,0:T(8,128)(2,1)S(1)}, u32[]{:S(2)}, u32[]{:S(2)}) collective-permute-start(bf16[4,128,128]{1,2,0:T(8,128)(2,1)S(1)} %copy.46), channel_id=1, source_target_pairs={{0,1},{1,2},{2,3},{3,4},{4,5},{5,6},{6,7},{7,8},{8,9},{9,10},{10,1... | collective-permute-start | bytes 393224 | tf_op jit(solution)/shard_map/while/body/eval_jaxpr/ppermute | solution.py:10
  381.8 15.1 %collective-permute-start.3 = (f32[4,128,128]{1,2,0:T(8,128)S(1)}, f32[4,128,128]{1,2,0:T(8,128)S(1)}, u32[]{:S(2)}, u32[]{:S(2)}) collective-permute-start(f32[4,128,128]{1,2,0:T(8,128)S(1)} %bitcast_add_fusion.5), channel_id=1, source_target_pairs={{0,1},{1,2},{2,3},{3,4},{4,5},{5,6},{6,7},{7,8},{8,9},{9,10},{10,1... | collective-permute-start | bytes 786440 | tf_op jit(solution)/shard_map/while/body/eval_jaxpr/ppermute | solution.py:10
  (34 other events, 402.0 us)
Sparse Core Ops, SparseCore 0:
  397.0 123.7 reduce-scatter.1
where the time goes:
time: 533 us; the launch traced here: 528 us
  waiting for transfers between devices  273 us (51%)
  starting transfers between devices  147 us (28%)
  local copies, waits for them, and re-layouts  41.4 us (8%)
  matrix products  33.8 us (6%)
  other arithmetic  16.4 us (3%)
  between operations  14.1 us (3%)
    ppermute x64, waiting for transfers between devices, passed_along(): return lax.ppermute(value, axis, pairs)  151 us
    ppermute x64, starting transfers between devices, passed_along(): return lax.ppermute(value, axis, pairs)  147 us
    reduce_scatter x1, waiting for transfers between devices, body(): bias_grad = lax.psum_scatter(table, 'row', scatter_dimension=2, tiled=True)  122 us
    dynamic_slice x32, local copies, waits for them, and re-layouts, add_bias(): current = lax.dynamic_slice_in_dim(table, column, part.shape[2], 2)  17.8 us
    convert_element_type x16, other arithmetic, contribute(): lax.dynamic_slice_in_dim(bias, column, count, 2).astype(jnp.float32)  14.9 us
    dynamic_update_slice x32, local copies, waits for them, and re-layouts, add_bias(): return lax.dynamic_update_slice_in_dim(table, current + part, column, 2)  13.7 us
    dot_general x16, matrix products, contribute(): jnp.einsum('rjhd,rkhd->rhjk', query_four, key_four, preferred_element_typ...  11.2 us
  transfers between devices with their start and end apart: 65, of which 33 were waited for; matrix products, arithmetic and copies ran while one was open for 16% of the time, Pallas kernels for 0%

commit v1 on v0

v1 whole, which is shorter than its diff:
```python
import functools

import jax
import jax.numpy as jnp
from jax import lax
from jax.experimental import pallas as pl
from jax.experimental.pallas import tpu as pltpu
from jax.sharding import Mesh
from jax.sharding import PartitionSpec as P

ROW = ("xl", "z", "c")
BLK = ("xh", "yh", "yl")
QUERY_GROUP = ("xl", "c", "xh", "yl")
KEY_GROUP = ("xl", "c", "yh")
LOG2E = 1.4426950408889634
AUG = 16
F32, BF16 = jnp.float32, jnp.bfloat16


def three_parts(x):
    high = x.astype(BF16).astype(F32)
    rest = x - high
    mid = rest.astype(BF16).astype(F32)
    return high, mid, rest - mid


def pack_kernel(scale, which_ref, q_ref, k_ref, v_ref, g_ref, o_ref, l_ref, bias_ref, to_query_ref, to_key_ref):
    quarter = pl.multiple_of(which_ref[0] * 32, 32)
    lines = lax.broadcasted_iota(jnp.int32, (AUG, 128), 0)
    for i in range(4):
        k_t = k_ref[i].astype(F32).T.astype(BF16)
        v_t = v_ref[i].astype(F32).T.astype(BF16)
        q_t = q_ref[i].astype(F32).T.astype(BF16)
        g_f = g_ref[i].astype(F32)
        g_t = g_f.T
        gg = (g_f * o_ref[i].astype(F32)).T
        g_t = g_t.astype(BF16)
        for h in range(4):
            part = slice(h * 32, h * 32 + 32)
            offset = l_ref[i, h : h + 1, :] * (-1.0 / scale)
            delta = -jnp.sum(gg[part], axis=0, keepdims=True)
            extra = jnp.zeros((AUG, 128), F32)
            for at, piece in enumerate(three_parts(offset) + three_parts(delta)):
                extra = jnp.where(lines == at, piece, extra)
            extra = extra.astype(BF16)
            for a in range(4):
                to_query_ref[h * 4 + a, i * 80 : i * 80 + 32, :] = q_t[part]
                to_query_ref[h * 4 + a, i * 80 + 32 : i * 80 + 48, :] = extra
                to_query_ref[h * 4 + a, i * 80 + 48 : i * 80 + 80, :] = g_t[part]
                to_key_ref[h * 4 + a, i * 64 : i * 64 + 32, :] = k_t[part]
                to_key_ref[h * 4 + a, i * 64 + 32 : i * 64 + 64, :] = v_t[part]
    for h in range(4):
        for a in range(4):
            for yh in range(4):
                block = (a // 2) * 8 + yh * 2 + a % 2
                to_query_ref[h * 4 + a, 320 + yh * 32 : 352 + yh * 32, :] = bias_ref[
                    h, pl.ds(quarter, 32), block * 128 : block * 128 + 128
                ]


def attend_kernel(scale, chunk, jq_ref, kv_ref, dq_ref, dkv_ref, db_ref, bias_s, acc_s):
    for a in range(4):
        for s in range(4):
            for yh in range(4):
                bias_s[a * 128 + s * 32 : a * 128 + s * 32 + 32, yh * 128 : yh * 128 + 128] = (
                    jq_ref[s * 4 + a, 320 + yh * 32 : 352 + yh * 32, :].astype(F32) * LOG2E
                )
    acc_s[...] = jnp.zeros_like(acc_s)
    lines = lax.broadcasted_iota(jnp.int32, (AUG, 512), 0)
    ones_offset = jnp.where(lines < 3, 1.0, 0.0).astype(BF16)
    ones_delta = jnp.where((lines >= 3) & (lines < 6), 1.0, 0.0).astype(BF16)
    dims = (((0,), (0,)), ((), ()))

    def one_row(t, carry):
        s, i = t // 4, t % 4
        base = s * 4
        jb = pl.multiple_of(i * 80, 16)
        kb = pl.multiple_of(i * 64, 16)
        whole = jnp.concatenate([jq_ref[base + a, pl.ds(jb, 80), :] for a in range(4)], axis=1)
        keys = jnp.concatenate([kv_ref[base + b, pl.ds(kb, 64), :] for b in range(4)], axis=1)
        k_t, v_t = keys[:32], keys[32:]
        k_aug = jnp.concatenate([k_t, ones_offset], axis=0)
        v_aug = jnp.concatenate([ones_delta, v_t], axis=0)
        dk = dv = None
        for n in range(512 // chunk):
            at = slice(n * chunk, n * chunk + chunk)
            q_aug = whole[:48, at]
            g_aug = whole[32:80, at]
            scores = lax.dot_general(q_aug, k_aug, dims, preferred_element_type=F32)
            probs = jnp.exp2(scores * (scale * LOG2E) + bias_s[at, :])
            prob_grad = lax.dot_general(g_aug, v_aug, dims, preferred_element_type=F32)
            score_grad = probs * prob_grad
            acc_s[at, :] += score_grad
            low = score_grad.astype(BF16)
            dv_n = jnp.dot(whole[48:80, at], probs.astype(BF16), preferred_element_type=F32)
            dk_n = jnp.dot(whole[:32, at], low, preferred_element_type=F32)
            dv = dv_n if dv is None else dv + dv_n
            dk = dk_n if dk is None else dk + dk_n
            dq = lax.dot_general(k_t, low, (((1,), (1,)), ((), ())), preferred_element_type=F32)
            dq = (dq * scale).astype(BF16)
            for m in range(chunk // 128):
                dq_ref[base + n * (chunk // 128) + m, pl.ds(pl.multiple_of(i * 32, 32), 32), :] = dq[
                    :, m * 128 : m * 128 + 128
                ]
        dk = (dk * scale).astype(BF16)
        dv = dv.astype(BF16)
        for b in range(4):
            dkv_ref[base + b, pl.ds(kb, 32), :] = dk[:, b * 128 : b * 128 + 128]
            dkv_ref[base + b, pl.ds(pl.multiple_of(kb + 32, 16), 32), :] = dv[:, b * 128 : b * 128 + 128]
        return carry

    lax.fori_loop(0, 16, one_row, 0)
    for yh in range(4):
        for half in range(2):
            db_ref[yh * 2 + half] = acc_s[half * 256 : half * 256 + 256, yh * 128 : yh * 128 + 128].astype(BF16)


def unpack_kernel(q_ref, kv_ref, dq_ref, dk_ref, dv_ref):
    for i in range(4):
        for ref, width, first, out in ((q_ref, 32, 0, dq_ref), (kv_ref, 64, 0, dk_ref), (kv_ref, 64, 32, dv_ref)):
            at = slice(i * width + first, i * width + first + 32)
            heads = []
            for h in range(4):
                total = ref[h * 4, at, :].astype(F32)
                for a in range(1, 4):
                    total = total + ref[h * 4 + a, at, :].astype(F32)
                heads.append(total)
            out[i] = jnp.concatenate(heads, axis=0).T.astype(BF16)


def vmem(n=1):
    return [pl.BlockSpec(memory_space=pltpu.VMEM)] * n


def params():
    return pltpu.CompilerParams(vmem_limit_bytes=40 * 2**20)


def bias_moves():
    pairs = []
    for xl in range(2):
        for z in range(8):
            for c in range(2):
                for xh in range(2):
                    for yl in range(2):
                        source = (((xl * 8 + z) * 2 + c) * 2 + xh) * 2 + yl
                        target = (((xh * 8 + (z // 2) * 2 + yl) * 2 + xl) * 2 + z % 2) * 2 + c
                        pairs.append((source, target))
    return pairs


def body(queries, keys, values, bias, out_grad, outputs, logsumexp):
    scale = 32 ** (-0.5)
    shape = lambda *s: jax.ShapeDtypeStruct(s, BF16)
    which = (lax.axis_index("xl") * 2 + lax.axis_index("c")).astype(jnp.int32).reshape(1)
    to_query, to_key = pl.pallas_call(
        functools.partial(pack_kernel, scale),
        out_shape=(shape(16, 448, 128), shape(16, 256, 128)),
        in_specs=[pl.BlockSpec(memory_space=pltpu.SMEM)] + vmem(7),
        out_specs=tuple(vmem(2)),
        compiler_params=params(),
        name="pack",
    )(which, queries, keys, values, out_grad, outputs, logsumexp, bias)
    got_key = lax.all_to_all(to_key, KEY_GROUP, 0, 0)
    got_query = lax.all_to_all(to_query, QUERY_GROUP, 0, 0)
    dq_parts, dkv_parts, db_parts = pl.pallas_call(
        functools.partial(attend_kernel, scale, 256),
        out_shape=(shape(16, 128, 128), shape(16, 256, 128), shape(8, 256, 128)),
        in_specs=vmem(2),
        out_specs=tuple(vmem(3)),
        scratch_shapes=[pltpu.VMEM((512, 512), F32), pltpu.VMEM((512, 512), F32)],
        compiler_params=params(),
        name="attend",
    )(got_query, got_key)
    db = lax.all_to_all(db_parts, "z", 0, 0)
    db = jnp.sum(db.astype(F32), axis=0)
    db = lax.ppermute(db, ROW + ("xh", "yl"), bias_moves())
    db = db.reshape(2, 128, 2, 64).transpose(2, 0, 1, 3).reshape(4, 128, 64)
    bias_grad = lax.all_to_all(db, ("c", "yl"), 0, 0)
    dkv = lax.all_to_all(dkv_parts, KEY_GROUP, 0, 0)
    dq = lax.all_to_all(dq_parts, QUERY_GROUP, 0, 0)
    query_grad, key_grad, value_grad = pl.pallas_call(
        unpack_kernel,
        out_shape=(shape(4, 128, 128),) * 3,
        in_specs=vmem(2),
        out_specs=tuple(vmem(3)),
        compiler_params=params(),
        name="unpack",
    )(dq, dkv)
    return query_grad, key_grad, value_grad, bias_grad


def solution(mesh):
    fine = Mesh(mesh.devices.reshape(2, 8, 2, 2, 4, 2), ROW + BLK)
    rows = P(ROW, BLK, None)
    in_specs = (rows, rows, rows, P(None, BLK, None), rows, rows, P(ROW, None, BLK))
    out_specs = (rows, rows, rows, P(None, BLK, ROW))
    return jax.shard_map(body, mesh=fine, in_specs=in_specs, out_specs=out_specs, check_vma=False)
```

time: 533 us -> 173 us (0.32)
  waiting for transfers between devices: 273 us -> 7.26 us
  starting transfers between devices: 147 us -> 10.2 us
  blocking collectives: 0 us -> 130 us
  matrix products: 33.8 us -> 0 us
  local copies, waits for them, and re-layouts: 41.4 us -> 7.63 us
  Pallas kernels: 0 us -> 17 us
  other arithmetic: 16.4 us -> 0.07 us
  between operations: 14.1 us -> 0.7 us
    ppermute x64 -> x1, waiting for transfers between devices: 151 us -> 6.29 us  [body(): db = lax.ppermute(db, ROW + ('xh', 'yl'), bias_moves())]
    ppermute x64 -> x1, starting transfers between devices: 147 us -> 3.52 us  [body(): db = lax.ppermute(db, ROW + ('xh', 'yl'), bias_moves())]
    all_to_all x0 -> x5, blocking collectives: none -> 130 us  [the longest x1 38.1 us: body(): got_key = lax.all_to_all(to_key, KEY_GROUP, 0, 0)]
    reduce_scatter x1 -> x0, waiting for transfers between devices: 122 us -> none  [body(): bias_grad = lax.psum_scatter(table, 'row', scatter_dimension=2, tiled=True)]
    dot_general x80 -> x0, matrix products: 33.8 us -> none  [the longest x16 11.2 us: contribute(): jnp.einsum('rjhd,rkhd->rhjk', query_four, key_four, preferred_element_typ...]
    dynamic_slice x32 -> x0, local copies, waits for them, and re-layouts: 17.8 us -> none  [add_bias(): current = lax.dynamic_slice_in_dim(table, column, part.shape[2], 2)]
    pallas_call x0 -> x3, Pallas kernels: none -> 17 us  [the longest x1 15.7 us: body(): pl.pallas_call(functools.partial(attend_kernel, scale, 256), out_shape=(s...]
    convert_element_type x17 -> x0, other arithmetic: 14.9 us -> none  [the longest x16 14.9 us: contribute(): lax.dynamic_slice_in_dim(bias, column, count, 2).astype(jnp.float32)]
  transfers between devices with their start and end apart: 65 -> 2, of which waited for: 33 -> 2; matrix products, arithmetic and copies ran while one was open for 16% -> 0% of each run, Pallas kernels for 0% -> 0%
where the time goes in v1:
time: 173 us
  blocking collectives  130 us (75%)
  Pallas kernels  17 us (10%)
  starting transfers between devices  10.2 us (6%)
  local copies, waits for them, and re-layouts  7.63 us (4%)
  waiting for transfers between devices  7.26 us (4%)
    all_to_all x1, blocking collectives, body(): got_key = lax.all_to_all(to_key, KEY_GROUP, 0, 0)  38.1 us
    all_to_all x1, blocking collectives, body(): dkv = lax.all_to_all(dkv_parts, KEY_GROUP, 0, 0)  32.1 us
    all_to_all x1, blocking collectives, body(): got_query = lax.all_to_all(to_query, QUERY_GROUP, 0, 0)  28.4 us
    all_to_all x1, blocking collectives, body(): db = lax.all_to_all(db_parts, 'z', 0, 0)  25 us
    pallas_call x1, Pallas kernels, body(): pl.pallas_call(functools.partial(attend_kernel, scale, 256), out_shape=(s...  15.7 us
    unnamed x15, local copies, waits for them, and re-layouts  7.45 us
    all_to_all x1, starting transfers between devices, body(): dq = lax.all_to_all(dq_parts, QUERY_GROUP, 0, 0)  6.68 us
    all_to_all x1, blocking collectives, body(): bias_grad = lax.all_to_all(db, ('c', 'yl'), 0, 0)  6.51 us
  transfers between devices with their start and end apart: 2, of which 2 were waited for; matrix products, arithmetic and copies ran while one was open for 0% of the time, Pallas kernels for 0%

profile of v1, /device:TPU:1, one launch (start us, length us, event | category | flops | bytes accessed | tf_op | source)
XLA Modules:
  0.0 172.9 jit_solution(7796640097425307196)
XLA Ops:
  0.6 0.0 copy-start
  0.6 1.6 copy-done
  2.2 0.0 copy-start.1
  2.2 0.9 copy-done.1
  3.1 0.0 copy-start.2
  3.1 0.9 copy-done.2
  4.0 0.0 copy-start.3
  4.0 0.9 copy-done.3
  4.9 0.0 copy-start.4
  4.9 0.9 copy-done.4
  5.9 0.0 copy-start.5
  5.9 0.9 copy-done.5
  6.8 0.0 copy-start.6
  6.8 0.7 copy-done.6
  7.5 0.3 pack.1
  7.8 38.1 %all_to_all.30.kv_ref = bf16[16,256,128]{2,1,0:T(8,128)(2,1)S(1)} all-to-all(bf16[16,256,128]{2,1,0:T(8,128)(2,1)S(1)} %get-tuple-element.13), channel_id=1, replica_groups=mesh['xl'=2,'z'=8,'c'=2,'xh'=2,'yh'=4,'yl'=2] {'xl','c','yh'}, dimensions={0} | all-to-all | bytes 2097152 | tf_op jit(solution)/shard_map/all_to_all | solution.py:164
  45.9 28.4 %all_to_all.31.jq_ref = bf16[16,448,128]{2,1,0:T(8,128)(2,1)S(1)} all-to-all(bf16[16,448,128]{2,1,0:T(8,128)(2,1)S(1)} %get-tuple-element.12), channel_id=1, replica_groups=mesh['xl'=2,'z'=8,'c'=2,'xh'=2,'yh'=4,'yl'=2] {'xl','c','xh','yl'}, dimensions={0} | all-to-all | bytes 3670016 | tf_op jit(solution)/shard_map/all_to_all | solution.py:165
  74.3 15.7 %attend.1 = (bf16[16,128,128]{2,1,0:T(8,128)(2,1)}, bf16[16,256,128]{2,1,0:T(8,128)(2,1)S(1)}, bf16[8,256,128]{2,1,0:T(8,128)(2,1)S(1)}) custom-call(bf16[16,448,128]{2,1,0:T(8,128)(2,1)S(1)} %all_to_all.31.jq_ref, bf16[16,256,128]{2,1,0:T(8,128)(2,1)S(1)} %all_to_all.30.kv_ref), custom_call_target="tpu_custom_call" | custom-call | tf_op jit(solution)/shard_map/attend/pallas_call | solution.py:166
  89.9 25.0 %all_to_all.32 = bf16[8,256,128]{2,1,0:T(8,128)(2,1)S(1)} all-to-all(bf16[8,256,128]{2,1,0:T(8,128)(2,1)S(1)} %get-tuple-element.19), channel_id=1, replica_groups=mesh['xl'=2,'z'=8,'c'=2,'xh'=2,'yh'=4,'yl'=2] {'z'}, dimensions={0} | all-to-all | bytes 1048576 | tf_op jit(solution)/shard_map/all_to_all | solution.py:175
  114.9 6.7 %all-to-all-start.2 = ((bf16[16,128,128]{2,1,0:T(8,128)(2,1)}), bf16[16,128,128]{2,1,0:T(8,128)(2,1)S(1)}, u32[]{:S(2)}, u32[]{:S(2)}) async-start(bf16[16,128,128]{2,1,0:T(8,128)(2,1)} %get-tuple-element.14), calls=%async_computation.2 | async-start | bytes 1048576 | tf_op jit(solution)/shard_map/all_to_all | solution.py:181
  121.6 0.1 convert_reduce_fusion
  121.6 3.5 %collective-permute-start = (f32[256,128]{1,0:T(8,128)S(1)}, f32[256,128]{1,0:T(8,128)S(1)}, u32[]{:S(2)}, u32[]{:S(2)}) collective-permute-start(f32[256,128]{1,0:T(8,128)S(1)} %convert_reduce_fusion), channel_id=1, source_target_pairs={{0,0},{1,32},{8,256},{9,288},{16,1},{17,33},{24,257},{25,289},{32,... | collective-permute-start | bytes 393224 | tf_op jit(solution)/shard_map/ppermute | solution.py:177
  125.2 6.3 %collective-permute-done = f32[256,128]{1,0:T(8,128)S(1)} collective-permute-done((f32[256,128]{1,0:T(8,128)S(1)}, f32[256,128]{1,0:T(8,128)S(1)}, u32[]{:S(2)}, u32[]{:S(2)}) %collective-permute-start) | collective-permute-done | bytes 131104 | tf_op jit(solution)/shard_map/ppermute | solution.py:177
  131.5 0.1 copy.12
  131.6 0.1 reshape.18
  131.7 1.0 all-to-all-done.2.q_ref
  132.6 6.5 %all_to_all.33 = f32[4,128,64]{1,2,0:T(8,128)S(1)} all-to-all(f32[4,128,64]{1,2,0:T(8,128)S(1)} %bitcast.5), channel_id=1, replica_groups=mesh['xl'=2,'z'=8,'c'=2,'xh'=2,'yh'=4,'yl'=2] {'c','yl'}, dimensions={0} | all-to-all | bytes 262144 | tf_op jit(solution)/shard_map/all_to_all | solution.py:179
  139.1 32.1 %all_to_all.34.kv_ref = bf16[16,256,128]{2,1,0:T(8,128)(2,1)S(1)} all-to-all(bf16[16,256,128]{2,1,0:T(8,128)(2,1)S(1)} %get-tuple-element.15), channel_id=1, replica_groups=mesh['xl'=2,'z'=8,'c'=2,'xh'=2,'yh'=4,'yl'=2] {'xl','c','yh'}, dimensions={0} | all-to-all | bytes 2097152 | tf_op jit(solution)/shard_map/all_to_all | solution.py:180
  171.2 1.0 unpack.1
  172.2 0.7 copy.15
  (1 shorter events, 0.0 us)
Async XLA Ops:
  0.6 1.6 copy-start
  2.2 0.9 copy-start.1
  3.1 0.9 copy-start.2
  4.0 0.9 copy-start.3
  4.9 0.9 copy-start.4
  5.9 0.9 copy-start.5
  6.8 0.7 copy-start.6
  114.9 17.7 %all-to-all-start.2 = ((bf16[16,128,128]{2,1,0:T(8,128)(2,1)}), bf16[16,128,128]{2,1,0:T(8,128)(2,1)S(1)}, u32[]{:S(2)}, u32[]{:S(2)}) async-start(bf16[16,128,128]{2,1,0:T(8,128)(2,1)} %get-tuple-element.14), calls=%async_computation.2 | async-start | bytes 1048576 | tf_op jit(solution)/shard_map/all_to_all | solution.py:181
  121.6 9.8 %collective-permute-start = (f32[256,128]{1,0:T(8,128)S(1)}, f32[256,128]{1,0:T(8,128)S(1)}, u32[]{:S(2)}, u32[]{:S(2)}) collective-permute-start(f32[256,128]{1,0:T(8,128)S(1)} %convert_reduce_fusion), channel_id=1, source_target_pairs={{0,0},{1,32},{8,256},{9,288},{16,1},{17,33},{24,257},{25,289},{32,... | collective-permute-start | bytes 393224 | tf_op jit(solution)/shard_map/ppermute | solution.py:177

commit v2 on v1

v2 whole, which is shorter than its diff:
```python
import functools

import jax
import jax.numpy as jnp
from jax import lax
from jax.experimental import pallas as pl
from jax.experimental.pallas import tpu as pltpu
from jax.sharding import Mesh
from jax.sharding import PartitionSpec as P

ROW = ("xl", "z", "c")
BLK = ("xh", "yh", "yl")
QUERY_GROUP = ("xl", "c", "xh", "yl")
KEY_GROUP = ("xl", "c", "yh")
LOG2E = 1.4426950408889634
AUG = 16
F32, BF16 = jnp.float32, jnp.bfloat16


def three_parts(x):
    high = x.astype(BF16).astype(F32)
    rest = x - high
    mid = rest.astype(BF16).astype(F32)
    return high, mid, rest - mid


def fetch(pairs, sems):
    copies = [pltpu.make_async_copy(src, dst, sems.at[at]) for at, (src, dst) in enumerate(pairs)]
    for copy in copies:
        copy.start()
    return copies


def turned(x):
    return x.astype(F32).T.astype(BF16)


def pack_key_kernel(k_hbm, v_hbm, to_key_ref, k_ref, v_ref, sems):
    copies = fetch(((k_hbm, k_ref), (v_hbm, v_ref)), sems)
    for copy in copies:
        copy.wait()
    for i in range(4):
        k_t, v_t = turned(k_ref[i]), turned(v_ref[i])
        for h in range(4):
            part = slice(h * 32, h * 32 + 32)
            for b in range(4):
                to_key_ref[h * 4 + b, i * 64 : i * 64 + 32, :] = k_t[part]
                to_key_ref[h * 4 + b, i * 64 + 32 : i * 64 + 64, :] = v_t[part]


def pack_query_kernel(
    scale, which_ref, q_hbm, g_hbm, o_hbm, l_hbm, bias_hbm, to_query_ref, q_ref, g_ref, o_ref, l_ref, bias_ref, sems
):
    quarter = pl.multiple_of(which_ref[0] * 32, 32)
    copies = fetch(
        (
            (q_hbm, q_ref),
            (g_hbm, g_ref),
            (o_hbm, o_ref),
            (l_hbm, l_ref),
            (bias_hbm.at[:, pl.ds(quarter, 32), :], bias_ref),
        ),
        sems,
    )
    lines = lax.broadcasted_iota(jnp.int32, (AUG, 128), 0)
    for copy in copies[:4]:
        copy.wait()
    for pair in range(2):
        extra = [jnp.zeros((AUG, 128), F32)] * 4
        for n in range(2):
            i = pair * 2 + n
            q_t = turned(q_ref[i])
            g_f = g_ref[i].astype(F32)
            gg = (g_f * o_ref[i].astype(F32)).T
            g_t = g_f.T.astype(BF16)
            for h in range(4):
                part = slice(h * 32, h * 32 + 32)
                offset = l_ref[i, h : h + 1, :] * (-1.0 / scale)
                delta = -jnp.sum(gg[part], axis=0, keepdims=True)
                for at, piece in enumerate(three_parts(offset) + three_parts(delta)):
                    extra[h] = jnp.where(lines == n * 6 + at, piece, extra[h])
                for a in range(4):
                    to_query_ref[h * 4 + a, i * 64 : i * 64 + 32, :] = q_t[part]
                    to_query_ref[h * 4 + a, i * 64 + 32 : i * 64 + 64, :] = g_t[part]
        for h in range(4):
            for a in range(4):
                to_query_ref[h * 4 + a, 256 + pair * 16 : 272 + pair * 16, :] = extra[h].astype(BF16)
    copies[4].wait()
    for h in range(4):
        for a in range(4):
            for yh in range(4):
                block = (a // 2) * 8 + yh * 2 + a % 2
                to_query_ref[h * 4 + a, 288 + yh * 32 : 320 + yh * 32, :] = bias_ref[
                    h, :, block * 128 : block * 128 + 128
                ]


def attend_kernel(scale, jq_ref, kv_ref, dq_ref, dkv_ref, db_ref, bias_s, acc_s):
    for a in range(4):
        for s in range(4):
            for yh in range(4):
                bias_s[a * 128 + s * 32 : a * 128 + s * 32 + 32, yh * 128 : yh * 128 + 128] = (
                    jq_ref[s * 4 + a, 288 + yh * 32 : 320 + yh * 32, :].astype(F32) * LOG2E
                )
    acc_s[...] = jnp.zeros_like(acc_s)
    lines = lax.broadcasted_iota(jnp.int32, (AUG, 512), 0)
    ones = [
        jnp.where((lines >= first) & (lines < first + 3), 1.0, 0.0).astype(BF16) for first in (0, 3, 6, 9)
    ]

    def four_rows(s, carry):
        base = s * 4
        for i in range(4):
            first = i * 64
            at = 256 + (i // 2) * 16
            q_t, g_t, extra = (
                jnp.concatenate([jq_ref[base + a, start : start + size, :] for a in range(4)], axis=1)
                for start, size in ((first, 32), (first + 32, 32), (at, 16))
            )
            k_t, v_t = (
                jnp.concatenate([kv_ref[base + b, start : start + 32, :] for b in range(4)], axis=1)
                for start in (first, first + 32)
            )
            q_rows = jnp.concatenate([q_t, extra], axis=0).T
            g_rows = jnp.concatenate([g_t, extra], axis=0).T
            k_aug = jnp.concatenate([k_t, ones[(i % 2) * 2]], axis=0)
            v_aug = jnp.concatenate([v_t, ones[(i % 2) * 2 + 1]], axis=0)
            scores = jnp.dot(q_rows, k_aug, preferred_element_type=F32)
            prob_grad = jnp.dot(g_rows, v_aug, preferred_element_type=F32)
            probs = jnp.exp2(scores * (scale * LOG2E) + bias_s[...])
            score_grad = probs * prob_grad
            acc_s[...] += score_grad
            low = score_grad.astype(BF16)
            dv = jnp.dot(g_t, probs.astype(BF16), preferred_element_type=F32).astype(BF16)
            dk = (jnp.dot(q_t, low, preferred_element_type=F32) * scale).astype(BF16)
            dq = (jnp.dot(low, k_t.T, preferred_element_type=F32).T * scale).astype(BF16)
            for b in range(4):
                block = slice(b * 128, b * 128 + 128)
                dq_ref[base + b, i * 32 : i * 32 + 32, :] = dq[:, block]
                dkv_ref[base + b, first : first + 32, :] = dk[:, block]
                dkv_ref[base + b, first + 32 : first + 64, :] = dv[:, block]
        return carry

    lax.fori_loop(0, 4, four_rows, 0)
    for yh in range(4):
        for half in range(2):
            db_ref[yh * 2 + half] = acc_s[half * 256 : half * 256 + 256, yh * 128 : yh * 128 + 128].astype(BF16)


def unpack_kernel(q_ref, kv_ref, dq_ref, dk_ref, dv_ref):
    for i in range(4):
        for ref, width, first, out in ((q_ref, 32, 0, dq_ref), (kv_ref, 64, 0, dk_ref), (kv_ref, 64, 32, dv_ref)):
            at = slice(i * width + first, i * width + first + 32)
            heads = []
            for h in range(4):
                total = ref[h * 4, at, :].astype(F32)
                for a in range(1, 4):
                    total = total + ref[h * 4 + a, at, :].astype(F32)
                heads.append(total)
            out[i] = jnp.concatenate(heads, axis=0).T.astype(BF16)


def vmem(n=1):
    return [pl.BlockSpec(memory_space=pltpu.VMEM)] * n


def params(mib=40):
    return pltpu.CompilerParams(vmem_limit_bytes=mib * 2**20)


def bias_moves():
    pairs = []
    for xl in range(2):
        for z in range(8):
            for c in range(2):
                for xh in range(2):
                    for yl in range(2):
                        source = (((xl * 8 + z) * 2 + c) * 2 + xh) * 2 + yl
                        target = (((xh * 8 + (z // 2) * 2 + yl) * 2 + xl) * 2 + z % 2) * 2 + c
                        pairs.append((source, target))
    return pairs


def body(queries, keys, values, bias, out_grad, outputs, logsumexp):
    scale = 32 ** (-0.5)
    shape = lambda *s: jax.ShapeDtypeStruct(s, BF16)
    which = (lax.axis_index("xl") * 2 + lax.axis_index("c")).astype(jnp.int32).reshape(1)
    hbm = pl.BlockSpec(memory_space=pltpu.HBM)
    to_key = pl.pallas_call(
        pack_key_kernel,
        out_shape=shape(16, 256, 128),
        in_specs=[hbm] * 2,
        out_specs=vmem()[0],
        scratch_shapes=[pltpu.VMEM((4, 128, 128), BF16)] * 2 + [pltpu.SemaphoreType.DMA((2,))],
        compiler_params=params(61),
        name="pack_key",
    )(keys, values)
    to_query = pl.pallas_call(
        functools.partial(pack_query_kernel, scale),
        out_shape=shape(16, 416, 128),
        in_specs=[pl.BlockSpec(memory_space=pltpu.SMEM)] + [hbm] * 5,
        out_specs=vmem()[0],
        scratch_shapes=[pltpu.VMEM((4, 128, 128), BF16)] * 3
        + [pltpu.VMEM((4, 4, 128), F32), pltpu.VMEM((4, 32, 2048), BF16), pltpu.SemaphoreType.DMA((5,))],
        compiler_params=params(61),
        name="pack_query",
    )(which, queries, out_grad, outputs, logsumexp, bias)
    got_key = lax.all_to_all(to_key, KEY_GROUP, 0, 0)
    got_query = lax.all_to_all(to_query, QUERY_GROUP, 0, 0)
    dq_parts, dkv_parts, db_parts = pl.pallas_call(
        functools.partial(attend_kernel, scale),
        out_shape=(shape(16, 128, 128), shape(16, 256, 128), shape(8, 256, 128)),
        in_specs=vmem(2),
        out_specs=tuple(vmem(3)),
        scratch_shapes=[pltpu.VMEM((512, 512), F32), pltpu.VMEM((512, 512), F32)],
        compiler_params=params(),
        name="attend",
    )(got_query, got_key)
    db = lax.all_to_all(db_parts, "z", 0, 0)
    db = jnp.sum(db.astype(F32), axis=0)
    db = lax.ppermute(db, ROW + ("xh", "yl"), bias_moves())
    db = db.reshape(2, 128, 2, 64).transpose(2, 0, 1, 3).reshape(4, 128, 64)
    bias_grad = lax.all_to_all(db, ("c", "yl"), 0, 0)
    dkv = lax.all_to_all(dkv_parts, KEY_GROUP, 0, 0)
    dq = lax.all_to_all(dq_parts, QUERY_GROUP, 0, 0)
    query_grad, key_grad, value_grad = pl.pallas_call(
        unpack_kernel,
        out_shape=(shape(4, 128, 128),) * 3,
        in_specs=vmem(2),
        out_specs=tuple(vmem(3)),
        compiler_params=params(),
        name="unpack",
    )(dq, dkv)
    return query_grad, key_grad, value_grad, bias_grad


def solution(mesh):
    fine = Mesh(mesh.devices.reshape(2, 8, 2, 2, 4, 2), ROW + BLK)
    rows = P(ROW, BLK, None)
    in_specs = (rows, rows, rows, P(None, BLK, None), rows, rows, P(ROW, None, BLK))
    out_specs = (rows, rows, rows, P(None, BLK, ROW))
    return jax.shard_map(body, mesh=fine, in_specs=in_specs, out_specs=out_specs, check_vma=False)
```

time: 173 us -> 163 us (0.942)
  blocking collectives: 130 us -> 91.7 us
  waiting for transfers between devices: 7.26 us -> 32.5 us
  starting transfers between devices: 10.2 us -> 20.2 us
  local copies, waits for them, and re-layouts: 7.63 us -> 0.83 us
    all_to_all x1 -> x0, blocking collectives: 38.1 us -> none  [body(): got_key = lax.all_to_all(to_key, KEY_GROUP, 0, 0)]
    all_to_all x0 -> x1, waiting for transfers between devices: none -> 25.2 us  [body(): got_key = lax.all_to_all(to_key, KEY_GROUP, 0, 0)]
    all_to_all x0 -> x1, starting transfers between devices: none -> 10.4 us  [body(): got_key = lax.all_to_all(to_key, KEY_GROUP, 0, 0)]
    unnamed x15 -> x1, local copies, waits for them, and re-layouts: 7.45 us -> 0.65 us
    pallas_call x2 -> x3, Pallas kernels: 16 us -> 15.6 us  [the longest x1 10.9 us: body(): pl.pallas_call(functools.partial(attend_kernel, scale), out_shape=(shape(...]
  transfers between devices with their start and end apart: 2 -> 3, of which waited for: 2 -> 3; matrix products, arithmetic and copies ran while one was open for 0% -> 0% of each run, Pallas kernels for 0% -> 2%
where the time goes in v2:
time: 163 us
  blocking collectives  91.7 us (56%)
  waiting for transfers between devices  32.5 us (20%)
  starting transfers between devices  20.2 us (12%)
  Pallas kernels  16.6 us (10%)
    all_to_all x1, blocking collectives, body(): dkv = lax.all_to_all(dkv_parts, KEY_GROUP, 0, 0)  32.5 us
    all_to_all x1, blocking collectives, body(): got_query = lax.all_to_all(to_query, QUERY_GROUP, 0, 0)  27.3 us
    all_to_all x1, blocking collectives, body(): db = lax.all_to_all(db_parts, 'z', 0, 0)  25.3 us
    all_to_all x1, waiting for transfers between devices, body(): got_key = lax.all_to_all(to_key, KEY_GROUP, 0, 0)  25.2 us
    pallas_call x1, Pallas kernels, body(): pl.pallas_call(functools.partial(attend_kernel, scale), out_shape=(shape(...  10.9 us
    all_to_all x1, starting transfers between devices, body(): got_key = lax.all_to_all(to_key, KEY_GROUP, 0, 0)  10.4 us
    all_to_all x1, blocking collectives, body(): bias_grad = lax.all_to_all(db, ('c', 'yl'), 0, 0)  6.51 us
    all_to_all x1, starting transfers between devices, body(): dq = lax.all_to_all(dq_parts, QUERY_GROUP, 0, 0)  6.31 us
  transfers between devices with their start and end apart: 3, of which 3 were waited for; matrix products, arithmetic and copies ran while one was open for 0% of the time, Pallas kernels for 2%

profile of v2, /device:TPU:1, one launch (start us, length us, event | category | flops | bytes accessed | tf_op | source)
XLA Modules:
  0.0 162.5 jit_solution(5020510771936321332)
XLA Ops:
  0.6 2.1 %pack_key.1 = bf16[16,256,128]{2,1,0:T(8,128)(2,1)} custom-call(bf16[4,128,128]{2,1,0:T(8,128)(2,1)} %k_hbm.1, bf16[4,128,128]{2,1,0:T(8,128)(2,1)} %v_hbm.1), custom_call_target="tpu_custom_call" | custom-call | tf_op jit(solution)/shard_map/pack_key/pallas_call | solution.py:189
  2.7 10.4 %all-to-all-start.1 = ((bf16[16,256,128]{2,1,0:T(8,128)(2,1)}), bf16[16,256,128]{2,1,0:T(8,128)(2,1)S(1)}, u32[]{:S(2)}, u32[]{:S(2)}) async-start(bf16[16,256,128]{2,1,0:T(8,128)(2,1)} %pack_key.1), calls=%async_computation.1 | async-start | bytes 2097152 | tf_op jit(solution)/shard_map/all_to_all | solution.py:208
  13.1 2.6 %pack_query.1 = bf16[16,416,128]{2,1,0:T(8,128)(2,1)} custom-call(s32[1]{0:T(128)} %bitcast.which_ref, bf16[4,128,128]{2,1,0:T(8,128)(2,1)} %q_hbm.1, bf16[4,128,128]{2,1,0:T(8,128)(2,1)} %g_hbm.1, bf16[4,128,128]{2,1,0:T(8,128)(2,1)} %o_hbm.1, f32[4,4,128]{2,1,0:T(4,128)} %l_hbm.1, bf16[4,128,2048]{2,1,0:T(8,128)(2,1)} %bias_hbm.1), custom_call_target="tpu_custom_call" | custom-call | tf_op jit(solution)/shard_map/pack_query/pallas_call | solution.py:198
  15.7 25.2 %all-to-all-done.1.kv_ref = bf16[16,256,128]{2,1,0:T(8,128)(2,1)S(1)} async-done(((bf16[16,256,128]{2,1,0:T(8,128)(2,1)}), bf16[16,256,128]{2,1,0:T(8,128)(2,1)S(1)}, u32[]{:S(2)}, u32[]{:S(2)}) %all-to-all-start.1) | async-done | bytes 1048608 | tf_op jit(solution)/shard_map/all_to_all | solution.py:208
  40.9 27.3 %all_to_all.30.jq_ref = bf16[16,416,128]{2,1,0:T(8,128)(2,1)S(1)} all-to-all(bf16[16,416,128]{2,1,0:T(8,128)(2,1)} %pack_query.1), channel_id=1, replica_groups=mesh['xl'=2,'z'=8,'c'=2,'xh'=2,'yh'=4,'yl'=2] {'xl','c','xh','yl'}, dimensions={0} | all-to-all | bytes 3407872 | tf_op jit(solution)/shard_map/all_to_all | solution.py:209
  68.3 10.9 %attend.1 = (bf16[16,128,128]{2,1,0:T(8,128)(2,1)}, bf16[16,256,128]{2,1,0:T(8,128)(2,1)S(1)}, bf16[8,256,128]{2,1,0:T(8,128)(2,1)S(1)}) custom-call(bf16[16,416,128]{2,1,0:T(8,128)(2,1)S(1)} %all_to_all.30.jq_ref, bf16[16,256,128]{2,1,0:T(8,128)(2,1)S(1)} %all-to-all-done.1.kv_ref), custom_call_target="tpu_custom_call" | custom-call | tf_op jit(solution)/shard_map/attend/pallas_call | solution.py:210
  79.1 25.3 %all_to_all.31 = bf16[8,256,128]{2,1,0:T(8,128)(2,1)S(1)} all-to-all(bf16[8,256,128]{2,1,0:T(8,128)(2,1)S(1)} %get-tuple-element.15), channel_id=1, replica_groups=mesh['xl'=2,'z'=8,'c'=2,'xh'=2,'yh'=4,'yl'=2] {'z'}, dimensions={0} | all-to-all | bytes 1048576 | tf_op jit(solution)/shard_map/all_to_all | solution.py:219
  104.5 6.3 %all-to-all-start.2 = ((bf16[16,128,128]{2,1,0:T(8,128)(2,1)}), bf16[16,128,128]{2,1,0:T(8,128)(2,1)S(1)}, u32[]{:S(2)}, u32[]{:S(2)}) async-start(bf16[16,128,128]{2,1,0:T(8,128)(2,1)} %get-tuple-element.10), calls=%async_computation.2 | async-start | bytes 1048576 | tf_op jit(solution)/shard_map/all_to_all | solution.py:225
  110.8 0.1 convert_reduce_fusion
  110.8 3.5 %collective-permute-start = (f32[256,128]{1,0:T(8,128)S(1)}, f32[256,128]{1,0:T(8,128)S(1)}, u32[]{:S(2)}, u32[]{:S(2)}) collective-permute-start(f32[256,128]{1,0:T(8,128)S(1)} %convert_reduce_fusion), channel_id=1, source_target_pairs={{0,0},{1,32},{8,256},{9,288},{16,1},{17,33},{24,257},{25,289},{32,... | collective-permute-start | bytes 393224 | tf_op jit(solution)/shard_map/ppermute | solution.py:221
  114.4 6.3 %collective-permute-done = f32[256,128]{1,0:T(8,128)S(1)} collective-permute-done((f32[256,128]{1,0:T(8,128)S(1)}, f32[256,128]{1,0:T(8,128)S(1)}, u32[]{:S(2)}, u32[]{:S(2)}) %collective-permute-start) | collective-permute-done | bytes 131104 | tf_op jit(solution)/shard_map/ppermute | solution.py:221
  120.7 0.1 copy.12
  120.8 0.1 reshape.18
  120.9 1.0 all-to-all-done.2.q_ref
  121.8 6.5 %all_to_all.32 = f32[4,128,64]{1,2,0:T(8,128)S(1)} all-to-all(f32[4,128,64]{1,2,0:T(8,128)S(1)} %bitcast.5), channel_id=1, replica_groups=mesh['xl'=2,'z'=8,'c'=2,'xh'=2,'yh'=4,'yl'=2] {'c','yl'}, dimensions={0} | all-to-all | bytes 262144 | tf_op jit(solution)/shard_map/all_to_all | solution.py:223
  128.3 32.5 %all_to_all.33.kv_ref = bf16[16,256,128]{2,1,0:T(8,128)(2,1)S(1)} all-to-all(bf16[16,256,128]{2,1,0:T(8,128)(2,1)S(1)} %get-tuple-element.11), channel_id=1, replica_groups=mesh['xl'=2,'z'=8,'c'=2,'xh'=2,'yh'=4,'yl'=2] {'xl','c','yh'}, dimensions={0} | all-to-all | bytes 2097152 | tf_op jit(solution)/shard_map/all_to_all | solution.py:224
  160.8 1.0 unpack.1
  161.9 0.7 copy.15
  (1 shorter events, 0.0 us)
Async XLA Ops:
  2.7 38.2 %all-to-all-start.1 = ((bf16[16,256,128]{2,1,0:T(8,128)(2,1)}), bf16[16,256,128]{2,1,0:T(8,128)(2,1)S(1)}, u32[]{:S(2)}, u32[]{:S(2)}) async-start(bf16[16,256,128]{2,1,0:T(8,128)(2,1)} %pack_key.1), calls=%async_computation.1 | async-start | bytes 2097152 | tf_op jit(solution)/shard_map/all_to_all | solution.py:208
  104.5 17.4 %all-to-all-start.2 = ((bf16[16,128,128]{2,1,0:T(8,128)(2,1)}), bf16[16,128,128]{2,1,0:T(8,128)(2,1)S(1)}, u32[]{:S(2)}, u32[]{:S(2)}) async-start(bf16[16,128,128]{2,1,0:T(8,128)(2,1)} %get-tuple-element.10), calls=%async_computation.2 | async-start | bytes 1048576 | tf_op jit(solution)/shard_map/all_to_all | solution.py:225
  110.8 9.8 %collective-permute-start = (f32[256,128]{1,0:T(8,128)S(1)}, f32[256,128]{1,0:T(8,128)S(1)}, u32[]{:S(2)}, u32[]{:S(2)}) collective-permute-start(f32[256,128]{1,0:T(8,128)S(1)} %convert_reduce_fusion), channel_id=1, source_target_pairs={{0,0},{1,32},{8,256},{9,288},{16,1},{17,33},{24,257},{25,289},{32,... | collective-permute-start | bytes 393224 | tf_op jit(solution)/shard_map/ppermute | solution.py:221

commit v3 on v2

--- a/solution.py
+++ b/solution.py
@@ -95,12 +95,14 @@
                 ]
 
 
-def attend_kernel(scale, jq_ref, kv_ref, dq_ref, dkv_ref, db_ref, bias_s, acc_s):
+def attend_kernel(scale, yh_ref, jq_ref, kv_ref, dq_ref, dkv0_ref, dkv1_ref, dkv2_ref, dkv3_ref, db_ref, bias_s, acc_s):
+    dkv_refs = (dkv0_ref, dkv1_ref, dkv2_ref, dkv3_ref)
+    owner = [lax.rem(yh_ref[0] + p, 4) for p in range(4)]
     for a in range(4):
         for s in range(4):
-            for yh in range(4):
-                bias_s[a * 128 + s * 32 : a * 128 + s * 32 + 32, yh * 128 : yh * 128 + 128] = (
-                    jq_ref[s * 4 + a, 288 + yh * 32 : 320 + yh * 32, :].astype(F32) * LOG2E
+            for p in range(4):
+                bias_s[a * 128 + s * 32 : a * 128 + s * 32 + 32, p * 128 : p * 128 + 128] = (
+                    jq_ref[s * 4 + a, pl.ds(pl.multiple_of(288 + owner[p] * 32, 32), 32), :].astype(F32) * LOG2E
                 )
     acc_s[...] = jnp.zeros_like(acc_s)
     lines = lax.broadcasted_iota(jnp.int32, (AUG, 512), 0)
@@ -118,7 +120,7 @@
                 for start, size in ((first, 32), (first + 32, 32), (at, 16))
             )
             k_t, v_t = (
-                jnp.concatenate([kv_ref[base + b, start : start + 32, :] for b in range(4)], axis=1)
+                jnp.concatenate([kv_ref[base + owner[p], start : start + 32, :] for p in range(4)], axis=1)
                 for start in (first, first + 32)
             )
             q_rows = jnp.concatenate([q_t, extra], axis=0).T
@@ -137,27 +139,26 @@
             for b in range(4):
                 block = slice(b * 128, b * 128 + 128)
                 dq_ref[base + b, i * 32 : i * 32 + 32, :] = dq[:, block]
-                dkv_ref[base + b, first : first + 32, :] = dk[:, block]
-                dkv_ref[base + b, first + 32 : first + 64, :] = dv[:, block]
+                dkv_refs[b][s, first : first + 32, :] = dk[:, block]
+                dkv_refs[b][s, first + 32 : first + 64, :] = dv[:, block]
         return carry
 
     lax.fori_loop(0, 4, four_rows, 0)
-    for yh in range(4):
+    for p in range(4):
         for half in range(2):
-            db_ref[yh * 2 + half] = acc_s[half * 256 : half * 256 + 256, yh * 128 : yh * 128 + 128].astype(BF16)
+            db_ref[owner[p] * 2 + half] = acc_s[half * 256 : half * 256 + 256, p * 128 : p * 128 + 128].astype(BF16)
 
 
 def unpack_kernel(q_ref, kv_ref, dq_ref, dk_ref, dv_ref):
     for i in range(4):
-        for ref, width, first, out in ((q_ref, 32, 0, dq_ref), (kv_ref, 64, 0, dk_ref), (kv_ref, 64, 32, dv_ref)):
-            at = slice(i * width + first, i * width + first + 32)
-            heads = []
-            for h in range(4):
-                total = ref[h * 4, at, :].astype(F32)
-                for a in range(1, 4):
-                    total = total + ref[h * 4 + a, at, :].astype(F32)
-                heads.append(total)
-            out[i] = jnp.concatenate(heads, axis=0).T.astype(BF16)
+        heads = []
+        for h in range(4):
+            parts = [q_ref[h * 4 + a, i * 32 : i * 32 + 32, :].astype(F32) for a in range(4)]
+            heads.append(parts[0] + parts[1] + parts[2] + parts[3])
+        dq_ref[i] = jnp.concatenate(heads, axis=0).T.astype(BF16)
+        for first, out in ((0, dk_ref), (32, dv_ref)):
+            at = i * 64 + first
+            out[i] = turned(jnp.concatenate([kv_ref[h, at : at + 32, :] for h in range(4)], axis=0))
 
 
 def vmem(n=1):
@@ -207,22 +208,28 @@
     )(which, queries, out_grad, outputs, logsumexp, bias)
     got_key = lax.all_to_all(to_key, KEY_GROUP, 0, 0)
     got_query = lax.all_to_all(to_query, QUERY_GROUP, 0, 0)
-    dq_parts, dkv_parts, db_parts = pl.pallas_call(
+    yh = lax.axis_index("yh").astype(jnp.int32).reshape(1)
+    dq_parts, *dkv_parts, db_parts = pl.pallas_call(
         functools.partial(attend_kernel, scale),
-        out_shape=(shape(16, 128, 128), shape(16, 256, 128), shape(8, 256, 128)),
-        in_specs=vmem(2),
-        out_specs=tuple(vmem(3)),
+        out_shape=(shape(16, 128, 128),) + (shape(4, 256, 128),) * 4 + (shape(8, 256, 128),),
+        in_specs=[pl.BlockSpec(memory_space=pltpu.SMEM)] + vmem(2),
+        out_specs=tuple(vmem(6)),
         scratch_shapes=[pltpu.VMEM((512, 512), F32), pltpu.VMEM((512, 512), F32)],
         compiler_params=params(),
         name="attend",
-    )(got_query, got_key)
+    )(yh, got_query, got_key)
+    dkv = [dkv_parts[0]] + [
+        lax.ppermute(dkv_parts[p], "yh", [(n, (n + p) % 4) for n in range(4)]) for p in (2, 1, 3)
+    ]
     db = lax.all_to_all(db_parts, "z", 0, 0)
     db = jnp.sum(db.astype(F32), axis=0)
     db = lax.ppermute(db, ROW + ("xh", "yl"), bias_moves())
     db = db.reshape(2, 128, 2, 64).transpose(2, 0, 1, 3).reshape(4, 128, 64)
     bias_grad = lax.all_to_all(db, ("c", "yl"), 0, 0)
-    dkv = lax.all_to_all(dkv_parts, KEY_GROUP, 0, 0)
     dq = lax.all_to_all(dq_parts, QUERY_GROUP, 0, 0)
+    dkv, dq, bias_grad = lax.optimization_barrier((dkv, dq, bias_grad))
+    dkv = sum(part.astype(F32) for part in dkv).astype(BF16)
+    dkv = lax.all_to_all(dkv, ("xl", "c"), 0, 0)
     query_grad, key_grad, value_grad = pl.pallas_call(
         unpack_kernel,
         out_shape=(shape(4, 128, 128),) * 3,

time: 163 us -> 157 us (0.963)
  blocking collectives: 91.7 us -> 27.9 us
  waiting for transfers between devices: 32.5 us -> 68.2 us
  starting transfers between devices: 20.2 us -> 40.4 us
    all_to_all x3 -> x0, blocking collectives: 66.4 us -> none  [the longest x1 32.5 us: body(): dkv = lax.all_to_all(dkv_parts, KEY_GROUP, 0, 0)]
    all_to_all x0 -> x3, waiting for transfers between devices: none -> 28.3 us  [the longest x1 22.7 us: body(): got_query = lax.all_to_all(to_query, QUERY_GROUP, 0, 0)]
    ppermute x0 -> x3, waiting for transfers between devices: none -> 14.7 us  [body(): lax.ppermute(dkv_parts[p], 'yh', [(n, (n + p) % 4) for n in range(4)])]
    all_to_all x0 -> x3, starting transfers between devices: none -> 12.3 us  [the longest x1 4.59 us: body(): got_query = lax.all_to_all(to_query, QUERY_GROUP, 0, 0)]
    ppermute x0 -> x3, starting transfers between devices: none -> 10.1 us  [body(): lax.ppermute(dkv_parts[p], 'yh', [(n, (n + p) % 4) for n in range(4)])]
    ppermute x1, waiting for transfers between devices: 6.29 us -> 0.01 us  [body(): db = lax.ppermute(db, ROW + ('xh', 'yl'), bias_moves())]
    all_to_all x1, blocking collectives: 25.3 us -> 27.9 us  [body(): db = lax.all_to_all(db_parts, 'z', 0, 0)]
    all_to_all x1, starting transfers between devices: 6.31 us -> 4.05 us  [body(): dq = lax.all_to_all(dq_parts, QUERY_GROUP, 0, 0)]
  transfers between devices with their start and end apart: 3 -> 9, of which waited for: 3 -> 7; matrix products, arithmetic and copies ran while one was open for 0% -> 1% of each run, Pallas kernels for 2% -> 2%
where the time goes in v3:
time: 157 us; the launch traced here: 156 us
  waiting for transfers between devices  68.2 us (43%)
  starting transfers between devices  40.4 us (26%)
  blocking collectives  27.9 us (18%)
  Pallas kernels  16.4 us (10%)
    all_to_all x1, blocking collectives, body(): db = lax.all_to_all(db_parts, 'z', 0, 0)  27.9 us
    all_to_all x1, waiting for transfers between devices, body(): got_key = lax.all_to_all(to_key, KEY_GROUP, 0, 0)  25.2 us
    all_to_all x1, waiting for transfers between devices, body(): got_query = lax.all_to_all(to_query, QUERY_GROUP, 0, 0)  22.7 us
    ppermute x3, waiting for transfers between devices, body(): lax.ppermute(dkv_parts[p], 'yh', [(n, (n + p) % 4) for n in range(4)])  14.7 us
    pallas_call x1, Pallas kernels, body(): pl.pallas_call(functools.partial(attend_kernel, scale), out_shape=(shape(...  10.9 us
    all_to_all x1, starting transfers between devices, body(): got_key = lax.all_to_all(to_key, KEY_GROUP, 0, 0)  10.4 us
    ppermute x3, starting transfers between devices, body(): lax.ppermute(dkv_parts[p], 'yh', [(n, (n + p) % 4) for n in range(4)])  10.1 us
    all_to_all x1, waiting for transfers between devices, body(): dkv = lax.all_to_all(dkv, ('xl', 'c'), 0, 0)  5.17 us
  transfers between devices with their start and end apart: 9, of which 7 were waited for; matrix products, arithmetic and copies ran while one was open for 1% of the time, Pallas kernels for 2%

profile of v3, /device:TPU:1, one launch (start us, length us, event | category | flops | bytes accessed | tf_op | source)
XLA Modules:
  0.0 156.0 jit_solution(17942280160478872138)
XLA Ops:
  0.6 2.1 %pack_key.1 = bf16[16,256,128]{2,1,0:T(8,128)(2,1)} custom-call(bf16[4,128,128]{2,1,0:T(8,128)(2,1)} %k_hbm.1, bf16[4,128,128]{2,1,0:T(8,128)(2,1)} %v_hbm.1), custom_call_target="tpu_custom_call" | custom-call | tf_op jit(solution)/shard_map/pack_key/pallas_call | solution.py:190
  2.7 10.4 %all-to-all-start.1 = ((bf16[16,256,128]{2,1,0:T(8,128)(2,1)}), bf16[16,256,128]{2,1,0:T(8,128)(2,1)S(1)}, u32[]{:S(2)}, u32[]{:S(2)}) async-start(bf16[16,256,128]{2,1,0:T(8,128)(2,1)} %pack_key.1), calls=%async_computation.1 | async-start | bytes 2097152 | tf_op jit(solution)/shard_map/all_to_all | solution.py:209
  13.1 2.6 %pack_query.1 = bf16[16,416,128]{2,1,0:T(8,128)(2,1)} custom-call(s32[1]{0:T(128)} %bitcast.1.which_ref, bf16[4,128,128]{2,1,0:T(8,128)(2,1)} %q_hbm.1, bf16[4,128,128]{2,1,0:T(8,128)(2,1)} %g_hbm.1, bf16[4,128,128]{2,1,0:T(8,128)(2,1)} %o_hbm.1, f32[4,4,128]{2,1,0:T(4,128)} %l_hbm.1, bf16[4,128,2048]{2,1,0:T(8,128)(2,1)} %bias_hbm.1), custom_call_target="tpu_custom_call" | custom-call | tf_op jit(solution)/shard_map/pack_query/pallas_call | solution.py:199
  15.7 25.2 %all-to-all-done.1.kv_ref = bf16[16,256,128]{2,1,0:T(8,128)(2,1)S(1)} async-done(((bf16[16,256,128]{2,1,0:T(8,128)(2,1)}), bf16[16,256,128]{2,1,0:T(8,128)(2,1)S(1)}, u32[]{:S(2)}, u32[]{:S(2)}) %all-to-all-start.1) | async-done | bytes 1048608 | tf_op jit(solution)/shard_map/all_to_all | solution.py:209
  40.9 4.6 %all-to-all-start = ((bf16[16,416,128]{2,1,0:T(8,128)(2,1)}), bf16[16,416,128]{2,1,0:T(8,128)(2,1)S(1)}, u32[]{:S(2)}, u32[]{:S(2)}) async-start(bf16[16,416,128]{2,1,0:T(8,128)(2,1)} %pack_query.1), calls=%async_computation | async-start | bytes 3407872 | tf_op jit(solution)/shard_map/all_to_all | solution.py:210
  45.5 22.7 %all-to-all-done.jq_ref = bf16[16,416,128]{2,1,0:T(8,128)(2,1)S(1)} async-done(((bf16[16,416,128]{2,1,0:T(8,128)(2,1)}), bf16[16,416,128]{2,1,0:T(8,128)(2,1)S(1)}, u32[]{:S(2)}, u32[]{:S(2)}) %all-to-all-start) | async-done | bytes 1703968 | tf_op jit(solution)/shard_map/all_to_all | solution.py:210
  68.2 10.9 %attend.1 = (bf16[16,128,128]{2,1,0:T(8,128)(2,1)}, bf16[4,256,128]{2,1,0:T(8,128)(2,1)S(1)}, bf16[4,256,128]{2,1,0:T(8,128)(2,1)S(1)}, bf16[4,256,128]{2,1,0:T(...) custom-call(s32[1]{0:T(128)} %bitcast.yh_ref, ...), custom_call_target="tpu_custom_call" | custom-call | tf_op jit(solution)/shard_map/attend/pallas_call | solution.py:212
  79.0 27.9 %all_to_all.30 = bf16[8,256,128]{2,1,0:T(8,128)(2,1)S(1)} all-to-all(bf16[8,256,128]{2,1,0:T(8,128)(2,1)S(1)} %get-tuple-element.24), channel_id=1, replica_groups=mesh['xl'=2,'z'=8,'c'=2,'xh'=2,'yh'=4,'yl'=2] {'z'}, dimensions={0} | all-to-all | bytes 1048576 | tf_op jit(solution)/shard_map/all_to_all | solution.py:224
  106.9 0.0 copy-done
  106.9 0.0 copy-start.1
  106.9 4.1 %all-to-all-start.2 = ((bf16[16,128,128]{2,1,0:T(8,128)(2,1)}), bf16[16,128,128]{2,1,0:T(8,128)(2,1)S(1)}, u32[]{:S(2)}, u32[]{:S(2)}) async-start(bf16[16,128,128]{2,1,0:T(8,128)(2,1)} %get-tuple-element.23), calls=%async_computation.2 | async-start | bytes 1048576 | tf_op jit(solution)/shard_map/all_to_all | solution.py:229
  110.9 0.1 convert_reduce_fusion
  111.0 3.5 %collective-permute-start.3 = (f32[256,128]{1,0:T(8,128)S(1)}, f32[256,128]{1,0:T(8,128)S(1)}, u32[]{:S(2)}, u32[]{:S(2)}) collective-permute-start(f32[256,128]{1,0:T(8,128)S(1)} %convert_reduce_fusion), channel_id=1, source_target_pairs={{0,0},{1,32},{8,256},{9,288},{16,1},{17,33},{24,257},{25,289},{32,... | collective-permute-start | bytes 393224 | tf_op jit(solution)/shard_map/ppermute | solution.py:226
  114.5 0.0 copy-done.1
  114.6 2.7 %collective-permute-start = (bf16[4,256,128]{2,1,0:T(8,128)(2,1)S(1)}, bf16[4,256,128]{2,1,0:T(8,128)(2,1)S(1)}, u32[]{:S(2)}, u32[]{:S(2)}) collective-permute-start(bf16[4,256,128]{2,1,0:T(8,128)(2,1)S(1)} %copy-done.1), channel_id=1, source_target_pairs={{0,4},{2,6},{4,0},{6,2},{1,5},{3,7},{5,1},{7,3},{8,12},{10,14},{12... | collective-permute-start | bytes 786440 | tf_op jit(solution)/shard_map/ppermute | solution.py:222
  117.3 3.2 %collective-permute-start.1 = (bf16[4,256,128]{2,1,0:T(8,128)(2,1)S(1)}, bf16[4,256,128]{2,1,0:T(8,128)(2,1)S(1)}, u32[]{:S(2)}, u32[]{:S(2)}) collective-permute-start(bf16[4,256,128]{2,1,0:T(8,128)(2,1)S(1)} %get-tuple-element.21), channel_id=1, source_target_pairs={{0,2},{2,4},{4,6},{6,0},{1,3},{3,5},{5,7},{7,1},{8,10},{10,12},{12... | collective-permute-start | bytes 786440 | tf_op jit(solution)/shard_map/ppermute | solution.py:222
  120.5 4.2 %collective-permute-start.2 = (bf16[4,256,128]{2,1,0:T(8,128)(2,1)S(1)}, bf16[4,256,128]{2,1,0:T(8,128)(2,1)S(1)}, u32[]{:S(2)}, u32[]{:S(2)}) collective-permute-start(bf16[4,256,128]{2,1,0:T(8,128)(2,1)S(1)} %get-tuple-element.22), channel_id=1, source_target_pairs={{0,6},{2,0},{4,2},{6,4},{1,7},{3,1},{5,3},{7,5},{8,14},{10,8},{12,... | collective-permute-start | bytes 786440 | tf_op jit(solution)/shard_map/ppermute | solution.py:222
  124.7 0.0 collective-permute-done.3
  124.7 0.1 copy.12
  124.8 0.1 reshape.22
  124.9 0.7 copy.13
  125.6 0.0 all-to-all-done.2.q_ref
  125.6 3.3 %all-to-all-start.4 = ((f32[4,128,64]{1,2,0:T(8,128)}), f32[4,128,64]{1,2,0:T(8,128)S(1)}, u32[]{:S(2)}, u32[]{:S(2)}) async-start(f32[4,128,64]{1,2,0:T(8,128)} %bitcast.3), calls=%async_computation.4 | async-start | bytes 262144 | tf_op jit(solution)/shard_map/all_to_all | solution.py:228
  128.9 4.1 %collective-permute-done = bf16[4,256,128]{2,1,0:T(8,128)(2,1)S(1)} collective-permute-done((bf16[4,256,128]{2,1,0:T(8,128)(2,1)S(1)}, bf16[4,256,128]{2,1,0:T(8,128)(2,1)S(1)}, u32[]{:S(2)}, u32[]{:S(2)}) %collective-permute-start) | collective-permute-done | bytes 262176 | tf_op jit(solution)/shard_map/ppermute | solution.py:222
  132.9 8.9 %collective-permute-done.1 = bf16[4,256,128]{2,1,0:T(8,128)(2,1)S(1)} collective-permute-done((bf16[4,256,128]{2,1,0:T(8,128)(2,1)S(1)}, bf16[4,256,128]{2,1,0:T(8,128)(2,1)S(1)}, u32[]{:S(2)}, u32[]{:S(2)}) %collective-permute-start.1) | collective-permute-done | bytes 262176 | tf_op jit(solution)/shard_map/ppermute | solution.py:222
  141.8 1.8 %collective-permute-done.2 = bf16[4,256,128]{2,1,0:T(8,128)(2,1)S(1)} collective-permute-done((bf16[4,256,128]{2,1,0:T(8,128)(2,1)S(1)}, bf16[4,256,128]{2,1,0:T(8,128)(2,1)S(1)}, u32[]{:S(2)}, u32[]{:S(2)}) %collective-permute-start.2) | collective-permute-done | bytes 262176 | tf_op jit(solution)/shard_map/ppermute | solution.py:222
  143.6 0.4 all-to-all-done.4
  144.0 0.8 add_convert_fusion
  144.9 4.4 %all-to-all-start.5 = ((bf16[4,256,128]{2,1,0:T(8,128)(2,1)}), bf16[4,256,128]{2,1,0:T(8,128)(2,1)S(1)}, u32[]{:S(2)}, u32[]{:S(2)}) async-start(bf16[4,256,128]{2,1,0:T(8,128)(2,1)} %add_convert_fusion), calls=%async_computation.5 | async-start | bytes 524288 | tf_op jit(solution)/shard_map/all_to_all | solution.py:232
  149.3 5.2 %all-to-all-done.5.kv_ref = bf16[4,256,128]{2,1,0:T(8,128)(2,1)S(1)} async-done(((bf16[4,256,128]{2,1,0:T(8,128)(2,1)}), bf16[4,256,128]{2,1,0:T(8,128)(2,1)S(1)}, u32[]{:S(2)}, u32[]{:S(2)}) %all-to-all-start.5) | async-done | bytes 262176 | tf_op jit(solution)/shard_map/all_to_all | solution.py:232
  154.4 0.9 unpack.1
  155.3 0.7 copy.15
  (1 shorter events, 0.0 us)
Async XLA Ops:
  2.7 38.2 %all-to-all-start.1 = ((bf16[16,256,128]{2,1,0:T(8,128)(2,1)}), bf16[16,256,128]{2,1,0:T(8,128)(2,1)S(1)}, u32[]{:S(2)}, u32[]{:S(2)}) async-start(bf16[16,256,128]{2,1,0:T(8,128)(2,1)} %pack_key.1), calls=%async_computation.1 | async-start | bytes 2097152 | tf_op jit(solution)/shard_map/all_to_all | solution.py:209
  40.9 27.3 %all-to-all-start = ((bf16[16,416,128]{2,1,0:T(8,128)(2,1)}), bf16[16,416,128]{2,1,0:T(8,128)(2,1)S(1)}, u32[]{:S(2)}, u32[]{:S(2)}) async-start(bf16[16,416,128]{2,1,0:T(8,128)(2,1)} %pack_query.1), calls=%async_computation | async-start | bytes 3407872 | tf_op jit(solution)/shard_map/all_to_all | solution.py:210
  79.0 27.9 %copy-start = (bf16[4,256,128]{2,1,0:T(8,128)(2,1)}, bf16[4,256,128]{2,1,0:T(8,128)(2,1)S(1)}, u32[]{:S(2)}) copy-start(bf16[4,256,128]{2,1,0:T(8,128)(2,1)S(1)} %get-tuple-element.20) | copy-start | bytes 786436
  106.9 7.7 %copy-start.1 = (bf16[4,256,128]{2,1,0:T(8,128)(2,1)S(1)}, bf16[4,256,128]{2,1,0:T(8,128)(2,1)}, u32[]{:S(2)}) copy-start(bf16[4,256,128]{2,1,0:T(8,128)(2,1)} %copy-done) | copy-start | bytes 786436
  106.9 18.7 %all-to-all-start.2 = ((bf16[16,128,128]{2,1,0:T(8,128)(2,1)}), bf16[16,128,128]{2,1,0:T(8,128)(2,1)S(1)}, u32[]{:S(2)}, u32[]{:S(2)}) async-start(bf16[16,128,128]{2,1,0:T(8,128)(2,1)} %get-tuple-element.23), calls=%async_computation.2 | async-start | bytes 1048576 | tf_op jit(solution)/shard_map/all_to_all | solution.py:229
  111.0 13.7 %collective-permute-start.3 = (f32[256,128]{1,0:T(8,128)S(1)}, f32[256,128]{1,0:T(8,128)S(1)}, u32[]{:S(2)}, u32[]{:S(2)}) collective-permute-start(f32[256,128]{1,0:T(8,128)S(1)} %convert_reduce_fusion), channel_id=1, source_target_pairs={{0,0},{1,32},{8,256},{9,288},{16,1},{17,33},{24,257},{25,289},{32,... | collective-permute-start | bytes 393224 | tf_op jit(solution)/shard_map/ppermute | solution.py:226
  114.6 18.4 %collective-permute-start = (bf16[4,256,128]{2,1,0:T(8,128)(2,1)S(1)}, bf16[4,256,128]{2,1,0:T(8,128)(2,1)S(1)}, u32[]{:S(2)}, u32[]{:S(2)}) collective-permute-start(bf16[4,256,128]{2,1,0:T(8,128)(2,1)S(1)} %copy-done.1), channel_id=1, source_target_pairs={{0,4},{2,6},{4,0},{6,2},{1,5},{3,7},{5,1},{7,3},{8,12},{10,14},{12... | collective-permute-start | bytes 786440 | tf_op jit(solution)/shard_map/ppermute | solution.py:222
  117.3 24.6 %collective-permute-start.1 = (bf16[4,256,128]{2,1,0:T(8,128)(2,1)S(1)}, bf16[4,256,128]{2,1,0:T(8,128)(2,1)S(1)}, u32[]{:S(2)}, u32[]{:S(2)}) collective-permute-start(bf16[4,256,128]{2,1,0:T(8,128)(2,1)S(1)} %get-tuple-element.21), channel_id=1, source_target_pairs={{0,2},{2,4},{4,6},{6,0},{1,3},{3,5},{5,7},{7,1},{8,10},{10,12},{12... | collective-permute-start | bytes 786440 | tf_op jit(solution)/shard_map/ppermute | solution.py:222
  120.5 23.1 %collective-permute-start.2 = (bf16[4,256,128]{2,1,0:T(8,128)(2,1)S(1)}, bf16[4,256,128]{2,1,0:T(8,128)(2,1)S(1)}, u32[]{:S(2)}, u32[]{:S(2)}) collective-permute-start(bf16[4,256,128]{2,1,0:T(8,128)(2,1)S(1)} %get-tuple-element.22), channel_id=1, source_target_pairs={{0,6},{2,0},{4,2},{6,4},{1,7},{3,1},{5,3},{7,5},{8,14},{10,8},{12,... | collective-permute-start | bytes 786440 | tf_op jit(solution)/shard_map/ppermute | solution.py:222
  125.6 18.5 %all-to-all-start.4 = ((f32[4,128,64]{1,2,0:T(8,128)}), f32[4,128,64]{1,2,0:T(8,128)S(1)}, u32[]{:S(2)}, u32[]{:S(2)}) async-start(f32[4,128,64]{1,2,0:T(8,128)} %bitcast.3), calls=%async_computation.4 | async-start | bytes 262144 | tf_op jit(solution)/shard_map/all_to_all | solution.py:228
  144.9 9.6 %all-to-all-start.5 = ((bf16[4,256,128]{2,1,0:T(8,128)(2,1)}), bf16[4,256,128]{2,1,0:T(8,128)(2,1)S(1)}, u32[]{:S(2)}, u32[]{:S(2)}) async-start(bf16[4,256,128]{2,1,0:T(8,128)(2,1)} %add_convert_fusion), calls=%async_computation.5 | async-start | bytes 524288 | tf_op jit(solution)/shard_map/all_to_all | solution.py:232

commit v4 on v3

--- a/solution.py
+++ b/solution.py
@@ -95,8 +95,8 @@
                 ]
 
 
-def attend_kernel(scale, yh_ref, jq_ref, kv_ref, dq_ref, dkv0_ref, dkv1_ref, dkv2_ref, dkv3_ref, db_ref, bias_s, acc_s):
-    dkv_refs = (dkv0_ref, dkv1_ref, dkv2_ref, dkv3_ref)
+def attend_kernel(scale, yh_ref, jq_ref, kv_ref, dq_ref, dkv0_ref, dkv1_ref, dk2_ref, dv2_ref, dkv3_ref, db_ref, bias_s, acc_s):
+    dkv_refs = (dkv0_ref, dkv1_ref, None, dkv3_ref)
     owner = [lax.rem(yh_ref[0] + p, 4) for p in range(4)]
     for a in range(4):
         for s in range(4):
@@ -139,25 +139,56 @@
             for b in range(4):
                 block = slice(b * 128, b * 128 + 128)
                 dq_ref[base + b, i * 32 : i * 32 + 32, :] = dq[:, block]
-                dkv_refs[b][s, first : first + 32, :] = dk[:, block]
-                dkv_refs[b][s, first + 32 : first + 64, :] = dv[:, block]
+                low_at, high_at = slice(i * 32, i * 32 + 32), slice(128 + i * 32, 160 + i * 32)
+                if b == 2:
+                    dk2_ref[s, low_at, :] = dk[:, block]
+                    dv2_ref[s, low_at, :] = dv[:, block]
+                else:
+                    dkv_refs[b][s, low_at, :] = dk[:, block]
+                    dkv_refs[b][s, high_at, :] = dv[:, block]
         return carry
 
     lax.fori_loop(0, 4, four_rows, 0)
     for p in range(4):
-        for half in range(2):
-            db_ref[owner[p] * 2 + half] = acc_s[half * 256 : half * 256 + 256, p * 128 : p * 128 + 128].astype(BF16)
-
-
-def unpack_kernel(q_ref, kv_ref, dq_ref, dk_ref, dv_ref):
+        for xh in range(2):
+            for yl in range(2):
+                j = (xh * 2 + yl) * 128
+                db_ref[owner[p] * 4 + yl * 2 + xh] = acc_s[j : j + 128, p * 128 : p * 128 + 128].astype(BF16)
+
+
+def fold_kernel(up_ref, up_more_ref, down_ref, down_more_ref, up_out_ref, down_out_ref):
+    for s in range(4):
+        up_out_ref[s, :128, :] = (up_ref[s, :128, :].astype(F32) + up_more_ref[s].astype(F32)).astype(BF16)
+        up_out_ref[s, 128:, :] = up_ref[s, 128:, :]
+        down_out_ref[s, :128, :] = down_ref[s, :128, :]
+        down_out_ref[s, 128:, :] = (down_ref[s, 128:, :].astype(F32) + down_more_ref[s].astype(F32)).astype(BF16)
+
+
+def join_kernel(own_ref, up_ref, down_ref, db_ref, out_ref):
+    for s in range(4):
+        total = own_ref[s].astype(F32) + up_ref[s].astype(F32) + down_ref[s].astype(F32)
+        out_ref[s, :256, :] = total.astype(BF16)
+    first_half = lax.broadcasted_iota(jnp.int32, (128, 128), 1) < 64
+    for xl in range(2):
+        whole = db_ref[xl]
+        high = whole.astype(BF16).astype(F32)
+        low = whole - high
+        out_ref[xl * 2, 256:, :] = jnp.where(first_half, high, pltpu.roll(low, 64, 1)).astype(BF16)
+        out_ref[xl * 2 + 1, 256:, :] = jnp.where(first_half, pltpu.roll(high, 64, 1), low).astype(BF16)
+
+
+def unpack_kernel(q_ref, kv_ref, dq_ref, dk_ref, dv_ref, db_ref):
+    for h in range(4):
+        parts = kv_ref[h, 256:, :].astype(F32)
+        db_ref[h] = (parts + pltpu.roll(parts, 64, 1)).T[:64]
     for i in range(4):
         heads = []
         for h in range(4):
             parts = [q_ref[h * 4 + a, i * 32 : i * 32 + 32, :].astype(F32) for a in range(4)]
             heads.append(parts[0] + parts[1] + parts[2] + parts[3])
         dq_ref[i] = jnp.concatenate(heads, axis=0).T.astype(BF16)
-        for first, out in ((0, dk_ref), (32, dv_ref)):
-            at = i * 64 + first
+        for first, out in ((0, dk_ref), (128, dv_ref)):
+            at = i * 32 + first
             out[i] = turned(jnp.concatenate([kv_ref[h, at : at + 32, :] for h in range(4)], axis=0))
 
 
@@ -169,17 +200,12 @@
     return pltpu.CompilerParams(vmem_limit_bytes=mib * 2**20)
 
 
-def bias_moves():
-    pairs = []
-    for xl in range(2):
-        for z in range(8):
-            for c in range(2):
-                for xh in range(2):
-                    for yl in range(2):
-                        source = (((xl * 8 + z) * 2 + c) * 2 + xh) * 2 + yl
-                        target = (((xh * 8 + (z // 2) * 2 + yl) * 2 + xl) * 2 + z % 2) * 2 + c
-                        pairs.append((source, target))
-    return pairs
+def swaps():
+    return [(z * 2 + yl, ((z // 2) * 2 + yl) * 2 + z % 2) for z in range(8) for yl in range(2)]
+
+
+def along(value, steps):
+    return lax.ppermute(value, "yh", [(n, (n + steps) % 4) for n in range(4)])
 
 
 def body(queries, keys, values, bias, out_grad, outputs, logsumexp):
@@ -209,36 +235,52 @@
     got_key = lax.all_to_all(to_key, KEY_GROUP, 0, 0)
     got_query = lax.all_to_all(to_query, QUERY_GROUP, 0, 0)
     yh = lax.axis_index("yh").astype(jnp.int32).reshape(1)
-    dq_parts, *dkv_parts, db_parts = pl.pallas_call(
+    dq_parts, own, up, dk_far, dv_far, down, db_parts = pl.pallas_call(
         functools.partial(attend_kernel, scale),
-        out_shape=(shape(16, 128, 128),) + (shape(4, 256, 128),) * 4 + (shape(8, 256, 128),),
+        out_shape=(shape(16, 128, 128),)
+        + (shape(4, 256, 128),) * 2
+        + (shape(4, 128, 128),) * 2
+        + (shape(4, 256, 128), shape(16, 128, 128)),
         in_specs=[pl.BlockSpec(memory_space=pltpu.SMEM)] + vmem(2),
-        out_specs=tuple(vmem(6)),
+        out_specs=tuple(vmem(7)),
         scratch_shapes=[pltpu.VMEM((512, 512), F32), pltpu.VMEM((512, 512), F32)],
         compiler_params=params(),
         name="attend",
     )(yh, got_query, got_key)
-    dkv = [dkv_parts[0]] + [
-        lax.ppermute(dkv_parts[p], "yh", [(n, (n + p) % 4) for n in range(4)]) for p in (2, 1, 3)
-    ]
-    db = lax.all_to_all(db_parts, "z", 0, 0)
-    db = jnp.sum(db.astype(F32), axis=0)
-    db = lax.ppermute(db, ROW + ("xh", "yl"), bias_moves())
-    db = db.reshape(2, 128, 2, 64).transpose(2, 0, 1, 3).reshape(4, 128, 64)
-    bias_grad = lax.all_to_all(db, ("c", "yl"), 0, 0)
+    up_more, down_more = along(dk_far, 1), along(dv_far, -1)
+    up, down = pl.pallas_call(
+        fold_kernel,
+        out_shape=(shape(4, 256, 128),) * 2,
+        in_specs=vmem(4),
+        out_specs=tuple(vmem(2)),
+        compiler_params=params(),
+        name="fold",
+    )(up, up_more, down, down_more)
+    db = lax.all_to_all(db_parts, ("z", "xh"), 0, 0)
+    up, down, db, dq_parts = lax.optimization_barrier((up, down, db, dq_parts))
+    up, down = along(up, 1), along(down, -1)
+    db = jnp.sum(db.reshape(8, 2, 128, 128).astype(F32), axis=0)
+    db = lax.ppermute(db, ("z", "yl"), swaps())
     dq = lax.all_to_all(dq_parts, QUERY_GROUP, 0, 0)
-    dkv, dq, bias_grad = lax.optimization_barrier((dkv, dq, bias_grad))
-    dkv = sum(part.astype(F32) for part in dkv).astype(BF16)
-    dkv = lax.all_to_all(dkv, ("xl", "c"), 0, 0)
-    query_grad, key_grad, value_grad = pl.pallas_call(
+    up, down, db, dq = lax.optimization_barrier((up, down, db, dq))
+    joined = pl.pallas_call(
+        join_kernel,
+        out_shape=shape(4, 384, 128),
+        in_specs=vmem(4),
+        out_specs=vmem()[0],
+        compiler_params=params(),
+        name="join",
+    )(own, up, down, db)
+    joined = lax.all_to_all(joined, ("xl", "c"), 0, 0)
+    query_grad, key_grad, value_grad, bias_grad = pl.pallas_call(
         unpack_kernel,
-        out_shape=(shape(4, 128, 128),) * 3,
+        out_shape=(shape(4, 128, 128),) * 3 + (jax.ShapeDtypeStruct((4, 64, 128), F32),),
         in_specs=vmem(2),
-        out_specs=tuple(vmem(3)),
+        out_specs=tuple(vmem(4)),
         compiler_params=params(),
         name="unpack",
-    )(dq, dkv)
-    return query_grad, key_grad, value_grad, bias_grad
+    )(dq, joined)
+    return query_grad, key_grad, value_grad, bias_grad.transpose(0, 2, 1)
 
 
 def solution(mesh):

time: 157 us -> 147 us (0.936); the launches traced: 156 us -> 144 us
  blocking collectives: 27.9 us -> 10.2 us
  starting transfers between devices: 40.4 us -> 46.8 us
    all_to_all x1, blocking collectives: 27.9 us -> 10.2 us  [body(): joined = lax.all_to_all(joined, ('xl', 'c'), 0, 0)]
    all_to_all x2 -> x1, starting transfers between devices: 7.73 us -> 10.6 us  [body(): db = lax.all_to_all(db_parts, ('z', 'xh'), 0, 0)]
    ppermute x4 -> x5, waiting for transfers between devices: 14.7 us -> 12.9 us  [the longest x4 12.9 us: along(): return lax.ppermute(value, 'yh', [(n, (n + steps) % 4) for n in range(4)])]
    ppermute x4 -> x5, starting transfers between devices: 13.7 us -> 15.4 us  [the longest x4 14.8 us: along(): return lax.ppermute(value, 'yh', [(n, (n + steps) % 4) for n in range(4)])]
    all_to_all x1, starting transfers between devices: 4.05 us -> 5.83 us  [body(): dq = lax.all_to_all(dq_parts, QUERY_GROUP, 0, 0)]
    all_to_all x2 -> x1, waiting for transfers between devices: 5.58 us -> 7.15 us  [body(): db = lax.all_to_all(db_parts, ('z', 'xh'), 0, 0)]
  transfers between devices with their start and end apart: 9 -> 9, of which waited for: 7 -> 6; matrix products, arithmetic and copies ran while one was open for 1% -> 0% of each run, Pallas kernels for 2% -> 2%
where the time goes in v4:
time: 147 us; the launch traced here: 144 us
  waiting for transfers between devices  67.9 us (46%)
  starting transfers between devices  46.8 us (32%)
  Pallas kernels  17 us (12%)
  blocking collectives  10.2 us (7%)
    all_to_all x1, waiting for transfers between devices, body(): got_key = lax.all_to_all(to_key, KEY_GROUP, 0, 0)  25.2 us
    all_to_all x1, waiting for transfers between devices, body(): got_query = lax.all_to_all(to_query, QUERY_GROUP, 0, 0)  22.7 us
    ppermute x4, starting transfers between devices, along(): return lax.ppermute(value, 'yh', [(n, (n + steps) % 4) for n in range(4)])  14.8 us
    ppermute x4, waiting for transfers between devices, along(): return lax.ppermute(value, 'yh', [(n, (n + steps) % 4) for n in range(4)])  12.9 us
    pallas_call x1, Pallas kernels, body(): pl.pallas_call(functools.partial(attend_kernel, scale), out_shape=(shape(...  11 us
    all_to_all x1, starting transfers between devices, body(): db = lax.all_to_all(db_parts, ('z', 'xh'), 0, 0)  10.6 us
    all_to_all x1, starting transfers between devices, body(): got_key = lax.all_to_all(to_key, KEY_GROUP, 0, 0)  10.4 us
    all_to_all x1, blocking collectives, body(): joined = lax.all_to_all(joined, ('xl', 'c'), 0, 0)  10.2 us
  transfers between devices with their start and end apart: 9, of which 6 were waited for; matrix products, arithmetic and copies ran while one was open for 0% of the time, Pallas kernels for 2%

profile of v4, /device:TPU:1, one launch (start us, length us, event | category | flops | bytes accessed | tf_op | source)
XLA Modules:
  0.0 144.0 jit_solution(12290719905853820517)
XLA Ops:
  0.6 2.1 %pack_key.1 = bf16[16,256,128]{2,1,0:T(8,128)(2,1)} custom-call(bf16[4,128,128]{2,1,0:T(8,128)(2,1)} %k_hbm.1, bf16[4,128,128]{2,1,0:T(8,128)(2,1)} %v_hbm.1), custom_call_target="tpu_custom_call" | custom-call | tf_op jit(solution)/shard_map/pack_key/pallas_call | solution.py:216
  2.7 10.4 %all-to-all-start.1 = ((bf16[16,256,128]{2,1,0:T(8,128)(2,1)}), bf16[16,256,128]{2,1,0:T(8,128)(2,1)S(1)}, u32[]{:S(2)}, u32[]{:S(2)}) async-start(bf16[16,256,128]{2,1,0:T(8,128)(2,1)} %pack_key.1), calls=%async_computation.1 | async-start | bytes 2097152 | tf_op jit(solution)/shard_map/all_to_all | solution.py:235
  13.1 2.6 %pack_query.1 = bf16[16,416,128]{2,1,0:T(8,128)(2,1)} custom-call(s32[1]{0:T(128)} %bitcast.1.which_ref, bf16[4,128,128]{2,1,0:T(8,128)(2,1)} %q_hbm.1, bf16[4,128,128]{2,1,0:T(8,128)(2,1)} %g_hbm.1, bf16[4,128,128]{2,1,0:T(8,128)(2,1)} %o_hbm.1, f32[4,4,128]{2,1,0:T(4,128)} %l_hbm.1, bf16[4,128,2048]{2,1,0:T(8,128)(2,1)} %bias_hbm.1), custom_call_target="tpu_custom_call" | custom-call | tf_op jit(solution)/shard_map/pack_query/pallas_call | solution.py:225
  15.7 25.2 %all-to-all-done.1.kv_ref = bf16[16,256,128]{2,1,0:T(8,128)(2,1)S(1)} async-done(((bf16[16,256,128]{2,1,0:T(8,128)(2,1)}), bf16[16,256,128]{2,1,0:T(8,128)(2,1)S(1)}, u32[]{:S(2)}, u32[]{:S(2)}) %all-to-all-start.1) | async-done | bytes 1048608 | tf_op jit(solution)/shard_map/all_to_all | solution.py:235
  40.9 4.6 %all-to-all-start = ((bf16[16,416,128]{2,1,0:T(8,128)(2,1)}), bf16[16,416,128]{2,1,0:T(8,128)(2,1)S(1)}, u32[]{:S(2)}, u32[]{:S(2)}) async-start(bf16[16,416,128]{2,1,0:T(8,128)(2,1)} %pack_query.1), calls=%async_computation | async-start | bytes 3407872 | tf_op jit(solution)/shard_map/all_to_all | solution.py:236
  45.5 22.7 %all-to-all-done.jq_ref = bf16[16,416,128]{2,1,0:T(8,128)(2,1)S(1)} async-done(((bf16[16,416,128]{2,1,0:T(8,128)(2,1)}), bf16[16,416,128]{2,1,0:T(8,128)(2,1)S(1)}, u32[]{:S(2)}, u32[]{:S(2)}) %all-to-all-start) | async-done | bytes 1703968 | tf_op jit(solution)/shard_map/all_to_all | solution.py:236
  68.2 11.0 %attend.1 = (bf16[16,128,128]{2,1,0:T(8,128)(2,1)}, bf16[4,256,128]{2,1,0:T(8,128)(2,1)S(1)}, bf16[4,256,128]{2,1,0:T(8,128)(2,1)S(1)}, bf16[4,128,128]{2,1,0:T(...) custom-call(s32[1]{0:T(128)} %bitcast.yh_ref, ...), custom_call_target="tpu_custom_call" | custom-call | tf_op jit(solution)/shard_map/attend/pallas_call | solution.py:238
  79.2 0.0 copy-start
  79.2 0.7 copy-done
  79.9 0.0 copy-start.1
  79.9 0.7 copy-done.1
  80.5 10.6 %all-to-all-start.2 = ((bf16[16,128,128]{2,1,0:T(8,128)(2,1)}), bf16[16,128,128]{2,1,0:T(8,128)(2,1)S(1)}, u32[]{:S(2)}, u32[]{:S(2)}) async-start(bf16[16,128,128]{2,1,0:T(8,128)(2,1)} %get-tuple-element.31), calls=%async_computation.2 | async-start | bytes 1048576 | tf_op jit(solution)/shard_map/all_to_all | solution.py:259
  91.1 2.6 %collective-permute-start = (bf16[4,128,128]{2,1,0:T(8,128)(2,1)}, bf16[4,128,128]{2,1,0:T(8,128)(2,1)S(1)}, u32[]{:S(2)}, u32[]{:S(2)}) collective-permute-start(bf16[4,128,128]{2,1,0:T(8,128)(2,1)} %copy-done.1), channel_id=1, source_target_pairs={{0,2},{2,4},{4,6},{6,0},{1,3},{3,5},{5,7},{7,1},{8,10},{10,12},{12... | collective-permute-start | bytes 393224 | tf_op jit(solution)/shard_map/ppermute | solution.py:208
  93.8 4.8 %collective-permute-start.1 = (bf16[4,128,128]{2,1,0:T(8,128)(2,1)}, bf16[4,128,128]{2,1,0:T(8,128)(2,1)S(1)}, u32[]{:S(2)}, u32[]{:S(2)}) collective-permute-start(bf16[4,128,128]{2,1,0:T(8,128)(2,1)} %copy-done), channel_id=1, source_target_pairs={{0,6},{2,0},{4,2},{6,4},{1,7},{3,1},{5,3},{7,5},{8,14},{10,8},{12,... | collective-permute-start | bytes 393224 | tf_op jit(solution)/shard_map/ppermute | solution.py:208
  98.5 1.0 collective-permute-done.up_more_ref
  99.5 1.6 %collective-permute-done.1.down_more_ref = bf16[4,128,128]{2,1,0:T(8,128)(2,1)S(1)} collective-permute-done((bf16[4,128,128]{2,1,0:T(8,128)(2,1)}, bf16[4,128,128]{2,1,0:T(8,128)(2,1)S(1)}, u32[]{:S(2)}, u32[]{:S(2)}) %collective-permute-start.1) | collective-permute-done | bytes 131104 | tf_op jit(solution)/shard_map/ppermute | solution.py:208
  101.1 0.1 fold.1
  101.2 7.2 %all-to-all-done.2 = bf16[16,128,128]{2,1,0:T(8,128)(2,1)S(1)} async-done(((bf16[16,128,128]{2,1,0:T(8,128)(2,1)}), bf16[16,128,128]{2,1,0:T(8,128)(2,1)S(1)}, u32[]{:S(2)}, u32[]{:S(2)}) %all-to-all-start.2) | async-done | bytes 524320 | tf_op jit(solution)/shard_map/all_to_all | solution.py:259
  108.3 5.8 %all-to-all-start.3 = ((bf16[16,128,128]{2,1,0:T(8,128)(2,1)}), bf16[16,128,128]{2,1,0:T(8,128)(2,1)S(1)}, u32[]{:S(2)}, u32[]{:S(2)}) async-start(bf16[16,128,128]{2,1,0:T(8,128)(2,1)} %get-tuple-element.36), calls=%async_computation.3 | async-start | bytes 1048576 | tf_op jit(solution)/shard_map/all_to_all | solution.py:264
  114.2 2.6 %collective-permute-start.2 = (bf16[4,256,128]{2,1,0:T(8,128)(2,1)S(1)}, bf16[4,256,128]{2,1,0:T(8,128)(2,1)S(1)}, u32[]{:S(2)}, u32[]{:S(2)}) collective-permute-start(bf16[4,256,128]{2,1,0:T(8,128)(2,1)S(1)} %get-tuple-element.33), channel_id=1, source_target_pairs={{0,2},{2,4},{4,6},{6,0},{1,3},{3,5},{5,7},{7,1},{8,10},{10,12},{12... | collective-permute-start | bytes 786440 | tf_op jit(solution)/shard_map/ppermute | solution.py:208
  116.8 4.8 %collective-permute-start.3 = (bf16[4,256,128]{2,1,0:T(8,128)(2,1)S(1)}, bf16[4,256,128]{2,1,0:T(8,128)(2,1)S(1)}, u32[]{:S(2)}, u32[]{:S(2)}) collective-permute-start(bf16[4,256,128]{2,1,0:T(8,128)(2,1)S(1)} %get-tuple-element.34), channel_id=1, source_target_pairs={{0,6},{2,0},{4,2},{6,4},{1,7},{3,1},{5,3},{7,5},{8,14},{10,8},{12,... | collective-permute-start | bytes 786440 | tf_op jit(solution)/shard_map/ppermute | solution.py:208
  121.5 0.1 convert_reduce_fusion
  121.6 0.7 collective-permute-start.4
  122.3 0.0 collective-permute-done.4.db_ref
  122.3 10.3 %collective-permute-done.2.up_ref = bf16[4,256,128]{2,1,0:T(8,128)(2,1)S(1)} collective-permute-done((bf16[4,256,128]{2,1,0:T(8,128)(2,1)S(1)}, bf16[4,256,128]{2,1,0:T(8,128)(2,1)S(1)}, u32[]{:S(2)}, u32[]{:S(2)}) %collective-permute-start.2) | collective-permute-done | bytes 262176 | tf_op jit(solution)/shard_map/ppermute | solution.py:208
  132.6 0.0 collective-permute-done.3.down_ref
  132.6 0.0 all-to-all-done.3.q_ref
  132.6 0.2 join.1
  132.8 10.2 %all_to_all.25.kv_ref = bf16[4,384,128]{2,1,0:T(8,128)(2,1)S(1)} all-to-all(bf16[4,384,128]{2,1,0:T(8,128)(2,1)S(1)} %join.1), channel_id=1, replica_groups=mesh['xl'=2,'z'=8,'c'=2,'xh'=2,'yh'=4,'yl'=2] {'xl','c'}, dimensions={0} | all-to-all | bytes 786432 | tf_op jit(solution)/shard_map/all_to_all | solution.py:274
  143.0 1.0 unpack.1
Async XLA Ops:
  2.7 38.2 %all-to-all-start.1 = ((bf16[16,256,128]{2,1,0:T(8,128)(2,1)}), bf16[16,256,128]{2,1,0:T(8,128)(2,1)S(1)}, u32[]{:S(2)}, u32[]{:S(2)}) async-start(bf16[16,256,128]{2,1,0:T(8,128)(2,1)} %pack_key.1), calls=%async_computation.1 | async-start | bytes 2097152 | tf_op jit(solution)/shard_map/all_to_all | solution.py:235
  40.9 27.3 %all-to-all-start = ((bf16[16,416,128]{2,1,0:T(8,128)(2,1)}), bf16[16,416,128]{2,1,0:T(8,128)(2,1)S(1)}, u32[]{:S(2)}, u32[]{:S(2)}) async-start(bf16[16,416,128]{2,1,0:T(8,128)(2,1)} %pack_query.1), calls=%async_computation | async-start | bytes 3407872 | tf_op jit(solution)/shard_map/all_to_all | solution.py:236
  79.2 0.7 copy-start
  79.9 0.7 copy-start.1
  80.5 27.8 %all-to-all-start.2 = ((bf16[16,128,128]{2,1,0:T(8,128)(2,1)}), bf16[16,128,128]{2,1,0:T(8,128)(2,1)S(1)}, u32[]{:S(2)}, u32[]{:S(2)}) async-start(bf16[16,128,128]{2,1,0:T(8,128)(2,1)} %get-tuple-element.31), calls=%async_computation.2 | async-start | bytes 1048576 | tf_op jit(solution)/shard_map/all_to_all | solution.py:259
  91.1 8.4 %collective-permute-start = (bf16[4,128,128]{2,1,0:T(8,128)(2,1)}, bf16[4,128,128]{2,1,0:T(8,128)(2,1)S(1)}, u32[]{:S(2)}, u32[]{:S(2)}) collective-permute-start(bf16[4,128,128]{2,1,0:T(8,128)(2,1)} %copy-done.1), channel_id=1, source_target_pairs={{0,2},{2,4},{4,6},{6,0},{1,3},{3,5},{5,7},{7,1},{8,10},{10,12},{12... | collective-permute-start | bytes 393224 | tf_op jit(solution)/shard_map/ppermute | solution.py:208
  93.8 7.3 %collective-permute-start.1 = (bf16[4,128,128]{2,1,0:T(8,128)(2,1)}, bf16[4,128,128]{2,1,0:T(8,128)(2,1)S(1)}, u32[]{:S(2)}, u32[]{:S(2)}) collective-permute-start(bf16[4,128,128]{2,1,0:T(8,128)(2,1)} %copy-done), channel_id=1, source_target_pairs={{0,6},{2,0},{4,2},{6,4},{1,7},{3,1},{5,3},{7,5},{8,14},{10,8},{12,... | collective-permute-start | bytes 393224 | tf_op jit(solution)/shard_map/ppermute | solution.py:208
  108.3 24.3 %all-to-all-start.3 = ((bf16[16,128,128]{2,1,0:T(8,128)(2,1)}), bf16[16,128,128]{2,1,0:T(8,128)(2,1)S(1)}, u32[]{:S(2)}, u32[]{:S(2)}) async-start(bf16[16,128,128]{2,1,0:T(8,128)(2,1)} %get-tuple-element.36), calls=%async_computation.3 | async-start | bytes 1048576 | tf_op jit(solution)/shard_map/all_to_all | solution.py:264
  114.2 18.5 %collective-permute-start.2 = (bf16[4,256,128]{2,1,0:T(8,128)(2,1)S(1)}, bf16[4,256,128]{2,1,0:T(8,128)(2,1)S(1)}, u32[]{:S(2)}, u32[]{:S(2)}) collective-permute-start(bf16[4,256,128]{2,1,0:T(8,128)(2,1)S(1)} %get-tuple-element.33), channel_id=1, source_target_pairs={{0,2},{2,4},{4,6},{6,0},{1,3},{3,5},{5,7},{7,1},{8,10},{10,12},{12... | collective-permute-start | bytes 786440 | tf_op jit(solution)/shard_map/ppermute | solution.py:208
  116.8 15.8 %collective-permute-start.3 = (bf16[4,256,128]{2,1,0:T(8,128)(2,1)S(1)}, bf16[4,256,128]{2,1,0:T(8,128)(2,1)S(1)}, u32[]{:S(2)}, u32[]{:S(2)}) collective-permute-start(bf16[4,256,128]{2,1,0:T(8,128)(2,1)S(1)} %get-tuple-element.34), channel_id=1, source_target_pairs={{0,6},{2,0},{4,2},{6,4},{1,7},{3,1},{5,3},{7,5},{8,14},{10,8},{12,... | collective-permute-start | bytes 786440 | tf_op jit(solution)/shard_map/ppermute | solution.py:208
  121.6 0.7 collective-permute-start.4

commit v5 on v4

--- a/solution.py
+++ b/solution.py
@@ -17,11 +17,9 @@
 F32, BF16 = jnp.float32, jnp.bfloat16
 
 
-def three_parts(x):
+def two_parts(x):
     high = x.astype(BF16).astype(F32)
-    rest = x - high
-    mid = rest.astype(BF16).astype(F32)
-    return high, mid, rest - mid
+    return high, x - high
 
 
 def fetch(pairs, sems):
@@ -65,32 +63,30 @@
     lines = lax.broadcasted_iota(jnp.int32, (AUG, 128), 0)
     for copy in copies[:4]:
         copy.wait()
-    for pair in range(2):
-        extra = [jnp.zeros((AUG, 128), F32)] * 4
-        for n in range(2):
-            i = pair * 2 + n
-            q_t = turned(q_ref[i])
-            g_f = g_ref[i].astype(F32)
-            gg = (g_f * o_ref[i].astype(F32)).T
-            g_t = g_f.T.astype(BF16)
-            for h in range(4):
-                part = slice(h * 32, h * 32 + 32)
-                offset = l_ref[i, h : h + 1, :] * (-1.0 / scale)
-                delta = -jnp.sum(gg[part], axis=0, keepdims=True)
-                for at, piece in enumerate(three_parts(offset) + three_parts(delta)):
-                    extra[h] = jnp.where(lines == n * 6 + at, piece, extra[h])
-                for a in range(4):
-                    to_query_ref[h * 4 + a, i * 64 : i * 64 + 32, :] = q_t[part]
-                    to_query_ref[h * 4 + a, i * 64 + 32 : i * 64 + 64, :] = g_t[part]
+    extra = [jnp.zeros((AUG, 128), F32)] * 4
+    for i in range(4):
+        q_t = turned(q_ref[i])
+        g_f = g_ref[i].astype(F32)
+        gg = (g_f * o_ref[i].astype(F32)).T
+        g_t = g_f.T.astype(BF16)
         for h in range(4):
+            part = slice(h * 32, h * 32 + 32)
+            offset = l_ref[i, h : h + 1, :] * (-1.0 / scale)
+            delta = -jnp.sum(gg[part], axis=0, keepdims=True)
+            for at, piece in enumerate(two_parts(offset) + two_parts(delta)):
+                extra[h] = jnp.where(lines == i * 4 + at, piece, extra[h])
             for a in range(4):
-                to_query_ref[h * 4 + a, 256 + pair * 16 : 272 + pair * 16, :] = extra[h].astype(BF16)
+                to_query_ref[h * 4 + a, i * 64 : i * 64 + 32, :] = q_t[part]
+                to_query_ref[h * 4 + a, i * 64 + 32 : i * 64 + 64, :] = g_t[part]
+    for h in range(4):
+        for a in range(4):
+            to_query_ref[h * 4 + a, 256:272, :] = extra[h].astype(BF16)
     copies[4].wait()
     for h in range(4):
         for a in range(4):
             for yh in range(4):
                 block = (a // 2) * 8 + yh * 2 + a % 2
-                to_query_ref[h * 4 + a, 288 + yh * 32 : 320 + yh * 32, :] = bias_ref[
+                to_query_ref[h * 4 + a, 272 + yh * 32 : 304 + yh * 32, :] = bias_ref[
                     h, :, block * 128 : block * 128 + 128
                 ]
 
@@ -102,22 +98,21 @@
         for s in range(4):
             for p in range(4):
                 bias_s[a * 128 + s * 32 : a * 128 + s * 32 + 32, p * 128 : p * 128 + 128] = (
-                    jq_ref[s * 4 + a, pl.ds(pl.multiple_of(288 + owner[p] * 32, 32), 32), :].astype(F32) * LOG2E
+                    jq_ref[s * 4 + a, pl.ds(pl.multiple_of(272 + owner[p] * 32, 16), 32), :].astype(F32) * LOG2E
                 )
     acc_s[...] = jnp.zeros_like(acc_s)
     lines = lax.broadcasted_iota(jnp.int32, (AUG, 512), 0)
     ones = [
-        jnp.where((lines >= first) & (lines < first + 3), 1.0, 0.0).astype(BF16) for first in (0, 3, 6, 9)
+        jnp.where((lines >= first) & (lines < first + 2), 1.0, 0.0).astype(BF16) for first in range(0, 16, 2)
     ]
 
     def four_rows(s, carry):
         base = s * 4
         for i in range(4):
             first = i * 64
-            at = 256 + (i // 2) * 16
             q_t, g_t, extra = (
                 jnp.concatenate([jq_ref[base + a, start : start + size, :] for a in range(4)], axis=1)
-                for start, size in ((first, 32), (first + 32, 32), (at, 16))
+                for start, size in ((first, 32), (first + 32, 32), (256, 16))
             )
             k_t, v_t = (
                 jnp.concatenate([kv_ref[base + owner[p], start : start + 32, :] for p in range(4)], axis=1)
@@ -125,8 +120,8 @@
             )
             q_rows = jnp.concatenate([q_t, extra], axis=0).T
             g_rows = jnp.concatenate([g_t, extra], axis=0).T
-            k_aug = jnp.concatenate([k_t, ones[(i % 2) * 2]], axis=0)
-            v_aug = jnp.concatenate([v_t, ones[(i % 2) * 2 + 1]], axis=0)
+            k_aug = jnp.concatenate([k_t, ones[i * 2]], axis=0)
+            v_aug = jnp.concatenate([v_t, ones[i * 2 + 1]], axis=0)
             scores = jnp.dot(q_rows, k_aug, preferred_element_type=F32)
             prob_grad = jnp.dot(g_rows, v_aug, preferred_element_type=F32)
             probs = jnp.exp2(scores * (scale * LOG2E) + bias_s[...])
@@ -153,7 +148,9 @@
         for xh in range(2):
             for yl in range(2):
                 j = (xh * 2 + yl) * 128
-                db_ref[owner[p] * 4 + yl * 2 + xh] = acc_s[j : j + 128, p * 128 : p * 128 + 128].astype(BF16)
+                piece = acc_s[j : j + 128, p * 128 : p * 128 + 128].astype(BF16)
+                for zl in range(2):
+                    db_ref[owner[p] * 8 + zl * 4 + xh * 2 + yl] = piece
 
 
 def fold_kernel(up_ref, up_more_ref, down_ref, down_more_ref, up_out_ref, down_out_ref):
@@ -164,29 +161,34 @@
         down_out_ref[s, 128:, :] = (down_ref[s, 128:, :].astype(F32) + down_more_ref[s].astype(F32)).astype(BF16)
 
 
-def join_kernel(own_ref, up_ref, down_ref, db_ref, out_ref):
+def join_kernel(zl_ref, own_ref, up_ref, down_ref, db_ref, out_ref):
     for s in range(4):
         total = own_ref[s].astype(F32) + up_ref[s].astype(F32) + down_ref[s].astype(F32)
         out_ref[s, :256, :] = total.astype(BF16)
     first_half = lax.broadcasted_iota(jnp.int32, (128, 128), 1) < 64
     for xl in range(2):
-        whole = db_ref[xl]
+        parts = [db_ref[z * 4 + xl * 2 + zl_ref[0]].astype(F32) for z in range(8)]
+        whole = ((parts[0] + parts[1]) + (parts[2] + parts[3])) + ((parts[4] + parts[5]) + (parts[6] + parts[7]))
         high = whole.astype(BF16).astype(F32)
         low = whole - high
         out_ref[xl * 2, 256:, :] = jnp.where(first_half, high, pltpu.roll(low, 64, 1)).astype(BF16)
         out_ref[xl * 2 + 1, 256:, :] = jnp.where(first_half, pltpu.roll(high, 64, 1), low).astype(BF16)
 
 
-def unpack_kernel(q_ref, kv_ref, dq_ref, dk_ref, dv_ref, db_ref):
-    for h in range(4):
-        parts = kv_ref[h, 256:, :].astype(F32)
-        db_ref[h] = (parts + pltpu.roll(parts, 64, 1)).T[:64]
+def unpack_query_kernel(q_ref, dq_ref):
     for i in range(4):
         heads = []
         for h in range(4):
             parts = [q_ref[h * 4 + a, i * 32 : i * 32 + 32, :].astype(F32) for a in range(4)]
             heads.append(parts[0] + parts[1] + parts[2] + parts[3])
         dq_ref[i] = jnp.concatenate(heads, axis=0).T.astype(BF16)
+
+
+def unpack_kernel(kv_ref, dk_ref, dv_ref, db_ref):
+    for h in range(4):
+        parts = kv_ref[h, 256:, :].astype(F32)
+        db_ref[h] = (parts + pltpu.roll(parts, 64, 1)).T[:64]
+    for i in range(4):
         for first, out in ((0, dk_ref), (128, dv_ref)):
             at = i * 32 + first
             out[i] = turned(jnp.concatenate([kv_ref[h, at : at + 32, :] for h in range(4)], axis=0))
@@ -198,10 +200,6 @@
 
 def params(mib=40):
     return pltpu.CompilerParams(vmem_limit_bytes=mib * 2**20)
-
-
-def swaps():
-    return [(z * 2 + yl, ((z // 2) * 2 + yl) * 2 + z % 2) for z in range(8) for yl in range(2)]
 
 
 def along(value, steps):
@@ -224,7 +222,7 @@
     )(keys, values)
     to_query = pl.pallas_call(
         functools.partial(pack_query_kernel, scale),
-        out_shape=shape(16, 416, 128),
+        out_shape=shape(16, 400, 128),
         in_specs=[pl.BlockSpec(memory_space=pltpu.SMEM)] + [hbm] * 5,
         out_specs=vmem()[0],
         scratch_shapes=[pltpu.VMEM((4, 128, 128), BF16)] * 3
@@ -240,7 +238,7 @@
         out_shape=(shape(16, 128, 128),)
         + (shape(4, 256, 128),) * 2
         + (shape(4, 128, 128),) * 2
-        + (shape(4, 256, 128), shape(16, 128, 128)),
+        + (shape(4, 256, 128), shape(32, 128, 128)),
         in_specs=[pl.BlockSpec(memory_space=pltpu.SMEM)] + vmem(2),
         out_specs=tuple(vmem(7)),
         scratch_shapes=[pltpu.VMEM((512, 512), F32), pltpu.VMEM((512, 512), F32)],
@@ -256,30 +254,36 @@
         compiler_params=params(),
         name="fold",
     )(up, up_more, down, down_more)
-    db = lax.all_to_all(db_parts, ("z", "xh"), 0, 0)
+    db = lax.all_to_all(db_parts, ("z", "xh", "yl"), 0, 0)
     up, down, db, dq_parts = lax.optimization_barrier((up, down, db, dq_parts))
     up, down = along(up, 1), along(down, -1)
-    db = jnp.sum(db.reshape(8, 2, 128, 128).astype(F32), axis=0)
-    db = lax.ppermute(db, ("z", "yl"), swaps())
     dq = lax.all_to_all(dq_parts, QUERY_GROUP, 0, 0)
     up, down, db, dq = lax.optimization_barrier((up, down, db, dq))
     joined = pl.pallas_call(
         join_kernel,
         out_shape=shape(4, 384, 128),
-        in_specs=vmem(4),
+        in_specs=[pl.BlockSpec(memory_space=pltpu.SMEM)] + vmem(4),
         out_specs=vmem()[0],
         compiler_params=params(),
         name="join",
-    )(own, up, down, db)
+    )(lax.rem(lax.axis_index("z"), 2).astype(jnp.int32).reshape(1), own, up, down, db)
     joined = lax.all_to_all(joined, ("xl", "c"), 0, 0)
-    query_grad, key_grad, value_grad, bias_grad = pl.pallas_call(
+    query_grad = pl.pallas_call(
+        unpack_query_kernel,
+        out_shape=shape(4, 128, 128),
+        in_specs=vmem(1),
+        out_specs=vmem()[0],
+        compiler_params=params(),
+        name="unpack_query",
+    )(dq)
+    key_grad, value_grad, bias_grad = pl.pallas_call(
         unpack_kernel,
-        out_shape=(shape(4, 128, 128),) * 3 + (jax.ShapeDtypeStruct((4, 64, 128), F32),),
-        in_specs=vmem(2),
-        out_specs=tuple(vmem(4)),
+        out_shape=(shape(4, 128, 128),) * 2 + (jax.ShapeDtypeStruct((4, 64, 128), F32),),
+        in_specs=vmem(1),
+        out_specs=tuple(vmem(3)),
         compiler_params=params(),
         name="unpack",
-    )(dq, joined)
+    )(joined)
     return query_grad, key_grad, value_grad, bias_grad.transpose(0, 2, 1)
 
 

time: 147 us -> 160 us (1.088); the launches traced: 144 us -> 160 us
  waiting for transfers between devices: 67.9 us -> 82.2 us
  blocking collectives: 10.2 us -> 0 us
  starting transfers between devices: 46.8 us -> 55.3 us
  local copies, waits for them, and re-layouts: 1.31 us -> 3.05 us
    all_to_all x1 -> x0, blocking collectives: 10.2 us -> none  [body(): joined = lax.all_to_all(joined, ('xl', 'c'), 0, 0)]
    all_to_all x1 -> x2, waiting for transfers between devices: 7.15 us -> 14.9 us  [the longest x1 9.08 us: body(): db = lax.all_to_all(db_parts, ('z', 'xh', 'yl'), 0, 0)]
    ppermute x4, waiting for transfers between devices: 12.9 us -> 20.2 us  [along(): return lax.ppermute(value, 'yh', [(n, (n + steps) % 4) for n in range(4)])]
    all_to_all x1 -> x2, starting transfers between devices: 10.6 us -> 17.1 us  [the longest x1 12.2 us: body(): db = lax.all_to_all(db_parts, ('z', 'xh', 'yl'), 0, 0)]
    all_to_all x1, starting transfers between devices: 5.83 us -> 8.41 us  [body(): dq = lax.all_to_all(dq_parts, QUERY_GROUP, 0, 0)]
    unnamed x4 -> x14, local copies, waits for them, and re-layouts: 1.31 us -> 3.05 us
where the time goes in v5:
time: 160 us
  waiting for transfers between devices  82.2 us (51%)
  starting transfers between devices  55.3 us (35%)
  Pallas kernels  18.4 us (11%)
  local copies, waits for them, and re-layouts  3.05 us (2%)
    all_to_all x1, waiting for transfers between devices, body(): got_key = lax.all_to_all(to_key, KEY_GROUP, 0, 0)  25.2 us
    all_to_all x1, waiting for transfers between devices, body(): got_query = lax.all_to_all(to_query, QUERY_GROUP, 0, 0)  22 us
    ppermute x4, waiting for transfers between devices, along(): return lax.ppermute(value, 'yh', [(n, (n + steps) % 4) for n in range(4)])  20.2 us
    ppermute x4, starting transfers between devices, along(): return lax.ppermute(value, 'yh', [(n, (n + steps) % 4) for n in range(4)])  14.8 us
    all_to_all x1, starting transfers between devices, body(): db = lax.all_to_all(db_parts, ('z', 'xh', 'yl'), 0, 0)  12.2 us
    pallas_call x1, Pallas kernels, body(): pl.pallas_call(functools.partial(attend_kernel, scale), out_shape=(shape(...  10.9 us
    all_to_all x1, starting transfers between devices, body(): got_key = lax.all_to_all(to_key, KEY_GROUP, 0, 0)  10.4 us
    all_to_all x1, waiting for transfers between devices, body(): db = lax.all_to_all(db_parts, ('z', 'xh', 'yl'), 0, 0)  9.08 us
  transfers between devices with their start and end apart: 9, of which 6 were waited for; matrix products, arithmetic and copies ran while one was open for 0% of the time, Pallas kernels for 2%

profile of v5, /device:TPU:1, one launch (start us, length us, event | category | flops | bytes accessed | tf_op | source)
XLA Modules:
  0.0 159.7 jit_solution(3017072570003829979)
XLA Ops:
  0.6 2.1 %pack_key.1 = bf16[16,256,128]{2,1,0:T(8,128)(2,1)} custom-call(bf16[4,128,128]{2,1,0:T(8,128)(2,1)} %k_hbm.1, bf16[4,128,128]{2,1,0:T(8,128)(2,1)} %v_hbm.1), custom_call_target="tpu_custom_call" | custom-call | tf_op jit(solution)/shard_map/pack_key/pallas_call | solution.py:214
  2.7 10.4 %all-to-all-start.1 = ((bf16[16,256,128]{2,1,0:T(8,128)(2,1)}), bf16[16,256,128]{2,1,0:T(8,128)(2,1)S(1)}, u32[]{:S(2)}, u32[]{:S(2)}) async-start(bf16[16,256,128]{2,1,0:T(8,128)(2,1)} %pack_key.1), calls=%async_computation.1 | async-start | bytes 2097152 | tf_op jit(solution)/shard_map/all_to_all | solution.py:233
  13.1 2.6 %pack_query.1 = bf16[16,400,128]{2,1,0:T(8,128)(2,1)} custom-call(s32[1]{0:T(128)} %bitcast.1.which_ref, bf16[4,128,128]{2,1,0:T(8,128)(2,1)} %q_hbm.1, bf16[4,128,128]{2,1,0:T(8,128)(2,1)} %g_hbm.1, bf16[4,128,128]{2,1,0:T(8,128)(2,1)} %o_hbm.1, f32[4,4,128]{2,1,0:T(4,128)} %l_hbm.1, bf16[4,128,2048]{2,1,0:T(8,128)(2,1)} %bias_hbm.1), custom_call_target="tpu_custom_call" | custom-call | tf_op jit(solution)/shard_map/pack_query/pallas_call | solution.py:223
  15.7 25.2 %all-to-all-done.1.kv_ref = bf16[16,256,128]{2,1,0:T(8,128)(2,1)S(1)} async-done(((bf16[16,256,128]{2,1,0:T(8,128)(2,1)}), bf16[16,256,128]{2,1,0:T(8,128)(2,1)S(1)}, u32[]{:S(2)}, u32[]{:S(2)}) %all-to-all-start.1) | async-done | bytes 1048608 | tf_op jit(solution)/shard_map/all_to_all | solution.py:233
  40.9 4.6 %all-to-all-start = ((bf16[16,400,128]{2,1,0:T(8,128)(2,1)}), bf16[16,400,128]{2,1,0:T(8,128)(2,1)S(1)}, u32[]{:S(2)}, u32[]{:S(2)}) async-start(bf16[16,400,128]{2,1,0:T(8,128)(2,1)} %pack_query.1), calls=%async_computation | async-start | bytes 3276800 | tf_op jit(solution)/shard_map/all_to_all | solution.py:234
  45.5 22.0 %all-to-all-done.jq_ref = bf16[16,400,128]{2,1,0:T(8,128)(2,1)S(1)} async-done(((bf16[16,400,128]{2,1,0:T(8,128)(2,1)}), bf16[16,400,128]{2,1,0:T(8,128)(2,1)S(1)}, u32[]{:S(2)}, u32[]{:S(2)}) %all-to-all-start) | async-done | bytes 1638432 | tf_op jit(solution)/shard_map/all_to_all | solution.py:234
  67.5 10.9 %attend.1 = (bf16[16,128,128]{2,1,0:T(8,128)(2,1)}, bf16[4,256,128]{2,1,0:T(8,128)(2,1)S(1)}, bf16[4,256,128]{2,1,0:T(8,128)(2,1)S(1)}, bf16[4,128,128]{2,1,0:T(...) custom-call(s32[1]{0:T(128)} %bitcast.yh_ref, ...), custom_call_target="tpu_custom_call" | custom-call | tf_op jit(solution)/shard_map/attend/pallas_call | solution.py:236
  78.3 1.0 copy-done
  79.3 0.7 copy-done.1
  80.0 0.7 copy-done.3
  80.7 0.7 copy-done.5
  81.4 12.2 %all-to-all-start.2 = ((bf16[32,128,128]{2,1,0:T(8,128)(2,1)}), bf16[32,128,128]{2,1,0:T(8,128)(2,1)S(1)}, u32[]{:S(2)}, u32[]{:S(2)}) async-start(bf16[32,128,128]{2,1,0:T(8,128)(2,1)} %copy-done), calls=%async_computation.2 | async-start | bytes 2097152 | tf_op jit(solution)/shard_map/all_to_all | solution.py:257
  93.6 0.0 copy-done.6
  93.6 2.6 %collective-permute-start = (bf16[4,128,128]{2,1,0:T(8,128)(2,1)S(1)}, bf16[4,128,128]{2,1,0:T(8,128)(2,1)S(1)}, u32[]{:S(2)}, u32[]{:S(2)}) collective-permute-start(bf16[4,128,128]{2,1,0:T(8,128)(2,1)S(1)} %copy-done.6), channel_id=1, source_target_pairs={{0,2},{2,4},{4,6},{6,0},{1,3},{3,5},{5,7},{7,1},{8,10},{10,12},{12... | collective-permute-start | bytes 393224 | tf_op jit(solution)/shard_map/ppermute | solution.py:206
  96.2 4.8 %collective-permute-start.1 = (bf16[4,128,128]{2,1,0:T(8,128)(2,1)S(1)}, bf16[4,128,128]{2,1,0:T(8,128)(2,1)S(1)}, u32[]{:S(2)}, u32[]{:S(2)}) collective-permute-start(bf16[4,128,128]{2,1,0:T(8,128)(2,1)S(1)} %get-tuple-element.27), channel_id=1, source_target_pairs={{0,6},{2,0},{4,2},{6,4},{1,7},{3,1},{5,3},{7,5},{8,14},{10,8},{12,... | collective-permute-start | bytes 393224 | tf_op jit(solution)/shard_map/ppermute | solution.py:206
  101.0 9.5 %collective-permute-done.up_more_ref = bf16[4,128,128]{2,1,0:T(8,128)(2,1)S(1)} collective-permute-done((bf16[4,128,128]{2,1,0:T(8,128)(2,1)S(1)}, bf16[4,128,128]{2,1,0:T(8,128)(2,1)S(1)}, u32[]{:S(2)}, u32[]{:S(2)}) %collective-permute-start) | collective-permute-done | bytes 131104 | tf_op jit(solution)/shard_map/ppermute | solution.py:206
  110.5 0.0 collective-permute-done.1.down_more_ref
  110.5 0.0 copy-done.2
  110.5 0.0 copy-done.4
  110.5 0.1 fold.1
  110.6 9.1 %all-to-all-done.2.db_ref = bf16[32,128,128]{2,1,0:T(8,128)(2,1)S(1)} async-done(((bf16[32,128,128]{2,1,0:T(8,128)(2,1)}), bf16[32,128,128]{2,1,0:T(8,128)(2,1)S(1)}, u32[]{:S(2)}, u32[]{:S(2)}) %all-to-all-start.2) | async-done | bytes 1048608 | tf_op jit(solution)/shard_map/all_to_all | solution.py:257
  119.7 8.4 %all-to-all-start.3 = ((bf16[16,128,128]{2,1,0:T(8,128)(2,1)}), bf16[16,128,128]{2,1,0:T(8,128)(2,1)S(1)}, u32[]{:S(2)}, u32[]{:S(2)}) async-start(bf16[16,128,128]{2,1,0:T(8,128)(2,1)} %get-tuple-element.35), calls=%async_computation.3 | async-start | bytes 1048576 | tf_op jit(solution)/shard_map/all_to_all | solution.py:260
  128.1 2.6 %collective-permute-start.2 = (bf16[4,256,128]{2,1,0:T(8,128)(2,1)S(1)}, bf16[4,256,128]{2,1,0:T(8,128)(2,1)S(1)}, u32[]{:S(2)}, u32[]{:S(2)}) collective-permute-start(bf16[4,256,128]{2,1,0:T(8,128)(2,1)S(1)} %get-tuple-element.32), channel_id=1, source_target_pairs={{0,2},{2,4},{4,6},{6,0},{1,3},{3,5},{5,7},{7,1},{8,10},{10,12},{12... | collective-permute-start | bytes 786440 | tf_op jit(solution)/shard_map/ppermute | solution.py:206
  130.7 4.8 %collective-permute-start.3 = (bf16[4,256,128]{2,1,0:T(8,128)(2,1)S(1)}, bf16[4,256,128]{2,1,0:T(8,128)(2,1)S(1)}, u32[]{:S(2)}, u32[]{:S(2)}) collective-permute-start(bf16[4,256,128]{2,1,0:T(8,128)(2,1)S(1)} %get-tuple-element.33), channel_id=1, source_target_pairs={{0,6},{2,0},{4,2},{6,4},{1,7},{3,1},{5,3},{7,5},{8,14},{10,8},{12,... | collective-permute-start | bytes 786440 | tf_op jit(solution)/shard_map/ppermute | solution.py:206
  135.5 10.7 %collective-permute-done.2.up_ref = bf16[4,256,128]{2,1,0:T(8,128)(2,1)S(1)} collective-permute-done((bf16[4,256,128]{2,1,0:T(8,128)(2,1)S(1)}, bf16[4,256,128]{2,1,0:T(8,128)(2,1)S(1)}, u32[]{:S(2)}, u32[]{:S(2)}) %collective-permute-start.2) | collective-permute-done | bytes 262176 | tf_op jit(solution)/shard_map/ppermute | solution.py:206
  146.2 0.0 collective-permute-done.3.down_ref
  146.2 0.0 all-to-all-done.3.q_ref
  146.2 1.0 join.1
  147.1 4.9 %all-to-all-start.4 = ((bf16[4,384,128]{2,1,0:T(8,128)(2,1)}), bf16[4,384,128]{2,1,0:T(8,128)(2,1)S(1)}, u32[]{:S(2)}, u32[]{:S(2)}) async-start(bf16[4,384,128]{2,1,0:T(8,128)(2,1)} %join.1), calls=%async_computation.4 | async-start | bytes 786432 | tf_op jit(solution)/shard_map/all_to_all | solution.py:270
  152.1 0.8 unpack_query.1
  152.9 5.8 %all-to-all-done.4.kv_ref = bf16[4,384,128]{2,1,0:T(8,128)(2,1)S(1)} async-done(((bf16[4,384,128]{2,1,0:T(8,128)(2,1)}), bf16[4,384,128]{2,1,0:T(8,128)(2,1)S(1)}, u32[]{:S(2)}, u32[]{:S(2)}) %all-to-all-start.4) | async-done | bytes 393248 | tf_op jit(solution)/shard_map/all_to_all | solution.py:270
  158.6 1.0 unpack.1
  (7 shorter events, 0.0 us)
Async XLA Ops:
  2.7 38.2 %all-to-all-start.1 = ((bf16[16,256,128]{2,1,0:T(8,128)(2,1)}), bf16[16,256,128]{2,1,0:T(8,128)(2,1)S(1)}, u32[]{:S(2)}, u32[]{:S(2)}) async-start(bf16[16,256,128]{2,1,0:T(8,128)(2,1)} %pack_key.1), calls=%async_computation.1 | async-start | bytes 2097152 | tf_op jit(solution)/shard_map/all_to_all | solution.py:233
  40.9 26.5 %all-to-all-start = ((bf16[16,400,128]{2,1,0:T(8,128)(2,1)}), bf16[16,400,128]{2,1,0:T(8,128)(2,1)S(1)}, u32[]{:S(2)}, u32[]{:S(2)}) async-start(bf16[16,400,128]{2,1,0:T(8,128)(2,1)} %pack_query.1), calls=%async_computation | async-start | bytes 3276800 | tf_op jit(solution)/shard_map/all_to_all | solution.py:234
  78.3 1.0 copy-start
  79.3 0.7 copy-start.1
  80.0 0.7 copy-start.3
  80.7 0.7 copy-start.5
  81.4 12.2 %copy-start.6 = (bf16[4,128,128]{2,1,0:T(8,128)(2,1)S(1)}, bf16[4,128,128]{2,1,0:T(8,128)(2,1)}, u32[]{:S(2)}) copy-start(bf16[4,128,128]{2,1,0:T(8,128)(2,1)} %copy-done.5) | copy-start | bytes 393220
  81.4 29.1 %copy-start.2 = (bf16[4,256,128]{2,1,0:T(8,128)(2,1)S(1)}, bf16[4,256,128]{2,1,0:T(8,128)(2,1)}, u32[]{:S(2)}) copy-start(bf16[4,256,128]{2,1,0:T(8,128)(2,1)} %copy-done.1) | copy-start | bytes 786436
  81.4 29.1 %copy-start.4 = (bf16[4,256,128]{2,1,0:T(8,128)(2,1)S(1)}, bf16[4,256,128]{2,1,0:T(8,128)(2,1)}, u32[]{:S(2)}) copy-start(bf16[4,256,128]{2,1,0:T(8,128)(2,1)} %copy-done.3) | copy-start | bytes 786436
  81.4 38.3 %all-to-all-start.2 = ((bf16[32,128,128]{2,1,0:T(8,128)(2,1)}), bf16[32,128,128]{2,1,0:T(8,128)(2,1)S(1)}, u32[]{:S(2)}, u32[]{:S(2)}) async-start(bf16[32,128,128]{2,1,0:T(8,128)(2,1)} %copy-done), calls=%async_computation.2 | async-start | bytes 2097152 | tf_op jit(solution)/shard_map/all_to_all | solution.py:257
  93.6 16.9 %collective-permute-start = (bf16[4,128,128]{2,1,0:T(8,128)(2,1)S(1)}, bf16[4,128,128]{2,1,0:T(8,128)(2,1)S(1)}, u32[]{:S(2)}, u32[]{:S(2)}) collective-permute-start(bf16[4,128,128]{2,1,0:T(8,128)(2,1)S(1)} %copy-done.6), channel_id=1, source_target_pairs={{0,2},{2,4},{4,6},{6,0},{1,3},{3,5},{5,7},{7,1},{8,10},{10,12},{12... | collective-permute-start | bytes 393224 | tf_op jit(solution)/shard_map/ppermute | solution.py:206
  96.2 14.3 %collective-permute-start.1 = (bf16[4,128,128]{2,1,0:T(8,128)(2,1)S(1)}, bf16[4,128,128]{2,1,0:T(8,128)(2,1)S(1)}, u32[]{:S(2)}, u32[]{:S(2)}) collective-permute-start(bf16[4,128,128]{2,1,0:T(8,128)(2,1)S(1)} %get-tuple-element.27), channel_id=1, source_target_pairs={{0,6},{2,0},{4,2},{6,4},{1,7},{3,1},{5,3},{7,5},{8,14},{10,8},{12,... | collective-permute-start | bytes 393224 | tf_op jit(solution)/shard_map/ppermute | solution.py:206
  119.7 26.5 %all-to-all-start.3 = ((bf16[16,128,128]{2,1,0:T(8,128)(2,1)}), bf16[16,128,128]{2,1,0:T(8,128)(2,1)S(1)}, u32[]{:S(2)}, u32[]{:S(2)}) async-start(bf16[16,128,128]{2,1,0:T(8,128)(2,1)} %get-tuple-element.35), calls=%async_computation.3 | async-start | bytes 1048576 | tf_op jit(solution)/shard_map/all_to_all | solution.py:260
  128.1 18.1 %collective-permute-start.2 = (bf16[4,256,128]{2,1,0:T(8,128)(2,1)S(1)}, bf16[4,256,128]{2,1,0:T(8,128)(2,1)S(1)}, u32[]{:S(2)}, u32[]{:S(2)}) collective-permute-start(bf16[4,256,128]{2,1,0:T(8,128)(2,1)S(1)} %get-tuple-element.32), channel_id=1, source_target_pairs={{0,2},{2,4},{4,6},{6,0},{1,3},{3,5},{5,7},{7,1},{8,10},{10,12},{12... | collective-permute-start | bytes 786440 | tf_op jit(solution)/shard_map/ppermute | solution.py:206
  130.7 15.5 %collective-permute-start.3 = (bf16[4,256,128]{2,1,0:T(8,128)(2,1)S(1)}, bf16[4,256,128]{2,1,0:T(8,128)(2,1)S(1)}, u32[]{:S(2)}, u32[]{:S(2)}) collective-permute-start(bf16[4,256,128]{2,1,0:T(8,128)(2,1)S(1)} %get-tuple-element.33), channel_id=1, source_target_pairs={{0,6},{2,0},{4,2},{6,4},{1,7},{3,1},{5,3},{7,5},{8,14},{10,8},{12,... | collective-permute-start | bytes 786440 | tf_op jit(solution)/shard_map/ppermute | solution.py:206
  147.1 11.5 %all-to-all-start.4 = ((bf16[4,384,128]{2,1,0:T(8,128)(2,1)}), bf16[4,384,128]{2,1,0:T(8,128)(2,1)S(1)}, u32[]{:S(2)}, u32[]{:S(2)}) async-start(bf16[4,384,128]{2,1,0:T(8,128)(2,1)} %join.1), calls=%async_computation.4 | async-start | bytes 786432 | tf_op jit(solution)/shard_map/all_to_all | solution.py:270

commit v6 on v5

--- a/solution.py
+++ b/solution.py
@@ -11,7 +11,6 @@
 ROW = ("xl", "z", "c")
 BLK = ("xh", "yh", "yl")
 QUERY_GROUP = ("xl", "c", "xh", "yl")
-KEY_GROUP = ("xl", "c", "yh")
 LOG2E = 1.4426950408889634
 AUG = 16
 F32, BF16 = jnp.float32, jnp.bfloat16
@@ -41,9 +40,8 @@
         k_t, v_t = turned(k_ref[i]), turned(v_ref[i])
         for h in range(4):
             part = slice(h * 32, h * 32 + 32)
-            for b in range(4):
-                to_key_ref[h * 4 + b, i * 64 : i * 64 + 32, :] = k_t[part]
-                to_key_ref[h * 4 + b, i * 64 + 32 : i * 64 + 64, :] = v_t[part]
+            to_key_ref[h, i * 32 : i * 32 + 32, :] = k_t[part]
+            to_key_ref[h, 128 + i * 32 : 160 + i * 32, :] = v_t[part]
 
 
 def pack_query_kernel(
@@ -91,7 +89,25 @@
                 ]
 
 
-def attend_kernel(scale, yh_ref, jq_ref, kv_ref, dq_ref, dkv0_ref, dkv1_ref, dk2_ref, dv2_ref, dkv3_ref, db_ref, bias_s, acc_s):
+def attend_kernel(
+    scale,
+    yh_ref,
+    jq_ref,
+    kv0_ref,
+    kv1_ref,
+    k2_ref,
+    v2_ref,
+    kv3_ref,
+    dq_ref,
+    dkv0_ref,
+    dkv1_ref,
+    dk2_ref,
+    dv2_ref,
+    dkv3_ref,
+    db_ref,
+    bias_s,
+    acc_s,
+):
     dkv_refs = (dkv0_ref, dkv1_ref, None, dkv3_ref)
     owner = [lax.rem(yh_ref[0] + p, 4) for p in range(4)]
     for a in range(4):
@@ -114,9 +130,12 @@
                 jnp.concatenate([jq_ref[base + a, start : start + size, :] for a in range(4)], axis=1)
                 for start, size in ((first, 32), (first + 32, 32), (256, 16))
             )
-            k_t, v_t = (
-                jnp.concatenate([kv_ref[base + owner[p], start : start + 32, :] for p in range(4)], axis=1)
-                for start in (first, first + 32)
+            low_at, high_at = slice(i * 32, i * 32 + 32), slice(128 + i * 32, 160 + i * 32)
+            k_t = jnp.concatenate(
+                [kv0_ref[s, low_at, :], kv1_ref[s, low_at, :], k2_ref[s, low_at, :], kv3_ref[s, low_at, :]], axis=1
+            )
+            v_t = jnp.concatenate(
+                [kv0_ref[s, high_at, :], kv1_ref[s, high_at, :], v2_ref[s, low_at, :], kv3_ref[s, high_at, :]], axis=1
             )
             q_rows = jnp.concatenate([q_t, extra], axis=0).T
             g_rows = jnp.concatenate([g_t, extra], axis=0).T
@@ -134,7 +153,6 @@
             for b in range(4):
                 block = slice(b * 128, b * 128 + 128)
                 dq_ref[base + b, i * 32 : i * 32 + 32, :] = dq[:, block]
-                low_at, high_at = slice(i * 32, i * 32 + 32), slice(128 + i * 32, 160 + i * 32)
                 if b == 2:
                     dk2_ref[s, low_at, :] = dk[:, block]
                     dv2_ref[s, low_at, :] = dv[:, block]
@@ -149,8 +167,7 @@
             for yl in range(2):
                 j = (xh * 2 + yl) * 128
                 piece = acc_s[j : j + 128, p * 128 : p * 128 + 128].astype(BF16)
-                for zl in range(2):
-                    db_ref[owner[p] * 8 + zl * 4 + xh * 2 + yl] = piece
+                db_ref[owner[p] * 4 + yl * 2 + xh] = piece
 
 
 def fold_kernel(up_ref, up_more_ref, down_ref, down_more_ref, up_out_ref, down_out_ref):
@@ -161,14 +178,13 @@
         down_out_ref[s, 128:, :] = (down_ref[s, 128:, :].astype(F32) + down_more_ref[s].astype(F32)).astype(BF16)
 
 
-def join_kernel(zl_ref, own_ref, up_ref, down_ref, db_ref, out_ref):
+def join_kernel(own_ref, up_ref, down_ref, db_ref, out_ref):
     for s in range(4):
         total = own_ref[s].astype(F32) + up_ref[s].astype(F32) + down_ref[s].astype(F32)
         out_ref[s, :256, :] = total.astype(BF16)
     first_half = lax.broadcasted_iota(jnp.int32, (128, 128), 1) < 64
     for xl in range(2):
-        parts = [db_ref[z * 4 + xl * 2 + zl_ref[0]].astype(F32) for z in range(8)]
-        whole = ((parts[0] + parts[1]) + (parts[2] + parts[3])) + ((parts[4] + parts[5]) + (parts[6] + parts[7]))
+        whole = db_ref[xl]
         high = whole.astype(BF16).astype(F32)
         low = whole - high
         out_ref[xl * 2, 256:, :] = jnp.where(first_half, high, pltpu.roll(low, 64, 1)).astype(BF16)
@@ -202,6 +218,10 @@
     return pltpu.CompilerParams(vmem_limit_bytes=mib * 2**20)
 
 
+def swaps():
+    return [(z * 2 + yl, ((z // 2) * 2 + yl) * 2 + z % 2) for z in range(8) for yl in range(2)]
+
+
 def along(value, steps):
     return lax.ppermute(value, "yh", [(n, (n + steps) % 4) for n in range(4)])
 
@@ -213,7 +233,7 @@
     hbm = pl.BlockSpec(memory_space=pltpu.HBM)
     to_key = pl.pallas_call(
         pack_key_kernel,
-        out_shape=shape(16, 256, 128),
+        out_shape=shape(4, 256, 128),
         in_specs=[hbm] * 2,
         out_specs=vmem()[0],
         scratch_shapes=[pltpu.VMEM((4, 128, 128), BF16)] * 2 + [pltpu.SemaphoreType.DMA((2,))],
@@ -230,7 +250,9 @@
         compiler_params=params(61),
         name="pack_query",
     )(which, queries, out_grad, outputs, logsumexp, bias)
-    got_key = lax.all_to_all(to_key, KEY_GROUP, 0, 0)
+    own = lax.all_to_all(to_key, ("xl", "c"), 0, 0)
+    after, before = along(own, -1), along(own, 1)
+    k_far, v_far = along(before[:, :128], 1), along(after[:, 128:], -1)
     got_query = lax.all_to_all(to_query, QUERY_GROUP, 0, 0)
     yh = lax.axis_index("yh").astype(jnp.int32).reshape(1)
     dq_parts, own, up, dk_far, dv_far, down, db_parts = pl.pallas_call(
@@ -238,13 +260,13 @@
         out_shape=(shape(16, 128, 128),)
         + (shape(4, 256, 128),) * 2
         + (shape(4, 128, 128),) * 2
-        + (shape(4, 256, 128), shape(32, 128, 128)),
-        in_specs=[pl.BlockSpec(memory_space=pltpu.SMEM)] + vmem(2),
+        + (shape(4, 256, 128), shape(16, 128, 128)),
+        in_specs=[pl.BlockSpec(memory_space=pltpu.SMEM)] + vmem(6),
         out_specs=tuple(vmem(7)),
         scratch_shapes=[pltpu.VMEM((512, 512), F32), pltpu.VMEM((512, 512), F32)],
         compiler_params=params(),
         name="attend",
-    )(yh, got_query, got_key)
+    )(yh, got_query, own, after, k_far, v_far, before)
     up_more, down_more = along(dk_far, 1), along(dv_far, -1)
     up, down = pl.pallas_call(
         fold_kernel,
@@ -254,19 +276,21 @@
         compiler_params=params(),
         name="fold",
     )(up, up_more, down, down_more)
-    db = lax.all_to_all(db_parts, ("z", "xh", "yl"), 0, 0)
+    db = lax.all_to_all(db_parts, ("z", "xh"), 0, 0)
     up, down, db, dq_parts = lax.optimization_barrier((up, down, db, dq_parts))
     up, down = along(up, 1), along(down, -1)
+    db = jnp.sum(db.reshape(8, 2, 128, 128).astype(F32), axis=0)
+    db = lax.ppermute(db, ("z", "yl"), swaps())
     dq = lax.all_to_all(dq_parts, QUERY_GROUP, 0, 0)
     up, down, db, dq = lax.optimization_barrier((up, down, db, dq))
     joined = pl.pallas_call(
         join_kernel,
         out_shape=shape(4, 384, 128),
-        in_specs=[pl.BlockSpec(memory_space=pltpu.SMEM)] + vmem(4),
+        in_specs=vmem(4),
         out_specs=vmem()[0],
         compiler_params=params(),
         name="join",
-    )(lax.rem(lax.axis_index("z"), 2).astype(jnp.int32).reshape(1), own, up, down, db)
+    )(own, up, down, db)
     joined = lax.all_to_all(joined, ("xl", "c"), 0, 0)
     query_grad = pl.pallas_call(
         unpack_query_kernel,

time: 160 us -> 148 us (0.925)
  waiting for transfers between devices: 82.2 us -> 58.3 us
  starting transfers between devices: 55.3 us -> 67.9 us
  local copies, waits for them, and re-layouts: 3.05 us -> 1.33 us
    all_to_all x2, waiting for transfers between devices: 34.3 us -> 6.13 us  [the longest x1 3.54 us: body(): db = lax.all_to_all(db_parts, ('z', 'xh'), 0, 0)]
    ppermute x4 -> x8, waiting for transfers between devices: 20.2 us -> 46.4 us  [along(): return lax.ppermute(value, 'yh', [(n, (n + steps) % 4) for n in range(4)])]
    all_to_all x1, waiting for transfers between devices: 22 us -> 0.01 us  [body(): got_query = lax.all_to_all(to_query, QUERY_GROUP, 0, 0)]
    ppermute x4 -> x8, starting transfers between devices: 14.8 us -> 30.2 us  [along(): return lax.ppermute(value, 'yh', [(n, (n + steps) % 4) for n in range(4)])]
    all_to_all x2, starting transfers between devices: 22.5 us -> 20.7 us  [the longest x1 10.5 us: body(): db = lax.all_to_all(db_parts, ('z', 'xh'), 0, 0)]
    unnamed x14 -> x4, local copies, waits for them, and re-layouts: 3.05 us -> 1.31 us
  transfers between devices with their start and end apart: 9 -> 14, of which waited for: 6 -> 9; matrix products, arithmetic and copies ran while one was open for 0% -> 0% of each run, Pallas kernels for 2% -> 2%
where the time goes in v6:
time: 148 us; the launch traced here: 147 us
  starting transfers between devices  67.9 us (46%)
  waiting for transfers between devices  58.3 us (39%)
  Pallas kernels  18.3 us (12%)
    ppermute x8, waiting for transfers between devices, along(): return lax.ppermute(value, 'yh', [(n, (n + steps) % 4) for n in range(4)])  46.4 us
    ppermute x8, starting transfers between devices, along(): return lax.ppermute(value, 'yh', [(n, (n + steps) % 4) for n in range(4)])  30.2 us
    pallas_call x1, Pallas kernels, body(): pl.pallas_call(functools.partial(attend_kernel, scale), out_shape=(shape(...  11.1 us
    all_to_all x1, starting transfers between devices, body(): db = lax.all_to_all(db_parts, ('z', 'xh'), 0, 0)  10.5 us
    all_to_all x1, starting transfers between devices, body(): own = lax.all_to_all(to_key, ('xl', 'c'), 0, 0)  10.3 us
    all_to_all x1, starting transfers between devices, body(): dq = lax.all_to_all(dq_parts, QUERY_GROUP, 0, 0)  7.73 us
    all_to_all x1, waiting for transfers between devices, body(): joined = lax.all_to_all(joined, ('xl', 'c'), 0, 0)  5.78 us
    all_to_all x1, starting transfers between devices, body(): got_query = lax.all_to_all(to_query, QUERY_GROUP, 0, 0)  4.39 us
  transfers between devices with their start and end apart: 14, of which 9 were waited for; matrix products, arithmetic and copies ran while one was open for 0% of the time, Pallas kernels for 2%

profile of v6, /device:TPU:1, one launch (start us, length us, event | category | flops | bytes accessed | tf_op | source)
XLA Modules:
  0.0 146.6 jit_solution(15179477631211249700)
XLA Ops:
  0.6 1.8 %pack_key.1 = bf16[4,256,128]{2,1,0:T(8,128)(2,1)} custom-call(bf16[4,128,128]{2,1,0:T(8,128)(2,1)} %k_hbm.1, bf16[4,128,128]{2,1,0:T(8,128)(2,1)} %v_hbm.1), custom_call_target="tpu_custom_call" | custom-call | tf_op jit(solution)/shard_map/pack_key/pallas_call | solution.py:234
  2.5 10.3 %all-to-all-start.1 = ((bf16[4,256,128]{2,1,0:T(8,128)(2,1)}), bf16[4,256,128]{2,1,0:T(8,128)(2,1)S(1)}, u32[]{:S(2)}, u32[]{:S(2)}) async-start(bf16[4,256,128]{2,1,0:T(8,128)(2,1)} %pack_key.1), calls=%async_computation.1 | async-start | bytes 524288 | tf_op jit(solution)/shard_map/all_to_all | solution.py:253
  12.7 2.6 %pack_query.1 = bf16[16,400,128]{2,1,0:T(8,128)(2,1)} custom-call(s32[1]{0:T(128)} %bitcast.1.which_ref, bf16[4,128,128]{2,1,0:T(8,128)(2,1)} %q_hbm.1, bf16[4,128,128]{2,1,0:T(8,128)(2,1)} %g_hbm.1, bf16[4,128,128]{2,1,0:T(8,128)(2,1)} %o_hbm.1, f32[4,4,128]{2,1,0:T(4,128)} %l_hbm.1, bf16[4,128,2048]{2,1,0:T(8,128)(2,1)} %bias_hbm.1), custom_call_target="tpu_custom_call" | custom-call | tf_op jit(solution)/shard_map/pack_query/pallas_call | solution.py:243
  15.3 2.6 %all-to-all-done.1.kv0_ref = bf16[4,256,128]{2,1,0:T(8,128)(2,1)S(1)} async-done(((bf16[4,256,128]{2,1,0:T(8,128)(2,1)}), bf16[4,256,128]{2,1,0:T(8,128)(2,1)S(1)}, u32[]{:S(2)}, u32[]{:S(2)}) %all-to-all-start.1) | async-done | bytes 262176 | tf_op jit(solution)/shard_map/all_to_all | solution.py:253
  17.9 4.4 %all-to-all-start = ((bf16[16,400,128]{2,1,0:T(8,128)(2,1)}), bf16[16,400,128]{2,1,0:T(8,128)(2,1)S(1)}, u32[]{:S(2)}, u32[]{:S(2)}) async-start(bf16[16,400,128]{2,1,0:T(8,128)(2,1)} %pack_query.1), calls=%async_computation | async-start | bytes 3276800 | tf_op jit(solution)/shard_map/all_to_all | solution.py:256
  22.3 1.9 %collective-permute-start.1 = (bf16[4,256,128]{2,1,0:T(8,128)(2,1)S(1)}, bf16[4,256,128]{2,1,0:T(8,128)(2,1)S(1)}, u32[]{:S(2)}, u32[]{:S(2)}) collective-permute-start(bf16[4,256,128]{2,1,0:T(8,128)(2,1)S(1)} %all-to-all-done.1.kv0_ref), channel_id=1, source_target_pairs={{0,2},{2,4},{4,6},{6,0},{1,3},{3,5},{5,7},{7,1},{8,10},{10,12},{12... | collective-permute-start | bytes 786440 | tf_op jit(solution)/shard_map/ppermute | solution.py:226
  24.2 5.5 %collective-permute-start = (bf16[4,256,128]{2,1,0:T(8,128)(2,1)S(1)}, bf16[4,256,128]{2,1,0:T(8,128)(2,1)S(1)}, u32[]{:S(2)}, u32[]{:S(2)}) collective-permute-start(bf16[4,256,128]{2,1,0:T(8,128)(2,1)S(1)} %all-to-all-done.1.kv0_ref), channel_id=1, source_target_pairs={{0,6},{2,0},{4,2},{6,4},{1,7},{3,1},{5,3},{7,5},{8,14},{10,8},{12,... | collective-permute-start | bytes 786440 | tf_op jit(solution)/shard_map/ppermute | solution.py:226
  29.7 25.0 %collective-permute-done.1.kv3_ref = bf16[4,256,128]{2,1,0:T(8,128)(2,1)S(1)} collective-permute-done((bf16[4,256,128]{2,1,0:T(8,128)(2,1)S(1)}, bf16[4,256,128]{2,1,0:T(8,128)(2,1)S(1)}, u32[]{:S(2)}, u32[]{:S(2)}) %collective-permute-start.1) | collective-permute-done | bytes 262176 | tf_op jit(solution)/shard_map/ppermute | solution.py:226
  54.7 4.7 %collective-permute-start.2 = (bf16[4,128,128]{2,1,0:T(8,128)(2,1)S(1)}, bf16[4,128,128]{2,1,0:T(8,128)(2,1)S(1)}, u32[]{:S(2)}, u32[]{:S(2)}) collective-permute-start(bf16[4,128,128]{2,1,0:T(8,128)(2,1)S(1)} %slice.8), channel_id=1, source_target_pairs={{0,2},{2,4},{4,6},{6,0},{1,3},{3,5},{5,7},{7,1},{8,10},{10,12},{12... | collective-permute-start | bytes 393224 | tf_op jit(solution)/shard_map/ppermute | solution.py:226
  59.4 2.7 %collective-permute-start.3 = (bf16[4,128,128]{2,1,0:T(8,128)(2,1)S(1)}, bf16[4,128,128]{2,1,0:T(8,128)(2,1)S(1)}, u32[]{:S(2)}, u32[]{:S(2)}) collective-permute-start(bf16[4,128,128]{2,1,0:T(8,128)(2,1)S(1)} %slice.9), channel_id=1, source_target_pairs={{0,6},{2,0},{4,2},{6,4},{1,7},{3,1},{5,3},{7,5},{8,14},{10,8},{12,... | collective-permute-start | bytes 393224 | tf_op jit(solution)/shard_map/ppermute | solution.py:226
  62.1 1.0 collective-permute-done.2.k2_ref
  63.1 2.9 %collective-permute-done.3.v2_ref = bf16[4,128,128]{2,1,0:T(8,128)(2,1)S(1)} collective-permute-done((bf16[4,128,128]{2,1,0:T(8,128)(2,1)S(1)}, bf16[4,128,128]{2,1,0:T(8,128)(2,1)S(1)}, u32[]{:S(2)}, u32[]{:S(2)}) %collective-permute-start.3) | collective-permute-done | bytes 131104 | tf_op jit(solution)/shard_map/ppermute | solution.py:226
  66.0 11.1 %attend.1 = (bf16[16,128,128]{2,1,0:T(8,128)(2,1)}, bf16[4,256,128]{2,1,0:T(8,128)(2,1)S(1)}, bf16[4,256,128]{2,1,0:T(8,128)(2,1)S(1)}, bf16[4,128,128]{2,1,0:T(...) custom-call(s32[1]{0:T(128)} %bitcast.yh_ref, ...), custom_call_target="tpu_custom_call" | custom-call | tf_op jit(solution)/shard_map/attend/pallas_call | solution.py:258
  77.1 0.7 copy-done
  77.7 0.7 copy-done.1
  78.4 10.5 %all-to-all-start.2 = ((bf16[16,128,128]{2,1,0:T(8,128)(2,1)}), bf16[16,128,128]{2,1,0:T(8,128)(2,1)S(1)}, u32[]{:S(2)}, u32[]{:S(2)}) async-start(bf16[16,128,128]{2,1,0:T(8,128)(2,1)} %get-tuple-element.30), calls=%async_computation.2 | async-start | bytes 1048576 | tf_op jit(solution)/shard_map/all_to_all | solution.py:279
  88.9 5.1 %collective-permute-start.4 = (bf16[4,128,128]{2,1,0:T(8,128)(2,1)}, bf16[4,128,128]{2,1,0:T(8,128)(2,1)S(1)}, u32[]{:S(2)}, u32[]{:S(2)}) collective-permute-start(bf16[4,128,128]{2,1,0:T(8,128)(2,1)} %copy-done.1), channel_id=1, source_target_pairs={{0,2},{2,4},{4,6},{6,0},{1,3},{3,5},{5,7},{7,1},{8,10},{10,12},{12... | collective-permute-start | bytes 393224 | tf_op jit(solution)/shard_map/ppermute | solution.py:226
  94.0 2.7 %collective-permute-start.5 = (bf16[4,128,128]{2,1,0:T(8,128)(2,1)}, bf16[4,128,128]{2,1,0:T(8,128)(2,1)S(1)}, u32[]{:S(2)}, u32[]{:S(2)}) collective-permute-start(bf16[4,128,128]{2,1,0:T(8,128)(2,1)} %copy-done), channel_id=1, source_target_pairs={{0,6},{2,0},{4,2},{6,4},{1,7},{3,1},{5,3},{7,5},{8,14},{10,8},{12,... | collective-permute-start | bytes 393224 | tf_op jit(solution)/shard_map/ppermute | solution.py:226
  96.7 0.9 collective-permute-done.4.up_more_ref
  97.6 3.2 %collective-permute-done.5.down_more_ref = bf16[4,128,128]{2,1,0:T(8,128)(2,1)S(1)} collective-permute-done((bf16[4,128,128]{2,1,0:T(8,128)(2,1)}, bf16[4,128,128]{2,1,0:T(8,128)(2,1)S(1)}, u32[]{:S(2)}, u32[]{:S(2)}) %collective-permute-start.5) | collective-permute-done | bytes 131104 | tf_op jit(solution)/shard_map/ppermute | solution.py:226
  100.9 3.5 %all-to-all-done.2 = bf16[16,128,128]{2,1,0:T(8,128)(2,1)S(1)} async-done(((bf16[16,128,128]{2,1,0:T(8,128)(2,1)}), bf16[16,128,128]{2,1,0:T(8,128)(2,1)S(1)}, u32[]{:S(2)}, u32[]{:S(2)}) %all-to-all-start.2) | async-done | bytes 524320 | tf_op jit(solution)/shard_map/all_to_all | solution.py:279
  104.5 7.7 %all-to-all-start.3 = ((bf16[16,128,128]{2,1,0:T(8,128)(2,1)}), bf16[16,128,128]{2,1,0:T(8,128)(2,1)S(1)}, u32[]{:S(2)}, u32[]{:S(2)}) async-start(bf16[16,128,128]{2,1,0:T(8,128)(2,1)} %get-tuple-element.35), calls=%async_computation.3 | async-start | bytes 1048576 | tf_op jit(solution)/shard_map/all_to_all | solution.py:284
  112.2 4.9 %collective-permute-start.6 = (bf16[4,256,128]{2,1,0:T(8,128)(2,1)S(1)}, bf16[4,256,128]{2,1,0:T(8,128)(2,1)S(1)}, u32[]{:S(2)}, u32[]{:S(2)}) collective-permute-start(bf16[4,256,128]{2,1,0:T(8,128)(2,1)S(1)} %get-tuple-element.32), channel_id=1, source_target_pairs={{0,2},{2,4},{4,6},{6,0},{1,3},{3,5},{5,7},{7,1},{8,10},{10,12},{12... | collective-permute-start | bytes 786440 | tf_op jit(solution)/shard_map/ppermute | solution.py:226
  117.1 2.7 %collective-permute-start.7 = (bf16[4,256,128]{2,1,0:T(8,128)(2,1)S(1)}, bf16[4,256,128]{2,1,0:T(8,128)(2,1)S(1)}, u32[]{:S(2)}, u32[]{:S(2)}) collective-permute-start(bf16[4,256,128]{2,1,0:T(8,128)(2,1)S(1)} %get-tuple-element.33), channel_id=1, source_target_pairs={{0,6},{2,0},{4,2},{6,4},{1,7},{3,1},{5,3},{7,5},{8,14},{10,8},{12,... | collective-permute-start | bytes 786440 | tf_op jit(solution)/shard_map/ppermute | solution.py:226
  119.8 0.1 convert_reduce_fusion
  119.9 0.7 collective-permute-start.8
  120.6 13.4 %collective-permute-done.6.up_ref = bf16[4,256,128]{2,1,0:T(8,128)(2,1)S(1)} collective-permute-done((bf16[4,256,128]{2,1,0:T(8,128)(2,1)S(1)}, bf16[4,256,128]{2,1,0:T(8,128)(2,1)S(1)}, u32[]{:S(2)}, u32[]{:S(2)}) %collective-permute-start.6) | collective-permute-done | bytes 262176 | tf_op jit(solution)/shard_map/ppermute | solution.py:226
  134.0 0.9 join.1
  134.9 4.1 %all-to-all-start.4 = ((bf16[4,384,128]{2,1,0:T(8,128)(2,1)}), bf16[4,384,128]{2,1,0:T(8,128)(2,1)S(1)}, u32[]{:S(2)}, u32[]{:S(2)}) async-start(bf16[4,384,128]{2,1,0:T(8,128)(2,1)} %join.1), calls=%async_computation.4 | async-start | bytes 786432 | tf_op jit(solution)/shard_map/all_to_all | solution.py:294
  139.0 0.8 unpack_query.1
  139.8 5.8 %all-to-all-done.4.kv_ref = bf16[4,384,128]{2,1,0:T(8,128)(2,1)S(1)} async-done(((bf16[4,384,128]{2,1,0:T(8,128)(2,1)}), bf16[4,384,128]{2,1,0:T(8,128)(2,1)S(1)}, u32[]{:S(2)}, u32[]{:S(2)}) %all-to-all-start.4) | async-done | bytes 393248 | tf_op jit(solution)/shard_map/all_to_all | solution.py:294
  145.6 1.0 unpack.1
  (10 shorter events, 0.1 us)
Async XLA Ops:
  2.5 15.4 %all-to-all-start.1 = ((bf16[4,256,128]{2,1,0:T(8,128)(2,1)}), bf16[4,256,128]{2,1,0:T(8,128)(2,1)S(1)}, u32[]{:S(2)}, u32[]{:S(2)}) async-start(bf16[4,256,128]{2,1,0:T(8,128)(2,1)} %pack_key.1), calls=%async_computation.1 | async-start | bytes 524288 | tf_op jit(solution)/shard_map/all_to_all | solution.py:253
  17.9 48.1 %all-to-all-start = ((bf16[16,400,128]{2,1,0:T(8,128)(2,1)}), bf16[16,400,128]{2,1,0:T(8,128)(2,1)S(1)}, u32[]{:S(2)}, u32[]{:S(2)}) async-start(bf16[16,400,128]{2,1,0:T(8,128)(2,1)} %pack_query.1), calls=%async_computation | async-start | bytes 3276800 | tf_op jit(solution)/shard_map/all_to_all | solution.py:256
  22.3 32.4 %collective-permute-start.1 = (bf16[4,256,128]{2,1,0:T(8,128)(2,1)S(1)}, bf16[4,256,128]{2,1,0:T(8,128)(2,1)S(1)}, u32[]{:S(2)}, u32[]{:S(2)}) collective-permute-start(bf16[4,256,128]{2,1,0:T(8,128)(2,1)S(1)} %all-to-all-done.1.kv0_ref), channel_id=1, source_target_pairs={{0,2},{2,4},{4,6},{6,0},{1,3},{3,5},{5,7},{7,1},{8,10},{10,12},{12... | collective-permute-start | bytes 786440 | tf_op jit(solution)/shard_map/ppermute | solution.py:226
  24.2 35.2 %collective-permute-start = (bf16[4,256,128]{2,1,0:T(8,128)(2,1)S(1)}, bf16[4,256,128]{2,1,0:T(8,128)(2,1)S(1)}, u32[]{:S(2)}, u32[]{:S(2)}) collective-permute-start(bf16[4,256,128]{2,1,0:T(8,128)(2,1)S(1)} %all-to-all-done.1.kv0_ref), channel_id=1, source_target_pairs={{0,6},{2,0},{4,2},{6,4},{1,7},{3,1},{5,3},{7,5},{8,14},{10,8},{12,... | collective-permute-start | bytes 786440 | tf_op jit(solution)/shard_map/ppermute | solution.py:226
  54.7 8.4 %collective-permute-start.2 = (bf16[4,128,128]{2,1,0:T(8,128)(2,1)S(1)}, bf16[4,128,128]{2,1,0:T(8,128)(2,1)S(1)}, u32[]{:S(2)}, u32[]{:S(2)}) collective-permute-start(bf16[4,128,128]{2,1,0:T(8,128)(2,1)S(1)} %slice.8), channel_id=1, source_target_pairs={{0,2},{2,4},{4,6},{6,0},{1,3},{3,5},{5,7},{7,1},{8,10},{10,12},{12... | collective-permute-start | bytes 393224 | tf_op jit(solution)/shard_map/ppermute | solution.py:226
  59.4 6.6 %collective-permute-start.3 = (bf16[4,128,128]{2,1,0:T(8,128)(2,1)S(1)}, bf16[4,128,128]{2,1,0:T(8,128)(2,1)S(1)}, u32[]{:S(2)}, u32[]{:S(2)}) collective-permute-start(bf16[4,128,128]{2,1,0:T(8,128)(2,1)S(1)} %slice.9), channel_id=1, source_target_pairs={{0,6},{2,0},{4,2},{6,4},{1,7},{3,1},{5,3},{7,5},{8,14},{10,8},{12,... | collective-permute-start | bytes 393224 | tf_op jit(solution)/shard_map/ppermute | solution.py:226
  77.1 0.7 copy-start
  77.7 0.7 copy-start.1
  78.4 26.1 %all-to-all-start.2 = ((bf16[16,128,128]{2,1,0:T(8,128)(2,1)}), bf16[16,128,128]{2,1,0:T(8,128)(2,1)S(1)}, u32[]{:S(2)}, u32[]{:S(2)}) async-start(bf16[16,128,128]{2,1,0:T(8,128)(2,1)} %get-tuple-element.30), calls=%async_computation.2 | async-start | bytes 1048576 | tf_op jit(solution)/shard_map/all_to_all | solution.py:279
  88.9 8.7 %collective-permute-start.4 = (bf16[4,128,128]{2,1,0:T(8,128)(2,1)}, bf16[4,128,128]{2,1,0:T(8,128)(2,1)S(1)}, u32[]{:S(2)}, u32[]{:S(2)}) collective-permute-start(bf16[4,128,128]{2,1,0:T(8,128)(2,1)} %copy-done.1), channel_id=1, source_target_pairs={{0,2},{2,4},{4,6},{6,0},{1,3},{3,5},{5,7},{7,1},{8,10},{10,12},{12... | collective-permute-start | bytes 393224 | tf_op jit(solution)/shard_map/ppermute | solution.py:226
  94.0 6.8 %collective-permute-start.5 = (bf16[4,128,128]{2,1,0:T(8,128)(2,1)}, bf16[4,128,128]{2,1,0:T(8,128)(2,1)S(1)}, u32[]{:S(2)}, u32[]{:S(2)}) collective-permute-start(bf16[4,128,128]{2,1,0:T(8,128)(2,1)} %copy-done), channel_id=1, source_target_pairs={{0,6},{2,0},{4,2},{6,4},{1,7},{3,1},{5,3},{7,5},{8,14},{10,8},{12,... | collective-permute-start | bytes 393224 | tf_op jit(solution)/shard_map/ppermute | solution.py:226
  104.5 29.5 %all-to-all-start.3 = ((bf16[16,128,128]{2,1,0:T(8,128)(2,1)}), bf16[16,128,128]{2,1,0:T(8,128)(2,1)S(1)}, u32[]{:S(2)}, u32[]{:S(2)}) async-start(bf16[16,128,128]{2,1,0:T(8,128)(2,1)} %get-tuple-element.35), calls=%async_computation.3 | async-start | bytes 1048576 | tf_op jit(solution)/shard_map/all_to_all | solution.py:284
  112.2 21.8 %collective-permute-start.6 = (bf16[4,256,128]{2,1,0:T(8,128)(2,1)S(1)}, bf16[4,256,128]{2,1,0:T(8,128)(2,1)S(1)}, u32[]{:S(2)}, u32[]{:S(2)}) collective-permute-start(bf16[4,256,128]{2,1,0:T(8,128)(2,1)S(1)} %get-tuple-element.32), channel_id=1, source_target_pairs={{0,2},{2,4},{4,6},{6,0},{1,3},{3,5},{5,7},{7,1},{8,10},{10,12},{12... | collective-permute-start | bytes 786440 | tf_op jit(solution)/shard_map/ppermute | solution.py:226
  117.1 16.9 %collective-permute-start.7 = (bf16[4,256,128]{2,1,0:T(8,128)(2,1)S(1)}, bf16[4,256,128]{2,1,0:T(8,128)(2,1)S(1)}, u32[]{:S(2)}, u32[]{:S(2)}) collective-permute-start(bf16[4,256,128]{2,1,0:T(8,128)(2,1)S(1)} %get-tuple-element.33), channel_id=1, source_target_pairs={{0,6},{2,0},{4,2},{6,4},{1,7},{3,1},{5,3},{7,5},{8,14},{10,8},{12,... | collective-permute-start | bytes 786440 | tf_op jit(solution)/shard_map/ppermute | solution.py:226
  119.9 0.7 collective-permute-start.8
  134.9 10.7 %all-to-all-start.4 = ((bf16[4,384,128]{2,1,0:T(8,128)(2,1)}), bf16[4,384,128]{2,1,0:T(8,128)(2,1)S(1)}, u32[]{:S(2)}, u32[]{:S(2)}) async-start(bf16[4,384,128]{2,1,0:T(8,128)(2,1)} %join.1), calls=%async_computation.4 | async-start | bytes 786432 | tf_op jit(solution)/shard_map/all_to_all | solution.py:294

commit v7 on v6

--- a/solution.py
+++ b/solution.py
@@ -32,36 +32,22 @@
     return x.astype(F32).T.astype(BF16)
 
 
-def pack_key_kernel(k_hbm, v_hbm, to_key_ref, k_ref, v_ref, sems):
-    copies = fetch(((k_hbm, k_ref), (v_hbm, v_ref)), sems)
-    for copy in copies:
+def pack_kernel(scale, k_hbm, v_hbm, q_hbm, g_hbm, o_hbm, l_hbm, out_ref, k_ref, v_ref, q_ref, g_ref, o_ref, l_ref, sems):
+    copies = fetch(
+        ((k_hbm, k_ref), (v_hbm, v_ref), (q_hbm, q_ref), (g_hbm, g_ref), (o_hbm, o_ref), (l_hbm, l_ref)), sems
+    )
+    lines = lax.broadcasted_iota(jnp.int32, (AUG, 128), 0)
+    extra = [jnp.zeros((AUG, 128), F32)] * 4
+    for copy in copies[:2]:
         copy.wait()
     for i in range(4):
         k_t, v_t = turned(k_ref[i]), turned(v_ref[i])
         for h in range(4):
             part = slice(h * 32, h * 32 + 32)
-            to_key_ref[h, i * 32 : i * 32 + 32, :] = k_t[part]
-            to_key_ref[h, 128 + i * 32 : 160 + i * 32, :] = v_t[part]
-
-
-def pack_query_kernel(
-    scale, which_ref, q_hbm, g_hbm, o_hbm, l_hbm, bias_hbm, to_query_ref, q_ref, g_ref, o_ref, l_ref, bias_ref, sems
-):
-    quarter = pl.multiple_of(which_ref[0] * 32, 32)
-    copies = fetch(
-        (
-            (q_hbm, q_ref),
-            (g_hbm, g_ref),
-            (o_hbm, o_ref),
-            (l_hbm, l_ref),
-            (bias_hbm.at[:, pl.ds(quarter, 32), :], bias_ref),
-        ),
-        sems,
-    )
-    lines = lax.broadcasted_iota(jnp.int32, (AUG, 128), 0)
-    for copy in copies[:4]:
+            out_ref[h, i * 32 : i * 32 + 32, :] = k_t[part]
+            out_ref[h, 128 + i * 32 : 160 + i * 32, :] = v_t[part]
+    for copy in copies[2:]:
         copy.wait()
-    extra = [jnp.zeros((AUG, 128), F32)] * 4
     for i in range(4):
         q_t = turned(q_ref[i])
         g_f = g_ref[i].astype(F32)
@@ -73,26 +59,39 @@
             delta = -jnp.sum(gg[part], axis=0, keepdims=True)
             for at, piece in enumerate(two_parts(offset) + two_parts(delta)):
                 extra[h] = jnp.where(lines == i * 4 + at, piece, extra[h])
-            for a in range(4):
-                to_query_ref[h * 4 + a, i * 64 : i * 64 + 32, :] = q_t[part]
-                to_query_ref[h * 4 + a, i * 64 + 32 : i * 64 + 64, :] = g_t[part]
+            out_ref[h, 256 + i * 64 : 288 + i * 64, :] = q_t[part]
+            out_ref[h, 288 + i * 64 : 320 + i * 64, :] = g_t[part]
     for h in range(4):
-        for a in range(4):
-            to_query_ref[h * 4 + a, 256:272, :] = extra[h].astype(BF16)
-    copies[4].wait()
-    for h in range(4):
-        for a in range(4):
-            for yh in range(4):
-                block = (a // 2) * 8 + yh * 2 + a % 2
-                to_query_ref[h * 4 + a, 272 + yh * 32 : 304 + yh * 32, :] = bias_ref[
-                    h, :, block * 128 : block * 128 + 128
-                ]
+        out_ref[h, 512:528, :] = extra[h].astype(BF16)
+
+
+def bias_kernel(where_ref, bias_hbm, out_ref, bias_ref, sem):
+    copy = pltpu.make_async_copy(bias_hbm.at[where_ref[0]], bias_ref, sem)
+    copy.start()
+    copy.wait()
+    for d in range(4):
+        for yh in range(4):
+            block = where_ref[1 + d] * 4 + yh
+            first = ((block // 8) * 8 + (block % 4) * 2 + (block // 4) % 2) * 128
+            out_ref[d, yh * 128 : yh * 128 + 128, :] = bias_ref[:, pl.ds(pl.multiple_of(first, 128), 128)]
+
+
+def assemble_kernel(got_ref, bias_ref, key_ref, *pay_refs):
+    for s in range(4):
+        key_ref[s] = got_ref[s, :256, :]
+    for d, pay_ref in enumerate(pay_refs):
+        for s in range(4):
+            pay_ref[s, :272, :] = got_ref[s, 256:528, :]
+            pay_ref[s, 272:400, :] = bias_ref[d, s * 128 : s * 128 + 128, :]
 
 
 def attend_kernel(
     scale,
-    yh_ref,
-    jq_ref,
+    where_ref,
+    pay0_ref,
+    pay1_ref,
+    pay2_ref,
+    pay3_ref,
     kv0_ref,
     kv1_ref,
     k2_ref,
@@ -109,13 +108,14 @@
     acc_s,
 ):
     dkv_refs = (dkv0_ref, dkv1_ref, None, dkv3_ref)
-    owner = [lax.rem(yh_ref[0] + p, 4) for p in range(4)]
-    for a in range(4):
-        for s in range(4):
-            for p in range(4):
-                bias_s[a * 128 + s * 32 : a * 128 + s * 32 + 32, p * 128 : p * 128 + 128] = (
-                    jq_ref[s * 4 + a, pl.ds(pl.multiple_of(272 + owner[p] * 32, 16), 32), :].astype(F32) * LOG2E
-                )
+    owner = [lax.rem(where_ref[5] + p, 4) for p in range(4)]
+    pay_refs = (pay0_ref, pay1_ref, pay2_ref, pay3_ref)
+    block_of = [where_ref[1 + d] for d in range(4)]
+    for d in range(4):
+        for p in range(4):
+            bias_s[d * 128 : d * 128 + 128, p * 128 : p * 128 + 128] = (
+                pay_refs[d][owner[p], 272:400, :].astype(F32) * LOG2E
+            )
     acc_s[...] = jnp.zeros_like(acc_s)
     lines = lax.broadcasted_iota(jnp.int32, (AUG, 512), 0)
     ones = [
@@ -127,7 +127,7 @@
         for i in range(4):
             first = i * 64
             q_t, g_t, extra = (
-                jnp.concatenate([jq_ref[base + a, start : start + size, :] for a in range(4)], axis=1)
+                jnp.concatenate([pay_ref[s, start : start + size, :] for pay_ref in pay_refs], axis=1)
                 for start, size in ((first, 32), (first + 32, 32), (256, 16))
             )
             low_at, high_at = slice(i * 32, i * 32 + 32), slice(128 + i * 32, 160 + i * 32)
@@ -152,7 +152,7 @@
             dq = (jnp.dot(low, k_t.T, preferred_element_type=F32).T * scale).astype(BF16)
             for b in range(4):
                 block = slice(b * 128, b * 128 + 128)
-                dq_ref[base + b, i * 32 : i * 32 + 32, :] = dq[:, block]
+                dq_ref[base + block_of[b], i * 32 : i * 32 + 32, :] = dq[:, block]
                 if b == 2:
                     dk2_ref[s, low_at, :] = dk[:, block]
                     dv2_ref[s, low_at, :] = dv[:, block]
@@ -163,11 +163,9 @@
 
     lax.fori_loop(0, 4, four_rows, 0)
     for p in range(4):
-        for xh in range(2):
-            for yl in range(2):
-                j = (xh * 2 + yl) * 128
-                piece = acc_s[j : j + 128, p * 128 : p * 128 + 128].astype(BF16)
-                db_ref[owner[p] * 4 + yl * 2 + xh] = piece
+        for d in range(4):
+            to = owner[p] * 4 + lax.rem(block_of[d], 2) * 2 + block_of[d] // 2
+            db_ref[to] = acc_s[d * 128 : d * 128 + 128, p * 128 : p * 128 + 128].astype(BF16)
 
 
 def fold_kernel(up_ref, up_more_ref, down_ref, down_more_ref, up_out_ref, down_out_ref):
@@ -229,44 +227,55 @@
 def body(queries, keys, values, bias, out_grad, outputs, logsumexp):
     scale = 32 ** (-0.5)
     shape = lambda *s: jax.ShapeDtypeStruct(s, BF16)
-    which = (lax.axis_index("xl") * 2 + lax.axis_index("c")).astype(jnp.int32).reshape(1)
+    head = lax.axis_index("xl") * 2 + lax.axis_index("c")
+    mine = lax.axis_index("xh") * 2 + lax.axis_index("yl")
+    where = jnp.stack([head] + [mine ^ d for d in range(4)] + [lax.axis_index("yh")]).astype(jnp.int32)
     hbm = pl.BlockSpec(memory_space=pltpu.HBM)
-    to_key = pl.pallas_call(
-        pack_key_kernel,
-        out_shape=shape(4, 256, 128),
-        in_specs=[hbm] * 2,
+    smem = pl.BlockSpec(memory_space=pltpu.SMEM)
+    packed = pl.pallas_call(
+        functools.partial(pack_kernel, scale),
+        out_shape=shape(4, 528, 128),
+        in_specs=[hbm] * 6,
         out_specs=vmem()[0],
-        scratch_shapes=[pltpu.VMEM((4, 128, 128), BF16)] * 2 + [pltpu.SemaphoreType.DMA((2,))],
+        scratch_shapes=[pltpu.VMEM((4, 128, 128), BF16)] * 5
+        + [pltpu.VMEM((4, 4, 128), F32), pltpu.SemaphoreType.DMA((6,))],
         compiler_params=params(61),
-        name="pack_key",
-    )(keys, values)
-    to_query = pl.pallas_call(
-        functools.partial(pack_query_kernel, scale),
-        out_shape=shape(16, 400, 128),
-        in_specs=[pl.BlockSpec(memory_space=pltpu.SMEM)] + [hbm] * 5,
+        name="pack",
+    )(keys, values, queries, out_grad, outputs, logsumexp)
+    bias_out = pl.pallas_call(
+        bias_kernel,
+        out_shape=shape(4, 512, 128),
+        in_specs=[smem, hbm],
         out_specs=vmem()[0],
-        scratch_shapes=[pltpu.VMEM((4, 128, 128), BF16)] * 3
-        + [pltpu.VMEM((4, 4, 128), F32), pltpu.VMEM((4, 32, 2048), BF16), pltpu.SemaphoreType.DMA((5,))],
-        compiler_params=params(61),
-        name="pack_query",
-    )(which, queries, out_grad, outputs, logsumexp, bias)
-    own = lax.all_to_all(to_key, ("xl", "c"), 0, 0)
+        scratch_shapes=[pltpu.VMEM((128, 2048), BF16), pltpu.SemaphoreType.DMA],
+        compiler_params=params(),
+        name="bias",
+    )(where, bias)
+    got = lax.all_to_all(packed, ("xl", "c"), 0, 0)
+    own, *pays = pl.pallas_call(
+        assemble_kernel,
+        out_shape=(shape(4, 256, 128),) + (shape(4, 400, 128),) * 4,
+        in_specs=vmem(2),
+        out_specs=tuple(vmem(5)),
+        compiler_params=params(),
+        name="assemble",
+    )(got, bias_out)
     after, before = along(own, -1), along(own, 1)
+    for d in range(1, 4):
+        pays[d] = lax.ppermute(pays[d], ("xh", "yl"), [(n, n ^ d) for n in range(4)])
     k_far, v_far = along(before[:, :128], 1), along(after[:, 128:], -1)
-    got_query = lax.all_to_all(to_query, QUERY_GROUP, 0, 0)
-    yh = lax.axis_index("yh").astype(jnp.int32).reshape(1)
     dq_parts, own, up, dk_far, dv_far, down, db_parts = pl.pallas_call(
         functools.partial(attend_kernel, scale),
         out_shape=(shape(16, 128, 128),)
         + (shape(4, 256, 128),) * 2
         + (shape(4, 128, 128),) * 2
         + (shape(4, 256, 128), shape(16, 128, 128)),
-        in_specs=[pl.BlockSpec(memory_space=pltpu.SMEM)] + vmem(6),
+        in_specs=[smem] + vmem(9),
         out_specs=tuple(vmem(7)),
         scratch_shapes=[pltpu.VMEM((512, 512), F32), pltpu.VMEM((512, 512), F32)],
         compiler_params=params(),
         name="attend",
-    )(yh, got_query, own, after, k_far, v_far, before)
+    )(where, *pays, own, after, k_far, v_far, before)
     up_more, down_more = along(dk_far, 1), along(dv_far, -1)
     up, down = pl.pallas_call(
         fold_kernel,

time: 148 us -> 147 us (level)
  starting transfers between devices: 67.9 us -> 74.5 us
  waiting for transfers between devices: 58.3 us -> 52.3 us
    ppermute x0 -> x3, starting transfers between devices: none -> 9.88 us  [body(): lax.ppermute(pays[d], ('xh', 'yl'), [(n, n ^ d) for n in range(4)])]
    ppermute x8, waiting for transfers between devices: 46.4 us -> 36.6 us  [along(): return lax.ppermute(value, 'yh', [(n, (n + steps) % 4) for n in range(4)])]
    all_to_all x2 -> x1, waiting for transfers between devices: 2.59 us -> 7.24 us  [body(): got = lax.all_to_all(packed, ('xl', 'c'), 0, 0)]
    all_to_all x2 -> x1, starting transfers between devices: 14.7 us -> 10.3 us  [body(): got = lax.all_to_all(packed, ('xl', 'c'), 0, 0)]
    pallas_call x2 -> x3, Pallas kernels: 4.41 us -> 3.4 us  [the longest x1 2.38 us: body(): pl.pallas_call(functools.partial(pack_kernel, scale), out_shape=shape(4,...]
  transfers between devices with their start and end apart: 14 -> 16, of which waited for: 9 -> 9; matrix products, arithmetic and copies ran while one was open for 0% -> 0% of each run, Pallas kernels for 2% -> 1%
where the time goes in v7:
time: 147 us; the launch traced here: 146 us
  starting transfers between devices  74.5 us (51%)
  waiting for transfers between devices  52.3 us (36%)
  Pallas kernels  18 us (12%)
    ppermute x8, waiting for transfers between devices, along(): return lax.ppermute(value, 'yh', [(n, (n + steps) % 4) for n in range(4)])  36.6 us
    ppermute x8, starting transfers between devices, along(): return lax.ppermute(value, 'yh', [(n, (n + steps) % 4) for n in range(4)])  30.4 us
    pallas_call x1, Pallas kernels, body(): pl.pallas_call(functools.partial(attend_kernel, scale), out_shape=(shape(...  11.8 us
    all_to_all x1, starting transfers between devices, body(): db = lax.all_to_all(db_parts, ('z', 'xh'), 0, 0)  11.1 us
    all_to_all x1, starting transfers between devices, body(): got = lax.all_to_all(packed, ('xl', 'c'), 0, 0)  10.3 us
    ppermute x3, starting transfers between devices, body(): lax.ppermute(pays[d], ('xh', 'yl'), [(n, n ^ d) for n in range(4)])  9.88 us
    all_to_all x1, starting transfers between devices, body(): dq = lax.all_to_all(dq_parts, QUERY_GROUP, 0, 0)  8.11 us
    all_to_all x1, waiting for transfers between devices, body(): got = lax.all_to_all(packed, ('xl', 'c'), 0, 0)  7.24 us
  transfers between devices with their start and end apart: 16, of which 9 were waited for; matrix products, arithmetic and copies ran while one was open for 0% of the time, Pallas kernels for 1%

profile of v7, /device:TPU:1, one launch (start us, length us, event | category | flops | bytes accessed | tf_op | source)
XLA Modules:
  0.0 145.8 jit_solution(11693065427512639286)
XLA Ops:
  0.6 2.4 %pack.1 = bf16[4,528,128]{2,1,0:T(8,128)(2,1)} custom-call(bf16[4,128,128]{2,1,0:T(8,128)(2,1)} %k_hbm.1, bf16[4,128,128]{2,1,0:T(8,128)(2,1)} %v_hbm.1, bf16[4,128,128]{2,1,0:T(8,128)(2,1)} %q_hbm.1, bf16[4,128,128]{2,1,0:T(8,128)(2,1)} %g_hbm.1, bf16[4,128,128]{2,1,0:T(8,128)(2,1)} %o_hbm.1, f32[4,4,128]{2,1,0:T(4,128)} %l_hbm.1), custom_call_target="tpu_custom_call" | custom-call | tf_op jit(solution)/shard_map/pack/pallas_call | solution.py:235
  3.0 10.3 %all-to-all-start = ((bf16[4,528,128]{2,1,0:T(8,128)(2,1)}), bf16[4,528,128]{2,1,0:T(8,128)(2,1)S(1)}, u32[]{:S(2)}, u32[]{:S(2)}) async-start(bf16[4,528,128]{2,1,0:T(8,128)(2,1)} %pack.1), calls=%async_computation | async-start | bytes 1081344 | tf_op jit(solution)/shard_map/all_to_all | solution.py:254
  13.4 0.8 bias.1.bias_ref
  14.3 7.2 %all-to-all-done.got_ref = bf16[4,528,128]{2,1,0:T(8,128)(2,1)S(1)} async-done(((bf16[4,528,128]{2,1,0:T(8,128)(2,1)}), bf16[4,528,128]{2,1,0:T(8,128)(2,1)S(1)}, u32[]{:S(2)}, u32[]{:S(2)}) %all-to-all-start) | async-done | bytes 540704 | tf_op jit(solution)/shard_map/all_to_all | solution.py:254
  21.5 0.2 assemble.1
  21.7 1.9 %collective-permute-start = (bf16[4,400,128]{2,1,0:T(8,128)(2,1)S(1)}, bf16[4,400,128]{2,1,0:T(8,128)(2,1)S(1)}, u32[]{:S(2)}, u32[]{:S(2)}) collective-permute-start(bf16[4,400,128]{2,1,0:T(8,128)(2,1)S(1)} %get-tuple-element.30), channel_id=1, source_target_pairs={{0,1},{1,0},{8,9},{9,8},{2,3},{3,2},{10,11},{11,10},{4,5},{5,4},{1... | collective-permute-start | bytes 1228808 | tf_op jit(solution)/shard_map/ppermute | solution.py:265
  23.6 1.9 %collective-permute-start.1 = (bf16[4,400,128]{2,1,0:T(8,128)(2,1)S(1)}, bf16[4,400,128]{2,1,0:T(8,128)(2,1)S(1)}, u32[]{:S(2)}, u32[]{:S(2)}) collective-permute-start(bf16[4,400,128]{2,1,0:T(8,128)(2,1)S(1)} %get-tuple-element.31), channel_id=1, source_target_pairs={{0,8},{1,9},{8,0},{9,1},{2,10},{3,11},{10,2},{11,3},{4,12},{5,13},... | collective-permute-start | bytes 1228808 | tf_op jit(solution)/shard_map/ppermute | solution.py:265
  25.6 6.0 %collective-permute-start.2 = (bf16[4,400,128]{2,1,0:T(8,128)(2,1)S(1)}, bf16[4,400,128]{2,1,0:T(8,128)(2,1)S(1)}, u32[]{:S(2)}, u32[]{:S(2)}) collective-permute-start(bf16[4,400,128]{2,1,0:T(8,128)(2,1)S(1)} %get-tuple-element.32), channel_id=1, source_target_pairs={{0,9},{1,8},{8,1},{9,0},{2,11},{3,10},{10,3},{11,2},{4,13},{5,12},... | collective-permute-start | bytes 1228808 | tf_op jit(solution)/shard_map/ppermute | solution.py:265
  31.6 1.9 %collective-permute-start.4 = (bf16[4,256,128]{2,1,0:T(8,128)(2,1)S(1)}, bf16[4,256,128]{2,1,0:T(8,128)(2,1)S(1)}, u32[]{:S(2)}, u32[]{:S(2)}) collective-permute-start(bf16[4,256,128]{2,1,0:T(8,128)(2,1)S(1)} %get-tuple-element.33.kv0_ref), channel_id=1, source_target_pairs={{0,2},{2,4},{4,6},{6,0},{1,3},{3,5},{5,7},{7,1},{8,10},{10,12},{12... | collective-permute-start | bytes 786440 | tf_op jit(solution)/shard_map/ppermute | solution.py:224
  33.5 5.5 %collective-permute-start.3 = (bf16[4,256,128]{2,1,0:T(8,128)(2,1)S(1)}, bf16[4,256,128]{2,1,0:T(8,128)(2,1)S(1)}, u32[]{:S(2)}, u32[]{:S(2)}) collective-permute-start(bf16[4,256,128]{2,1,0:T(8,128)(2,1)S(1)} %get-tuple-element.33.kv0_ref), channel_id=1, source_target_pairs={{0,6},{2,0},{4,2},{6,4},{1,7},{3,1},{5,3},{7,5},{8,14},{10,8},{12,... | collective-permute-start | bytes 786440 | tf_op jit(solution)/shard_map/ppermute | solution.py:224
  39.0 15.3 %collective-permute-done.4.kv3_ref = bf16[4,256,128]{2,1,0:T(8,128)(2,1)S(1)} collective-permute-done((bf16[4,256,128]{2,1,0:T(8,128)(2,1)S(1)}, bf16[4,256,128]{2,1,0:T(8,128)(2,1)S(1)}, u32[]{:S(2)}, u32[]{:S(2)}) %collective-permute-start.4) | collective-permute-done | bytes 262176 | tf_op jit(solution)/shard_map/ppermute | solution.py:224
  54.4 4.2 %collective-permute-start.5 = (bf16[4,128,128]{2,1,0:T(8,128)(2,1)S(1)}, bf16[4,128,128]{2,1,0:T(8,128)(2,1)S(1)}, u32[]{:S(2)}, u32[]{:S(2)}) collective-permute-start(bf16[4,128,128]{2,1,0:T(8,128)(2,1)S(1)} %slice.8), channel_id=1, source_target_pairs={{0,2},{2,4},{4,6},{6,0},{1,3},{3,5},{5,7},{7,1},{8,10},{10,12},{12... | collective-permute-start | bytes 393224 | tf_op jit(solution)/shard_map/ppermute | solution.py:224
  58.6 3.2 %collective-permute-start.6 = (bf16[4,128,128]{2,1,0:T(8,128)(2,1)S(1)}, bf16[4,128,128]{2,1,0:T(8,128)(2,1)S(1)}, u32[]{:S(2)}, u32[]{:S(2)}) collective-permute-start(bf16[4,128,128]{2,1,0:T(8,128)(2,1)S(1)} %slice.9), channel_id=1, source_target_pairs={{0,6},{2,0},{4,2},{6,4},{1,7},{3,1},{5,3},{7,5},{8,14},{10,8},{12,... | collective-permute-start | bytes 393224 | tf_op jit(solution)/shard_map/ppermute | solution.py:224
  61.8 0.4 collective-permute-done.5.k2_ref
  62.2 3.0 %collective-permute-done.6.v2_ref = bf16[4,128,128]{2,1,0:T(8,128)(2,1)S(1)} collective-permute-done((bf16[4,128,128]{2,1,0:T(8,128)(2,1)S(1)}, bf16[4,128,128]{2,1,0:T(8,128)(2,1)S(1)}, u32[]{:S(2)}, u32[]{:S(2)}) %collective-permute-start.6) | collective-permute-done | bytes 131104 | tf_op jit(solution)/shard_map/ppermute | solution.py:224
  65.3 11.8 %attend.1 = (bf16[16,128,128]{2,1,0:T(8,128)(2,1)}, bf16[4,256,128]{2,1,0:T(8,128)(2,1)S(1)}, bf16[4,256,128]{2,1,0:T(8,128)(2,1)S(1)}, bf16[4,128,128]{2,1,0:T(...) custom-call(s32[6]{0:T(128)S(1)} %stack.27.where_ref, ...), custom_call_target="tpu_custom_call" | custom-call | tf_op jit(solution)/shard_map/attend/pallas_call | solution.py:267
  77.0 11.1 %all-to-all-start.1 = ((bf16[16,128,128]{2,1,0:T(8,128)(2,1)}), bf16[16,128,128]{2,1,0:T(8,128)(2,1)S(1)}, u32[]{:S(2)}, u32[]{:S(2)}) async-start(bf16[16,128,128]{2,1,0:T(8,128)(2,1)} %get-tuple-element.40), calls=%async_computation.1 | async-start | bytes 1048576 | tf_op jit(solution)/shard_map/all_to_all | solution.py:288
  88.1 4.9 %collective-permute-start.7 = (bf16[4,128,128]{2,1,0:T(8,128)(2,1)S(1)}, bf16[4,128,128]{2,1,0:T(8,128)(2,1)S(1)}, u32[]{:S(2)}, u32[]{:S(2)}) collective-permute-start(bf16[4,128,128]{2,1,0:T(8,128)(2,1)S(1)} %get-tuple-element.35), channel_id=1, source_target_pairs={{0,2},{2,4},{4,6},{6,0},{1,3},{3,5},{5,7},{7,1},{8,10},{10,12},{12... | collective-permute-start | bytes 393224 | tf_op jit(solution)/shard_map/ppermute | solution.py:224
  93.0 2.9 %collective-permute-start.8 = (bf16[4,128,128]{2,1,0:T(8,128)(2,1)S(1)}, bf16[4,128,128]{2,1,0:T(8,128)(2,1)S(1)}, u32[]{:S(2)}, u32[]{:S(2)}) collective-permute-start(bf16[4,128,128]{2,1,0:T(8,128)(2,1)S(1)} %get-tuple-element.37), channel_id=1, source_target_pairs={{0,6},{2,0},{4,2},{6,4},{1,7},{3,1},{5,3},{7,5},{8,14},{10,8},{12,... | collective-permute-start | bytes 393224 | tf_op jit(solution)/shard_map/ppermute | solution.py:224
  95.9 0.4 collective-permute-done.7.up_more_ref
  96.3 4.0 %collective-permute-done.8.down_more_ref = bf16[4,128,128]{2,1,0:T(8,128)(2,1)S(1)} collective-permute-done((bf16[4,128,128]{2,1,0:T(8,128)(2,1)S(1)}, bf16[4,128,128]{2,1,0:T(8,128)(2,1)S(1)}, u32[]{:S(2)}, u32[]{:S(2)}) %collective-permute-start.8) | collective-permute-done | bytes 131104 | tf_op jit(solution)/shard_map/ppermute | solution.py:224
  100.4 2.7 %all-to-all-done.1 = bf16[16,128,128]{2,1,0:T(8,128)(2,1)S(1)} async-done(((bf16[16,128,128]{2,1,0:T(8,128)(2,1)}), bf16[16,128,128]{2,1,0:T(8,128)(2,1)S(1)}, u32[]{:S(2)}, u32[]{:S(2)}) %all-to-all-start.1) | async-done | bytes 524320 | tf_op jit(solution)/shard_map/all_to_all | solution.py:288
  103.1 8.1 %all-to-all-start.2 = ((bf16[16,128,128]{2,1,0:T(8,128)(2,1)}), bf16[16,128,128]{2,1,0:T(8,128)(2,1)S(1)}, u32[]{:S(2)}, u32[]{:S(2)}) async-start(bf16[16,128,128]{2,1,0:T(8,128)(2,1)} %get-tuple-element.45), calls=%async_computation.2 | async-start | bytes 1048576 | tf_op jit(solution)/shard_map/all_to_all | solution.py:293
  111.2 4.8 %collective-permute-start.9 = (bf16[4,256,128]{2,1,0:T(8,128)(2,1)S(1)}, bf16[4,256,128]{2,1,0:T(8,128)(2,1)S(1)}, u32[]{:S(2)}, u32[]{:S(2)}) collective-permute-start(bf16[4,256,128]{2,1,0:T(8,128)(2,1)S(1)} %get-tuple-element.42), channel_id=1, source_target_pairs={{0,2},{2,4},{4,6},{6,0},{1,3},{3,5},{5,7},{7,1},{8,10},{10,12},{12... | collective-permute-start | bytes 786440 | tf_op jit(solution)/shard_map/ppermute | solution.py:224
  116.0 2.9 %collective-permute-start.10 = (bf16[4,256,128]{2,1,0:T(8,128)(2,1)S(1)}, bf16[4,256,128]{2,1,0:T(8,128)(2,1)S(1)}, u32[]{:S(2)}, u32[]{:S(2)}) collective-permute-start(bf16[4,256,128]{2,1,0:T(8,128)(2,1)S(1)} %get-tuple-element.43), channel_id=1, source_target_pairs={{0,6},{2,0},{4,2},{6,4},{1,7},{3,1},{5,3},{7,5},{8,14},{10,8},{12,... | collective-permute-start | bytes 786440 | tf_op jit(solution)/shard_map/ppermute | solution.py:224
  119.1 0.7 collective-permute-start.11
  119.8 13.4 %collective-permute-done.9.up_ref = bf16[4,256,128]{2,1,0:T(8,128)(2,1)S(1)} collective-permute-done((bf16[4,256,128]{2,1,0:T(8,128)(2,1)S(1)}, bf16[4,256,128]{2,1,0:T(8,128)(2,1)S(1)}, u32[]{:S(2)}, u32[]{:S(2)}) %collective-permute-start.9) | collective-permute-done | bytes 262176 | tf_op jit(solution)/shard_map/ppermute | solution.py:224
  133.2 0.9 join.1
  134.1 4.1 %all-to-all-start.3 = ((bf16[4,384,128]{2,1,0:T(8,128)(2,1)}), bf16[4,384,128]{2,1,0:T(8,128)(2,1)S(1)}, u32[]{:S(2)}, u32[]{:S(2)}) async-start(bf16[4,384,128]{2,1,0:T(8,128)(2,1)} %join.1), calls=%async_computation.3 | async-start | bytes 786432 | tf_op jit(solution)/shard_map/all_to_all | solution.py:303
  138.2 0.8 unpack_query.1
  139.0 5.8 %all-to-all-done.3.kv_ref = bf16[4,384,128]{2,1,0:T(8,128)(2,1)S(1)} async-done(((bf16[4,384,128]{2,1,0:T(8,128)(2,1)}), bf16[4,384,128]{2,1,0:T(8,128)(2,1)S(1)}, u32[]{:S(2)}, u32[]{:S(2)}) %all-to-all-start.3) | async-done | bytes 393248 | tf_op jit(solution)/shard_map/all_to_all | solution.py:303
  144.8 1.0 unpack.1
  (14 shorter events, 0.3 us)
Async XLA Ops:
  0.6 12.8 %copy-start = (bf16[4,128,2048]{2,1,0:T(8,128)(2,1)S(1)}, bf16[4,128,2048]{2,1,0:T(8,128)(2,1)}, u32[]{:S(2)}) copy-start(bf16[4,128,2048]{2,1,0:T(8,128)(2,1)} %bias_hbm.1) | copy-start | bytes 6291460
  3.0 18.5 %all-to-all-start = ((bf16[4,528,128]{2,1,0:T(8,128)(2,1)}), bf16[4,528,128]{2,1,0:T(8,128)(2,1)S(1)}, u32[]{:S(2)}, u32[]{:S(2)}) async-start(bf16[4,528,128]{2,1,0:T(8,128)(2,1)} %pack.1), calls=%async_computation | async-start | bytes 1081344 | tf_op jit(solution)/shard_map/all_to_all | solution.py:254
  21.7 43.5 %collective-permute-start = (bf16[4,400,128]{2,1,0:T(8,128)(2,1)S(1)}, bf16[4,400,128]{2,1,0:T(8,128)(2,1)S(1)}, u32[]{:S(2)}, u32[]{:S(2)}) collective-permute-start(bf16[4,400,128]{2,1,0:T(8,128)(2,1)S(1)} %get-tuple-element.30), channel_id=1, source_target_pairs={{0,1},{1,0},{8,9},{9,8},{2,3},{3,2},{10,11},{11,10},{4,5},{5,4},{1... | collective-permute-start | bytes 1228808 | tf_op jit(solution)/shard_map/ppermute | solution.py:265
  23.6 41.6 %collective-permute-start.1 = (bf16[4,400,128]{2,1,0:T(8,128)(2,1)S(1)}, bf16[4,400,128]{2,1,0:T(8,128)(2,1)S(1)}, u32[]{:S(2)}, u32[]{:S(2)}) collective-permute-start(bf16[4,400,128]{2,1,0:T(8,128)(2,1)S(1)} %get-tuple-element.31), channel_id=1, source_target_pairs={{0,8},{1,9},{8,0},{9,1},{2,10},{3,11},{10,2},{11,3},{4,12},{5,13},... | collective-permute-start | bytes 1228808 | tf_op jit(solution)/shard_map/ppermute | solution.py:265
  25.6 39.7 %collective-permute-start.2 = (bf16[4,400,128]{2,1,0:T(8,128)(2,1)S(1)}, bf16[4,400,128]{2,1,0:T(8,128)(2,1)S(1)}, u32[]{:S(2)}, u32[]{:S(2)}) collective-permute-start(bf16[4,400,128]{2,1,0:T(8,128)(2,1)S(1)} %get-tuple-element.32), channel_id=1, source_target_pairs={{0,9},{1,8},{8,1},{9,0},{2,11},{3,10},{10,3},{11,2},{4,13},{5,12},... | collective-permute-start | bytes 1228808 | tf_op jit(solution)/shard_map/ppermute | solution.py:265
  31.6 22.8 %collective-permute-start.4 = (bf16[4,256,128]{2,1,0:T(8,128)(2,1)S(1)}, bf16[4,256,128]{2,1,0:T(8,128)(2,1)S(1)}, u32[]{:S(2)}, u32[]{:S(2)}) collective-permute-start(bf16[4,256,128]{2,1,0:T(8,128)(2,1)S(1)} %get-tuple-element.33.kv0_ref), channel_id=1, source_target_pairs={{0,2},{2,4},{4,6},{6,0},{1,3},{3,5},{5,7},{7,1},{8,10},{10,12},{12... | collective-permute-start | bytes 786440 | tf_op jit(solution)/shard_map/ppermute | solution.py:224
  33.5 25.0 %collective-permute-start.3 = (bf16[4,256,128]{2,1,0:T(8,128)(2,1)S(1)}, bf16[4,256,128]{2,1,0:T(8,128)(2,1)S(1)}, u32[]{:S(2)}, u32[]{:S(2)}) collective-permute-start(bf16[4,256,128]{2,1,0:T(8,128)(2,1)S(1)} %get-tuple-element.33.kv0_ref), channel_id=1, source_target_pairs={{0,6},{2,0},{4,2},{6,4},{1,7},{3,1},{5,3},{7,5},{8,14},{10,8},{12,... | collective-permute-start | bytes 786440 | tf_op jit(solution)/shard_map/ppermute | solution.py:224
  54.4 7.8 %collective-permute-start.5 = (bf16[4,128,128]{2,1,0:T(8,128)(2,1)S(1)}, bf16[4,128,128]{2,1,0:T(8,128)(2,1)S(1)}, u32[]{:S(2)}, u32[]{:S(2)}) collective-permute-start(bf16[4,128,128]{2,1,0:T(8,128)(2,1)S(1)} %slice.8), channel_id=1, source_target_pairs={{0,2},{2,4},{4,6},{6,0},{1,3},{3,5},{5,7},{7,1},{8,10},{10,12},{12... | collective-permute-start | bytes 393224 | tf_op jit(solution)/shard_map/ppermute | solution.py:224
  58.6 6.6 %collective-permute-start.6 = (bf16[4,128,128]{2,1,0:T(8,128)(2,1)S(1)}, bf16[4,128,128]{2,1,0:T(8,128)(2,1)S(1)}, u32[]{:S(2)}, u32[]{:S(2)}) collective-permute-start(bf16[4,128,128]{2,1,0:T(8,128)(2,1)S(1)} %slice.9), channel_id=1, source_target_pairs={{0,6},{2,0},{4,2},{6,4},{1,7},{3,1},{5,3},{7,5},{8,14},{10,8},{12,... | collective-permute-start | bytes 393224 | tf_op jit(solution)/shard_map/ppermute | solution.py:224
  77.0 26.1 %all-to-all-start.1 = ((bf16[16,128,128]{2,1,0:T(8,128)(2,1)}), bf16[16,128,128]{2,1,0:T(8,128)(2,1)S(1)}, u32[]{:S(2)}, u32[]{:S(2)}) async-start(bf16[16,128,128]{2,1,0:T(8,128)(2,1)} %get-tuple-element.40), calls=%async_computation.1 | async-start | bytes 1048576 | tf_op jit(solution)/shard_map/all_to_all | solution.py:288
  88.1 8.2 %collective-permute-start.7 = (bf16[4,128,128]{2,1,0:T(8,128)(2,1)S(1)}, bf16[4,128,128]{2,1,0:T(8,128)(2,1)S(1)}, u32[]{:S(2)}, u32[]{:S(2)}) collective-permute-start(bf16[4,128,128]{2,1,0:T(8,128)(2,1)S(1)} %get-tuple-element.35), channel_id=1, source_target_pairs={{0,2},{2,4},{4,6},{6,0},{1,3},{3,5},{5,7},{7,1},{8,10},{10,12},{12... | collective-permute-start | bytes 393224 | tf_op jit(solution)/shard_map/ppermute | solution.py:224
  93.0 7.4 %collective-permute-start.8 = (bf16[4,128,128]{2,1,0:T(8,128)(2,1)S(1)}, bf16[4,128,128]{2,1,0:T(8,128)(2,1)S(1)}, u32[]{:S(2)}, u32[]{:S(2)}) collective-permute-start(bf16[4,128,128]{2,1,0:T(8,128)(2,1)S(1)} %get-tuple-element.37), channel_id=1, source_target_pairs={{0,6},{2,0},{4,2},{6,4},{1,7},{3,1},{5,3},{7,5},{8,14},{10,8},{12,... | collective-permute-start | bytes 393224 | tf_op jit(solution)/shard_map/ppermute | solution.py:224
  103.1 30.1 %all-to-all-start.2 = ((bf16[16,128,128]{2,1,0:T(8,128)(2,1)}), bf16[16,128,128]{2,1,0:T(8,128)(2,1)S(1)}, u32[]{:S(2)}, u32[]{:S(2)}) async-start(bf16[16,128,128]{2,1,0:T(8,128)(2,1)} %get-tuple-element.45), calls=%async_computation.2 | async-start | bytes 1048576 | tf_op jit(solution)/shard_map/all_to_all | solution.py:293
  111.2 22.0 %collective-permute-start.9 = (bf16[4,256,128]{2,1,0:T(8,128)(2,1)S(1)}, bf16[4,256,128]{2,1,0:T(8,128)(2,1)S(1)}, u32[]{:S(2)}, u32[]{:S(2)}) collective-permute-start(bf16[4,256,128]{2,1,0:T(8,128)(2,1)S(1)} %get-tuple-element.42), channel_id=1, source_target_pairs={{0,2},{2,4},{4,6},{6,0},{1,3},{3,5},{5,7},{7,1},{8,10},{10,12},{12... | collective-permute-start | bytes 786440 | tf_op jit(solution)/shard_map/ppermute | solution.py:224
  116.0 17.1 %collective-permute-start.10 = (bf16[4,256,128]{2,1,0:T(8,128)(2,1)S(1)}, bf16[4,256,128]{2,1,0:T(8,128)(2,1)S(1)}, u32[]{:S(2)}, u32[]{:S(2)}) collective-permute-start(bf16[4,256,128]{2,1,0:T(8,128)(2,1)S(1)} %get-tuple-element.43), channel_id=1, source_target_pairs={{0,6},{2,0},{4,2},{6,4},{1,7},{3,1},{5,3},{7,5},{8,14},{10,8},{12,... | collective-permute-start | bytes 786440 | tf_op jit(solution)/shard_map/ppermute | solution.py:224
  119.1 0.7 collective-permute-start.11
  134.1 10.7 %all-to-all-start.3 = ((bf16[4,384,128]{2,1,0:T(8,128)(2,1)}), bf16[4,384,128]{2,1,0:T(8,128)(2,1)S(1)}, u32[]{:S(2)}, u32[]{:S(2)}) async-start(bf16[4,384,128]{2,1,0:T(8,128)(2,1)} %join.1), calls=%async_computation.3 | async-start | bytes 786432 | tf_op jit(solution)/shard_map/all_to_all | solution.py:303

commit v8 on v7

--- a/solution.py
+++ b/solution.py
@@ -78,7 +78,7 @@
 
 def assemble_kernel(got_ref, bias_ref, key_ref, *pay_refs):
     for s in range(4):
-        key_ref[s] = got_ref[s, :256, :]
+        key_ref[s] = got_ref[s, :272, :]
     for d, pay_ref in enumerate(pay_refs):
         for s in range(4):
             pay_ref[s, :272, :] = got_ref[s, 256:528, :]
@@ -254,7 +254,7 @@
     got = lax.all_to_all(packed, ("xl", "c"), 0, 0)
     own, *pays = pl.pallas_call(
         assemble_kernel,
-        out_shape=(shape(4, 256, 128),) + (shape(4, 400, 128),) * 4,
+        out_shape=(shape(4, 272, 128),) + (shape(4, 400, 128),) * 4,
         in_specs=vmem(2),
         out_specs=tuple(vmem(5)),
         compiler_params=params(),
@@ -263,7 +263,7 @@
     after, before = along(own, -1), along(own, 1)
     for d in range(1, 4):
         pays[d] = lax.ppermute(pays[d], ("xh", "yl"), [(n, n ^ d) for n in range(4)])
-    k_far, v_far = along(before[:, :128], 1), along(after[:, 128:], -1)
+    k_far, v_far = along(before[:, :128], 1), along(after[:, 128:256], -1)
     dq_parts, own, up, dk_far, dv_far, down, db_parts = pl.pallas_call(
         functools.partial(attend_kernel, scale),
         out_shape=(shape(16, 128, 128),)

time: 147 us -> 143 us (0.973)
  the two profiles are of different devices: /device:TPU:1 before, /device:TPU:64 now
where the time goes in v8:
time: 143 us; the launch traced here: 142 us
  starting transfers between devices  70.6 us (49%)
  waiting for transfers between devices  52.8 us (37%)
  Pallas kernels  17.9 us (13%)
    ppermute x8, starting transfers between devices, along(): return lax.ppermute(value, 'yh', [(n, (n + steps) % 4) for n in range(4)])  31.9 us
    ppermute x8, waiting for transfers between devices, along(): return lax.ppermute(value, 'yh', [(n, (n + steps) % 4) for n in range(4)])  18.7 us
    ppermute x1, waiting for transfers between devices, body(): db = lax.ppermute(db, ('z', 'yl'), swaps())  12.3 us
    pallas_call x1, Pallas kernels, body(): pl.pallas_call(functools.partial(attend_kernel, scale), out_shape=(shape(...  11.7 us
    ppermute x3, starting transfers between devices, body(): lax.ppermute(pays[d], ('xh', 'yl'), [(n, n ^ d) for n in range(4)])  10.7 us
    all_to_all x1, starting transfers between devices, body(): db = lax.all_to_all(db_parts, ('z', 'xh'), 0, 0)  9.98 us
    all_to_all x1, waiting for transfers between devices, body(): got = lax.all_to_all(packed, ('xl', 'c'), 0, 0)  8.06 us
    all_to_all x1, waiting for transfers between devices, body(): joined = lax.all_to_all(joined, ('xl', 'c'), 0, 0)  6.61 us
  transfers between devices with their start and end apart: 16, of which 9 were waited for; matrix products, arithmetic and copies ran while one was open for 0% of the time, Pallas kernels for 1%

profile of v8, /device:TPU:64, one launch (start us, length us, event | category | flops | bytes accessed | tf_op | source)
XLA Modules:
  0.0 142.4 jit_solution(222117822991048204)
XLA Ops:
  0.6 2.4 %pack.1 = bf16[4,528,128]{2,1,0:T(8,128)(2,1)} custom-call(bf16[4,128,128]{2,1,0:T(8,128)(2,1)} %k_hbm.1, bf16[4,128,128]{2,1,0:T(8,128)(2,1)} %v_hbm.1, bf16[4,128,128]{2,1,0:T(8,128)(2,1)} %q_hbm.1, bf16[4,128,128]{2,1,0:T(8,128)(2,1)} %g_hbm.1, bf16[4,128,128]{2,1,0:T(8,128)(2,1)} %o_hbm.1, f32[4,4,128]{2,1,0:T(4,128)} %l_hbm.1), custom_call_target="tpu_custom_call" | custom-call | tf_op jit(solution)/shard_map/pack/pallas_call | solution.py:235
  3.0 3.5 %all-to-all-start = ((bf16[4,528,128]{2,1,0:T(8,128)(2,1)}), bf16[4,528,128]{2,1,0:T(8,128)(2,1)S(1)}, u32[]{:S(2)}, u32[]{:S(2)}) async-start(bf16[4,528,128]{2,1,0:T(8,128)(2,1)} %pack.1), calls=%async_computation | async-start | bytes 1081344 | tf_op jit(solution)/shard_map/all_to_all | solution.py:254
  6.6 0.8 bias.1.bias_ref
  7.5 8.1 %all-to-all-done.got_ref = bf16[4,528,128]{2,1,0:T(8,128)(2,1)S(1)} async-done(((bf16[4,528,128]{2,1,0:T(8,128)(2,1)}), bf16[4,528,128]{2,1,0:T(8,128)(2,1)S(1)}, u32[]{:S(2)}, u32[]{:S(2)}) %all-to-all-start) | async-done | bytes 540704 | tf_op jit(solution)/shard_map/all_to_all | solution.py:254
  15.5 0.2 assemble.1
  15.7 4.5 %collective-permute-start.4 = (bf16[4,272,128]{2,1,0:T(8,128)(2,1)S(1)}, bf16[4,272,128]{2,1,0:T(8,128)(2,1)S(1)}, u32[]{:S(2)}, u32[]{:S(2)}) collective-permute-start(bf16[4,272,128]{2,1,0:T(8,128)(2,1)S(1)} %get-tuple-element.33.kv0_ref), channel_id=1, source_target_pairs={{0,2},{2,4},{4,6},{6,0},{1,3},{3,5},{5,7},{7,1},{8,10},{10,12},{12... | collective-permute-start | bytes 835592 | tf_op jit(solution)/shard_map/ppermute | solution.py:224
  20.2 3.6 %collective-permute-start.3 = (bf16[4,272,128]{2,1,0:T(8,128)(2,1)S(1)}, bf16[4,272,128]{2,1,0:T(8,128)(2,1)S(1)}, u32[]{:S(2)}, u32[]{:S(2)}) collective-permute-start(bf16[4,272,128]{2,1,0:T(8,128)(2,1)S(1)} %get-tuple-element.33.kv0_ref), channel_id=1, source_target_pairs={{0,6},{2,0},{4,2},{6,4},{1,7},{3,1},{5,3},{7,5},{8,14},{10,8},{12,... | collective-permute-start | bytes 835592 | tf_op jit(solution)/shard_map/ppermute | solution.py:224
  23.8 3.4 %collective-permute-start = (bf16[4,400,128]{2,1,0:T(8,128)(2,1)S(1)}, bf16[4,400,128]{2,1,0:T(8,128)(2,1)S(1)}, u32[]{:S(2)}, u32[]{:S(2)}) collective-permute-start(bf16[4,400,128]{2,1,0:T(8,128)(2,1)S(1)} %get-tuple-element.30), channel_id=1, source_target_pairs={{0,1},{1,0},{8,9},{9,8},{2,3},{3,2},{10,11},{11,10},{4,5},{5,4},{1... | collective-permute-start | bytes 1228808 | tf_op jit(solution)/shard_map/ppermute | solution.py:265
  27.2 4.9 %collective-permute-start.1 = (bf16[4,400,128]{2,1,0:T(8,128)(2,1)S(1)}, bf16[4,400,128]{2,1,0:T(8,128)(2,1)S(1)}, u32[]{:S(2)}, u32[]{:S(2)}) collective-permute-start(bf16[4,400,128]{2,1,0:T(8,128)(2,1)S(1)} %get-tuple-element.31), channel_id=1, source_target_pairs={{0,8},{1,9},{8,0},{9,1},{2,10},{3,11},{10,2},{11,3},{4,12},{5,13},... | collective-permute-start | bytes 1228808 | tf_op jit(solution)/shard_map/ppermute | solution.py:265
  32.1 2.4 %collective-permute-start.2 = (bf16[4,400,128]{2,1,0:T(8,128)(2,1)S(1)}, bf16[4,400,128]{2,1,0:T(8,128)(2,1)S(1)}, u32[]{:S(2)}, u32[]{:S(2)}) collective-permute-start(bf16[4,400,128]{2,1,0:T(8,128)(2,1)S(1)} %get-tuple-element.32), channel_id=1, source_target_pairs={{0,9},{1,8},{8,1},{9,0},{2,11},{3,10},{10,3},{11,2},{4,13},{5,12},... | collective-permute-start | bytes 1228808 | tf_op jit(solution)/shard_map/ppermute | solution.py:265
  34.6 0.8 collective-permute-done.4.kv3_ref
  35.4 3.2 %collective-permute-start.5 = (bf16[4,128,128]{2,1,0:T(8,128)(2,1)S(1)}, bf16[4,128,128]{2,1,0:T(8,128)(2,1)S(1)}, u32[]{:S(2)}, u32[]{:S(2)}) collective-permute-start(bf16[4,128,128]{2,1,0:T(8,128)(2,1)S(1)} %slice.8), channel_id=1, source_target_pairs={{0,2},{2,4},{4,6},{6,0},{1,3},{3,5},{5,7},{7,1},{8,10},{10,12},{12... | collective-permute-start | bytes 393224 | tf_op jit(solution)/shard_map/ppermute | solution.py:224
  38.7 4.7 %collective-permute-start.6 = (bf16[4,128,128]{2,1,0:T(8,128)(2,1)S(1)}, bf16[4,128,128]{2,1,0:T(8,128)(2,1)S(1)}, u32[]{:S(2)}, u32[]{:S(2)}) collective-permute-start(bf16[4,128,128]{2,1,0:T(8,128)(2,1)S(1)} %slice.9), channel_id=1, source_target_pairs={{0,6},{2,0},{4,2},{6,4},{1,7},{3,1},{5,3},{7,5},{8,14},{10,8},{12,... | collective-permute-start | bytes 393224 | tf_op jit(solution)/shard_map/ppermute | solution.py:224
  43.4 14.2 %collective-permute-done.5.k2_ref = bf16[4,128,128]{2,1,0:T(8,128)(2,1)S(1)} collective-permute-done((bf16[4,128,128]{2,1,0:T(8,128)(2,1)S(1)}, bf16[4,128,128]{2,1,0:T(8,128)(2,1)S(1)}, u32[]{:S(2)}, u32[]{:S(2)}) %collective-permute-start.5) | collective-permute-done | bytes 131104 | tf_op jit(solution)/shard_map/ppermute | solution.py:224
  57.6 3.8 %collective-permute-done.2.pay3_ref = bf16[4,400,128]{2,1,0:T(8,128)(2,1)S(1)} collective-permute-done((bf16[4,400,128]{2,1,0:T(8,128)(2,1)S(1)}, bf16[4,400,128]{2,1,0:T(8,128)(2,1)S(1)}, u32[]{:S(2)}, u32[]{:S(2)}) %collective-permute-start.2) | collective-permute-done | bytes 409632 | tf_op jit(solution)/shard_map/ppermute | solution.py:265
  61.3 11.7 %attend.1 = (bf16[16,128,128]{2,1,0:T(8,128)(2,1)}, bf16[4,256,128]{2,1,0:T(8,128)(2,1)S(1)}, bf16[4,256,128]{2,1,0:T(8,128)(2,1)S(1)}, bf16[4,128,128]{2,1,0:T(...) custom-call(s32[6]{0:T(128)S(1)} %stack.27.where_ref, ...), custom_call_target="tpu_custom_call" | custom-call | tf_op jit(solution)/shard_map/attend/pallas_call | solution.py:267
  73.1 10.0 %all-to-all-start.1 = ((bf16[16,128,128]{2,1,0:T(8,128)(2,1)}), bf16[16,128,128]{2,1,0:T(8,128)(2,1)S(1)}, u32[]{:S(2)}, u32[]{:S(2)}) async-start(bf16[16,128,128]{2,1,0:T(8,128)(2,1)} %get-tuple-element.40), calls=%async_computation.1 | async-start | bytes 1048576 | tf_op jit(solution)/shard_map/all_to_all | solution.py:288
  83.1 3.6 %collective-permute-start.7 = (bf16[4,128,128]{2,1,0:T(8,128)(2,1)S(1)}, bf16[4,128,128]{2,1,0:T(8,128)(2,1)S(1)}, u32[]{:S(2)}, u32[]{:S(2)}) collective-permute-start(bf16[4,128,128]{2,1,0:T(8,128)(2,1)S(1)} %get-tuple-element.35), channel_id=1, source_target_pairs={{0,2},{2,4},{4,6},{6,0},{1,3},{3,5},{5,7},{7,1},{8,10},{10,12},{12... | collective-permute-start | bytes 393224 | tf_op jit(solution)/shard_map/ppermute | solution.py:224
  86.6 4.4 %collective-permute-start.8 = (bf16[4,128,128]{2,1,0:T(8,128)(2,1)S(1)}, bf16[4,128,128]{2,1,0:T(8,128)(2,1)S(1)}, u32[]{:S(2)}, u32[]{:S(2)}) collective-permute-start(bf16[4,128,128]{2,1,0:T(8,128)(2,1)S(1)} %get-tuple-element.37), channel_id=1, source_target_pairs={{0,6},{2,0},{4,2},{6,4},{1,7},{3,1},{5,3},{7,5},{8,14},{10,8},{12,... | collective-permute-start | bytes 393224 | tf_op jit(solution)/shard_map/ppermute | solution.py:224
  91.0 1.3 collective-permute-done.7.up_more_ref
  92.4 2.4 %collective-permute-done.8.down_more_ref = bf16[4,128,128]{2,1,0:T(8,128)(2,1)S(1)} collective-permute-done((bf16[4,128,128]{2,1,0:T(8,128)(2,1)S(1)}, bf16[4,128,128]{2,1,0:T(8,128)(2,1)S(1)}, u32[]{:S(2)}, u32[]{:S(2)}) %collective-permute-start.8) | collective-permute-done | bytes 131104 | tf_op jit(solution)/shard_map/ppermute | solution.py:224
  94.8 3.4 %all-to-all-done.1 = bf16[16,128,128]{2,1,0:T(8,128)(2,1)S(1)} async-done(((bf16[16,128,128]{2,1,0:T(8,128)(2,1)}), bf16[16,128,128]{2,1,0:T(8,128)(2,1)S(1)}, u32[]{:S(2)}, u32[]{:S(2)}) %all-to-all-start.1) | async-done | bytes 524320 | tf_op jit(solution)/shard_map/all_to_all | solution.py:288
  98.2 5.7 %all-to-all-start.2 = ((bf16[16,128,128]{2,1,0:T(8,128)(2,1)}), bf16[16,128,128]{2,1,0:T(8,128)(2,1)S(1)}, u32[]{:S(2)}, u32[]{:S(2)}) async-start(bf16[16,128,128]{2,1,0:T(8,128)(2,1)} %get-tuple-element.45), calls=%async_computation.2 | async-start | bytes 1048576 | tf_op jit(solution)/shard_map/all_to_all | solution.py:293
  103.9 5.8 %collective-permute-start.9 = (bf16[4,256,128]{2,1,0:T(8,128)(2,1)S(1)}, bf16[4,256,128]{2,1,0:T(8,128)(2,1)S(1)}, u32[]{:S(2)}, u32[]{:S(2)}) collective-permute-start(bf16[4,256,128]{2,1,0:T(8,128)(2,1)S(1)} %get-tuple-element.42), channel_id=1, source_target_pairs={{0,2},{2,4},{4,6},{6,0},{1,3},{3,5},{5,7},{7,1},{8,10},{10,12},{12... | collective-permute-start | bytes 786440 | tf_op jit(solution)/shard_map/ppermute | solution.py:224
  109.8 2.1 %collective-permute-start.10 = (bf16[4,256,128]{2,1,0:T(8,128)(2,1)S(1)}, bf16[4,256,128]{2,1,0:T(8,128)(2,1)S(1)}, u32[]{:S(2)}, u32[]{:S(2)}) collective-permute-start(bf16[4,256,128]{2,1,0:T(8,128)(2,1)S(1)} %get-tuple-element.43), channel_id=1, source_target_pairs={{0,6},{2,0},{4,2},{6,4},{1,7},{3,1},{5,3},{7,5},{8,14},{10,8},{12,... | collective-permute-start | bytes 786440 | tf_op jit(solution)/shard_map/ppermute | solution.py:224
  112.0 5.3 %collective-permute-start.11 = (f32[2,128,128]{2,1,0:T(8,128)S(1)}, f32[2,128,128]{2,1,0:T(8,128)S(1)}, u32[]{:S(2)}, u32[]{:S(2)}) collective-permute-start(f32[2,128,128]{2,1,0:T(8,128)S(1)} %convert_reduce_fusion), channel_id=1, source_target_pairs={{0,0},{1,32},{32,1},{33,33},{64,64},{65,96},{96,65},{97,97},{128,1... | collective-permute-start | bytes 393224 | tf_op jit(solution)/shard_map/ppermute | solution.py:292
  117.3 12.3 %collective-permute-done.11.db_ref = f32[2,128,128]{2,1,0:T(8,128)S(1)} collective-permute-done((f32[2,128,128]{2,1,0:T(8,128)S(1)}, f32[2,128,128]{2,1,0:T(8,128)S(1)}, u32[]{:S(2)}, u32[]{:S(2)}) %collective-permute-start.11) | collective-permute-done | bytes 131104 | tf_op jit(solution)/shard_map/ppermute | solution.py:292
  129.6 0.9 join.1
  130.5 3.5 %all-to-all-start.3 = ((bf16[4,384,128]{2,1,0:T(8,128)(2,1)}), bf16[4,384,128]{2,1,0:T(8,128)(2,1)S(1)}, u32[]{:S(2)}, u32[]{:S(2)}) async-start(bf16[4,384,128]{2,1,0:T(8,128)(2,1)} %join.1), calls=%async_computation.3 | async-start | bytes 786432 | tf_op jit(solution)/shard_map/all_to_all | solution.py:303
  133.9 0.8 unpack_query.1
  134.7 6.6 %all-to-all-done.3.kv_ref = bf16[4,384,128]{2,1,0:T(8,128)(2,1)S(1)} async-done(((bf16[4,384,128]{2,1,0:T(8,128)(2,1)}), bf16[4,384,128]{2,1,0:T(8,128)(2,1)S(1)}, u32[]{:S(2)}, u32[]{:S(2)}) %all-to-all-start.3) | async-done | bytes 393248 | tf_op jit(solution)/shard_map/all_to_all | solution.py:303
  141.4 1.0 unpack.1
  (14 shorter events, 0.3 us)
Async XLA Ops:
  0.6 6.0 %copy-start = (bf16[4,128,2048]{2,1,0:T(8,128)(2,1)S(1)}, bf16[4,128,2048]{2,1,0:T(8,128)(2,1)}, u32[]{:S(2)}) copy-start(bf16[4,128,2048]{2,1,0:T(8,128)(2,1)} %bias_hbm.1) | copy-start | bytes 6291460
  3.0 12.5 %all-to-all-start = ((bf16[4,528,128]{2,1,0:T(8,128)(2,1)}), bf16[4,528,128]{2,1,0:T(8,128)(2,1)S(1)}, u32[]{:S(2)}, u32[]{:S(2)}) async-start(bf16[4,528,128]{2,1,0:T(8,128)(2,1)} %pack.1), calls=%async_computation | async-start | bytes 1081344 | tf_op jit(solution)/shard_map/all_to_all | solution.py:254
  15.7 19.7 %collective-permute-start.4 = (bf16[4,272,128]{2,1,0:T(8,128)(2,1)S(1)}, bf16[4,272,128]{2,1,0:T(8,128)(2,1)S(1)}, u32[]{:S(2)}, u32[]{:S(2)}) collective-permute-start(bf16[4,272,128]{2,1,0:T(8,128)(2,1)S(1)} %get-tuple-element.33.kv0_ref), channel_id=1, source_target_pairs={{0,2},{2,4},{4,6},{6,0},{1,3},{3,5},{5,7},{7,1},{8,10},{10,12},{12... | collective-permute-start | bytes 835592 | tf_op jit(solution)/shard_map/ppermute | solution.py:224
  20.2 18.4 %collective-permute-start.3 = (bf16[4,272,128]{2,1,0:T(8,128)(2,1)S(1)}, bf16[4,272,128]{2,1,0:T(8,128)(2,1)S(1)}, u32[]{:S(2)}, u32[]{:S(2)}) collective-permute-start(bf16[4,272,128]{2,1,0:T(8,128)(2,1)S(1)} %get-tuple-element.33.kv0_ref), channel_id=1, source_target_pairs={{0,6},{2,0},{4,2},{6,4},{1,7},{3,1},{5,3},{7,5},{8,14},{10,8},{12,... | collective-permute-start | bytes 835592 | tf_op jit(solution)/shard_map/ppermute | solution.py:224
  23.8 33.8 %collective-permute-start = (bf16[4,400,128]{2,1,0:T(8,128)(2,1)S(1)}, bf16[4,400,128]{2,1,0:T(8,128)(2,1)S(1)}, u32[]{:S(2)}, u32[]{:S(2)}) collective-permute-start(bf16[4,400,128]{2,1,0:T(8,128)(2,1)S(1)} %get-tuple-element.30), channel_id=1, source_target_pairs={{0,1},{1,0},{8,9},{9,8},{2,3},{3,2},{10,11},{11,10},{4,5},{5,4},{1... | collective-permute-start | bytes 1228808 | tf_op jit(solution)/shard_map/ppermute | solution.py:265
  27.2 30.4 %collective-permute-start.1 = (bf16[4,400,128]{2,1,0:T(8,128)(2,1)S(1)}, bf16[4,400,128]{2,1,0:T(8,128)(2,1)S(1)}, u32[]{:S(2)}, u32[]{:S(2)}) collective-permute-start(bf16[4,400,128]{2,1,0:T(8,128)(2,1)S(1)} %get-tuple-element.31), channel_id=1, source_target_pairs={{0,8},{1,9},{8,0},{9,1},{2,10},{3,11},{10,2},{11,3},{4,12},{5,13},... | collective-permute-start | bytes 1228808 | tf_op jit(solution)/shard_map/ppermute | solution.py:265
  32.1 29.2 %collective-permute-start.2 = (bf16[4,400,128]{2,1,0:T(8,128)(2,1)S(1)}, bf16[4,400,128]{2,1,0:T(8,128)(2,1)S(1)}, u32[]{:S(2)}, u32[]{:S(2)}) collective-permute-start(bf16[4,400,128]{2,1,0:T(8,128)(2,1)S(1)} %get-tuple-element.32), channel_id=1, source_target_pairs={{0,9},{1,8},{8,1},{9,0},{2,11},{3,10},{10,3},{11,2},{4,13},{5,12},... | collective-permute-start | bytes 1228808 | tf_op jit(solution)/shard_map/ppermute | solution.py:265
  35.4 22.1 %collective-permute-start.5 = (bf16[4,128,128]{2,1,0:T(8,128)(2,1)S(1)}, bf16[4,128,128]{2,1,0:T(8,128)(2,1)S(1)}, u32[]{:S(2)}, u32[]{:S(2)}) collective-permute-start(bf16[4,128,128]{2,1,0:T(8,128)(2,1)S(1)} %slice.8), channel_id=1, source_target_pairs={{0,2},{2,4},{4,6},{6,0},{1,3},{3,5},{5,7},{7,1},{8,10},{10,12},{12... | collective-permute-start | bytes 393224 | tf_op jit(solution)/shard_map/ppermute | solution.py:224
  38.7 18.9 %collective-permute-start.6 = (bf16[4,128,128]{2,1,0:T(8,128)(2,1)S(1)}, bf16[4,128,128]{2,1,0:T(8,128)(2,1)S(1)}, u32[]{:S(2)}, u32[]{:S(2)}) collective-permute-start(bf16[4,128,128]{2,1,0:T(8,128)(2,1)S(1)} %slice.9), channel_id=1, source_target_pairs={{0,6},{2,0},{4,2},{6,4},{1,7},{3,1},{5,3},{7,5},{8,14},{10,8},{12,... | collective-permute-start | bytes 393224 | tf_op jit(solution)/shard_map/ppermute | solution.py:224
  73.1 25.1 %all-to-all-start.1 = ((bf16[16,128,128]{2,1,0:T(8,128)(2,1)}), bf16[16,128,128]{2,1,0:T(8,128)(2,1)S(1)}, u32[]{:S(2)}, u32[]{:S(2)}) async-start(bf16[16,128,128]{2,1,0:T(8,128)(2,1)} %get-tuple-element.40), calls=%async_computation.1 | async-start | bytes 1048576 | tf_op jit(solution)/shard_map/all_to_all | solution.py:288
  83.1 9.3 %collective-permute-start.7 = (bf16[4,128,128]{2,1,0:T(8,128)(2,1)S(1)}, bf16[4,128,128]{2,1,0:T(8,128)(2,1)S(1)}, u32[]{:S(2)}, u32[]{:S(2)}) collective-permute-start(bf16[4,128,128]{2,1,0:T(8,128)(2,1)S(1)} %get-tuple-element.35), channel_id=1, source_target_pairs={{0,2},{2,4},{4,6},{6,0},{1,3},{3,5},{5,7},{7,1},{8,10},{10,12},{12... | collective-permute-start | bytes 393224 | tf_op jit(solution)/shard_map/ppermute | solution.py:224
  86.6 8.1 %collective-permute-start.8 = (bf16[4,128,128]{2,1,0:T(8,128)(2,1)S(1)}, bf16[4,128,128]{2,1,0:T(8,128)(2,1)S(1)}, u32[]{:S(2)}, u32[]{:S(2)}) collective-permute-start(bf16[4,128,128]{2,1,0:T(8,128)(2,1)S(1)} %get-tuple-element.37), channel_id=1, source_target_pairs={{0,6},{2,0},{4,2},{6,4},{1,7},{3,1},{5,3},{7,5},{8,14},{10,8},{12,... | collective-permute-start | bytes 393224 | tf_op jit(solution)/shard_map/ppermute | solution.py:224
  98.2 31.4 %all-to-all-start.2 = ((bf16[16,128,128]{2,1,0:T(8,128)(2,1)}), bf16[16,128,128]{2,1,0:T(8,128)(2,1)S(1)}, u32[]{:S(2)}, u32[]{:S(2)}) async-start(bf16[16,128,128]{2,1,0:T(8,128)(2,1)} %get-tuple-element.45), calls=%async_computation.2 | async-start | bytes 1048576 | tf_op jit(solution)/shard_map/all_to_all | solution.py:293
  103.9 25.6 %collective-permute-start.9 = (bf16[4,256,128]{2,1,0:T(8,128)(2,1)S(1)}, bf16[4,256,128]{2,1,0:T(8,128)(2,1)S(1)}, u32[]{:S(2)}, u32[]{:S(2)}) collective-permute-start(bf16[4,256,128]{2,1,0:T(8,128)(2,1)S(1)} %get-tuple-element.42), channel_id=1, source_target_pairs={{0,2},{2,4},{4,6},{6,0},{1,3},{3,5},{5,7},{7,1},{8,10},{10,12},{12... | collective-permute-start | bytes 786440 | tf_op jit(solution)/shard_map/ppermute | solution.py:224
  109.8 19.8 %collective-permute-start.10 = (bf16[4,256,128]{2,1,0:T(8,128)(2,1)S(1)}, bf16[4,256,128]{2,1,0:T(8,128)(2,1)S(1)}, u32[]{:S(2)}, u32[]{:S(2)}) collective-permute-start(bf16[4,256,128]{2,1,0:T(8,128)(2,1)S(1)} %get-tuple-element.43), channel_id=1, source_target_pairs={{0,6},{2,0},{4,2},{6,4},{1,7},{3,1},{5,3},{7,5},{8,14},{10,8},{12,... | collective-permute-start | bytes 786440 | tf_op jit(solution)/shard_map/ppermute | solution.py:224
  112.0 17.6 %collective-permute-start.11 = (f32[2,128,128]{2,1,0:T(8,128)S(1)}, f32[2,128,128]{2,1,0:T(8,128)S(1)}, u32[]{:S(2)}, u32[]{:S(2)}) collective-permute-start(f32[2,128,128]{2,1,0:T(8,128)S(1)} %convert_reduce_fusion), channel_id=1, source_target_pairs={{0,0},{1,32},{32,1},{33,33},{64,64},{65,96},{96,65},{97,97},{128,1... | collective-permute-start | bytes 393224 | tf_op jit(solution)/shard_map/ppermute | solution.py:292
  130.5 10.9 %all-to-all-start.3 = ((bf16[4,384,128]{2,1,0:T(8,128)(2,1)}), bf16[4,384,128]{2,1,0:T(8,128)(2,1)S(1)}, u32[]{:S(2)}, u32[]{:S(2)}) async-start(bf16[4,384,128]{2,1,0:T(8,128)(2,1)} %join.1), calls=%async_computation.3 | async-start | bytes 786432 | tf_op jit(solution)/shard_map/all_to_all | solution.py:303

commit v9 on v8

--- a/solution.py
+++ b/solution.py
@@ -10,7 +10,6 @@
 
 ROW = ("xl", "z", "c")
 BLK = ("xh", "yh", "yl")
-QUERY_GROUP = ("xl", "c", "xh", "yl")
 LOG2E = 1.4426950408889634
 AUG = 16
 F32, BF16 = jnp.float32, jnp.bfloat16
@@ -97,7 +96,10 @@
     k2_ref,
     v2_ref,
     kv3_ref,
-    dq_ref,
+    dq0_ref,
+    dq1_ref,
+    dq2_ref,
+    dq3_ref,
     dkv0_ref,
     dkv1_ref,
     dk2_ref,
@@ -109,6 +111,7 @@
 ):
     dkv_refs = (dkv0_ref, dkv1_ref, None, dkv3_ref)
     owner = [lax.rem(where_ref[5] + p, 4) for p in range(4)]
+    dq_refs = (dq0_ref, dq1_ref, dq2_ref, dq3_ref)
     pay_refs = (pay0_ref, pay1_ref, pay2_ref, pay3_ref)
     block_of = [where_ref[1 + d] for d in range(4)]
     for d in range(4):
@@ -123,7 +126,6 @@
     ]
 
     def four_rows(s, carry):
-        base = s * 4
         for i in range(4):
             first = i * 64
             q_t, g_t, extra = (
@@ -152,7 +154,7 @@
             dq = (jnp.dot(low, k_t.T, preferred_element_type=F32).T * scale).astype(BF16)
             for b in range(4):
                 block = slice(b * 128, b * 128 + 128)
-                dq_ref[base + block_of[b], i * 32 : i * 32 + 32, :] = dq[:, block]
+                dq_refs[b][s, low_at, :] = dq[:, block]
                 if b == 2:
                     dk2_ref[s, low_at, :] = dk[:, block]
                     dv2_ref[s, low_at, :] = dv[:, block]
@@ -176,8 +178,10 @@
         down_out_ref[s, 128:, :] = (down_ref[s, 128:, :].astype(F32) + down_more_ref[s].astype(F32)).astype(BF16)
 
 
-def join_kernel(own_ref, up_ref, down_ref, db_ref, out_ref):
+def join_kernel(own_ref, up_ref, down_ref, db_ref, dq0_ref, dq1_ref, dq2_ref, dq3_ref, out_ref):
     for s in range(4):
+        dq = (dq0_ref[s].astype(F32) + dq1_ref[s].astype(F32)) + (dq2_ref[s].astype(F32) + dq3_ref[s].astype(F32))
+        out_ref[s, 384:, :] = dq.astype(BF16)
         total = own_ref[s].astype(F32) + up_ref[s].astype(F32) + down_ref[s].astype(F32)
         out_ref[s, :256, :] = total.astype(BF16)
     first_half = lax.broadcasted_iota(jnp.int32, (128, 128), 1) < 64
@@ -185,27 +189,18 @@
         whole = db_ref[xl]
         high = whole.astype(BF16).astype(F32)
         low = whole - high
-        out_ref[xl * 2, 256:, :] = jnp.where(first_half, high, pltpu.roll(low, 64, 1)).astype(BF16)
-        out_ref[xl * 2 + 1, 256:, :] = jnp.where(first_half, pltpu.roll(high, 64, 1), low).astype(BF16)
-
-
-def unpack_query_kernel(q_ref, dq_ref):
-    for i in range(4):
-        heads = []
-        for h in range(4):
-            parts = [q_ref[h * 4 + a, i * 32 : i * 32 + 32, :].astype(F32) for a in range(4)]
-            heads.append(parts[0] + parts[1] + parts[2] + parts[3])
-        dq_ref[i] = jnp.concatenate(heads, axis=0).T.astype(BF16)
-
-
-def unpack_kernel(kv_ref, dk_ref, dv_ref, db_ref):
+        out_ref[xl * 2, 256:384, :] = jnp.where(first_half, high, pltpu.roll(low, 64, 1)).astype(BF16)
+        out_ref[xl * 2 + 1, 256:384, :] = jnp.where(first_half, pltpu.roll(high, 64, 1), low).astype(BF16)
+
+
+def unpack_kernel(got_ref, dq_ref, dk_ref, dv_ref, db_ref):
     for h in range(4):
-        parts = kv_ref[h, 256:, :].astype(F32)
+        parts = got_ref[h, 256:384, :].astype(F32)
         db_ref[h] = (parts + pltpu.roll(parts, 64, 1)).T[:64]
     for i in range(4):
-        for first, out in ((0, dk_ref), (128, dv_ref)):
+        for first, out in ((0, dk_ref), (128, dv_ref), (384, dq_ref)):
             at = i * 32 + first
-            out[i] = turned(jnp.concatenate([kv_ref[h, at : at + 32, :] for h in range(4)], axis=0))
+            out[i] = turned(jnp.concatenate([got_ref[h, at : at + 32, :] for h in range(4)], axis=0))
 
 
 def vmem(n=1):
@@ -264,14 +259,14 @@
     for d in range(1, 4):
         pays[d] = lax.ppermute(pays[d], ("xh", "yl"), [(n, n ^ d) for n in range(4)])
     k_far, v_far = along(before[:, :128], 1), along(after[:, 128:256], -1)
-    dq_parts, own, up, dk_far, dv_far, down, db_parts = pl.pallas_call(
+    *dq_parts, own, up, dk_far, dv_far, down, db_parts = pl.pallas_call(
         functools.partial(attend_kernel, scale),
-        out_shape=(shape(16, 128, 128),)
+        out_shape=(shape(4, 128, 128),) * 4
         + (shape(4, 256, 128),) * 2
         + (shape(4, 128, 128),) * 2
         + (shape(4, 256, 128), shape(16, 128, 128)),
         in_specs=[smem] + vmem(9),
-        out_specs=tuple(vmem(7)),
+        out_specs=tuple(vmem(10)),
         scratch_shapes=[pltpu.VMEM((512, 512), F32), pltpu.VMEM((512, 512), F32)],
         compiler_params=params(),
         name="attend",
@@ -286,34 +281,26 @@
         name="fold",
     )(up, up_more, down, down_more)
     db = lax.all_to_all(db_parts, ("z", "xh"), 0, 0)
+    for d in range(1, 4):
+        dq_parts[d] = lax.ppermute(dq_parts[d], ("xh", "yl"), [(n, n ^ d) for n in range(4)])
     up, down, db, dq_parts = lax.optimization_barrier((up, down, db, dq_parts))
     up, down = along(up, 1), along(down, -1)
     db = jnp.sum(db.reshape(8, 2, 128, 128).astype(F32), axis=0)
     db = lax.ppermute(db, ("z", "yl"), swaps())
-    dq = lax.all_to_all(dq_parts, QUERY_GROUP, 0, 0)
-    up, down, db, dq = lax.optimization_barrier((up, down, db, dq))
     joined = pl.pallas_call(
         join_kernel,
-        out_shape=shape(4, 384, 128),
-        in_specs=vmem(4),
+        out_shape=shape(4, 512, 128),
+        in_specs=vmem(8),
         out_specs=vmem()[0],
         compiler_params=params(),
         name="join",
-    )(own, up, down, db)
+    )(own, up, down, db, *dq_parts)
     joined = lax.all_to_all(joined, ("xl", "c"), 0, 0)
-    query_grad = pl.pallas_call(
-        unpack_query_kernel,
-        out_shape=shape(4, 128, 128),
+    query_grad, key_grad, value_grad, bias_grad = pl.pallas_call(
+        unpack_kernel,
+        out_shape=(shape(4, 128, 128),) * 3 + (jax.ShapeDtypeStruct((4, 64, 128), F32),),
         in_specs=vmem(1),
-        out_specs=vmem()[0],
-        compiler_params=params(),
-        name="unpack_query",
-    )(dq)
-    key_grad, value_grad, bias_grad = pl.pallas_call(
-        unpack_kernel,
-        out_shape=(shape(4, 128, 128),) * 2 + (jax.ShapeDtypeStruct((4, 64, 128), F32),),
-        in_specs=vmem(1),
-        out_specs=tuple(vmem(3)),
+        out_specs=tuple(vmem(4)),
         compiler_params=params(),
         name="unpack",
     )(joined)

time: 143 us -> 143 us (level)
  blocking collectives: 0 us -> 11.2 us
  waiting for transfers between devices: 52.8 us -> 43.5 us
  Pallas kernels: 17.9 us -> 16.4 us
    ppermute x0 -> x3, starting transfers between devices: none -> 11.9 us  [body(): lax.ppermute(dq_parts[d], ('xh', 'yl'), [(n, n ^ d) for n in range(4)])]
    all_to_all x0 -> x1, blocking collectives: none -> 11.2 us  [body(): joined = lax.all_to_all(joined, ('xl', 'c'), 0, 0)]
    all_to_all x2 -> x0, starting transfers between devices: 9.18 us -> none  [the longest x1 5.72 us: body(): dq = lax.all_to_all(dq_parts, QUERY_GROUP, 0, 0)]
    ppermute x0 -> x3, waiting for transfers between devices: none -> 7.24 us  [body(): lax.ppermute(dq_parts[d], ('xh', 'yl'), [(n, n ^ d) for n in range(4)])]
    all_to_all x2 -> x0, waiting for transfers between devices: 6.62 us -> none  [the longest x1 6.61 us: body(): joined = lax.all_to_all(joined, ('xl', 'c'), 0, 0)]
    ppermute x8, waiting for transfers between devices: 18.7 us -> 15 us  [along(): return lax.ppermute(value, 'yh', [(n, (n + steps) % 4) for n in range(4)])]
    all_to_all x1, waiting for transfers between devices: 3.37 us -> 0.01 us  [body(): db = lax.all_to_all(db_parts, ('z', 'xh'), 0, 0)]
    ppermute x1, starting transfers between devices: 5.29 us -> 1.92 us  [body(): db = lax.ppermute(db, ('z', 'yl'), swaps())]
  transfers between devices with their start and end apart: 16 -> 17, of which waited for: 9 -> 7; matrix products, arithmetic and copies ran while one was open for 0% -> 0% of each run, Pallas kernels for 1% -> 1%
where the time goes in v9:
time: 143 us; the launch traced here: 142 us
  starting transfers between devices  69.9 us (49%)
  waiting for transfers between devices  43.5 us (30%)
  Pallas kernels  16.4 us (11%)
  blocking collectives  11.2 us (8%)
    ppermute x8, starting transfers between devices, along(): return lax.ppermute(value, 'yh', [(n, (n + steps) % 4) for n in range(4)])  31.9 us
    ppermute x8, waiting for transfers between devices, along(): return lax.ppermute(value, 'yh', [(n, (n + steps) % 4) for n in range(4)])  15 us
    ppermute x3, starting transfers between devices, body(): lax.ppermute(dq_parts[d], ('xh', 'yl'), [(n, n ^ d) for n in range(4)])  11.9 us
    pallas_call x1, Pallas kernels, body(): pl.pallas_call(functools.partial(attend_kernel, scale), out_shape=(shape(...  11.6 us
    all_to_all x1, blocking collectives, body(): joined = lax.all_to_all(joined, ('xl', 'c'), 0, 0)  11.2 us
    ppermute x3, starting transfers between devices, body(): lax.ppermute(pays[d], ('xh', 'yl'), [(n, n ^ d) for n in range(4)])  10.7 us
    all_to_all x1, starting transfers between devices, body(): db = lax.all_to_all(db_parts, ('z', 'xh'), 0, 0)  9.98 us
    ppermute x1, waiting for transfers between devices, body(): db = lax.ppermute(db, ('z', 'yl'), swaps())  9.47 us
  transfers between devices with their start and end apart: 17, of which 7 were waited for; matrix products, arithmetic and copies ran while one was open for 0% of the time, Pallas kernels for 1%

profile of v9, /device:TPU:64, one launch (start us, length us, event | category | flops | bytes accessed | tf_op | source)
XLA Modules:
  0.0 142.1 jit_solution(17472418661994642768)
XLA Ops:
  0.6 2.4 %pack.1 = bf16[4,528,128]{2,1,0:T(8,128)(2,1)} custom-call(bf16[4,128,128]{2,1,0:T(8,128)(2,1)} %k_hbm.1, bf16[4,128,128]{2,1,0:T(8,128)(2,1)} %v_hbm.1, bf16[4,128,128]{2,1,0:T(8,128)(2,1)} %q_hbm.1, bf16[4,128,128]{2,1,0:T(8,128)(2,1)} %g_hbm.1, bf16[4,128,128]{2,1,0:T(8,128)(2,1)} %o_hbm.1, f32[4,4,128]{2,1,0:T(4,128)} %l_hbm.1), custom_call_target="tpu_custom_call" | custom-call | tf_op jit(solution)/shard_map/pack/pallas_call | solution.py:230
  3.0 3.5 %all-to-all-start = ((bf16[4,528,128]{2,1,0:T(8,128)(2,1)}), bf16[4,528,128]{2,1,0:T(8,128)(2,1)S(1)}, u32[]{:S(2)}, u32[]{:S(2)}) async-start(bf16[4,528,128]{2,1,0:T(8,128)(2,1)} %pack.1), calls=%async_computation | async-start | bytes 1081344 | tf_op jit(solution)/shard_map/all_to_all | solution.py:249
  6.5 0.1 stack.27.where_ref
  6.6 0.8 bias.1.bias_ref
  7.5 8.1 %all-to-all-done.got_ref = bf16[4,528,128]{2,1,0:T(8,128)(2,1)S(1)} async-done(((bf16[4,528,128]{2,1,0:T(8,128)(2,1)}), bf16[4,528,128]{2,1,0:T(8,128)(2,1)S(1)}, u32[]{:S(2)}, u32[]{:S(2)}) %all-to-all-start) | async-done | bytes 540704 | tf_op jit(solution)/shard_map/all_to_all | solution.py:249
  15.5 0.2 assemble.1
  15.7 4.5 %collective-permute-start.4 = (bf16[4,272,128]{2,1,0:T(8,128)(2,1)S(1)}, bf16[4,272,128]{2,1,0:T(8,128)(2,1)S(1)}, u32[]{:S(2)}, u32[]{:S(2)}) collective-permute-start(bf16[4,272,128]{2,1,0:T(8,128)(2,1)S(1)} %get-tuple-element.36.kv0_ref), channel_id=1, source_target_pairs={{0,2},{2,4},{4,6},{6,0},{1,3},{3,5},{5,7},{7,1},{8,10},{10,12},{12... | collective-permute-start | bytes 835592 | tf_op jit(solution)/shard_map/ppermute | solution.py:219
  20.2 3.6 %collective-permute-start.3 = (bf16[4,272,128]{2,1,0:T(8,128)(2,1)S(1)}, bf16[4,272,128]{2,1,0:T(8,128)(2,1)S(1)}, u32[]{:S(2)}, u32[]{:S(2)}) collective-permute-start(bf16[4,272,128]{2,1,0:T(8,128)(2,1)S(1)} %get-tuple-element.36.kv0_ref), channel_id=1, source_target_pairs={{0,6},{2,0},{4,2},{6,4},{1,7},{3,1},{5,3},{7,5},{8,14},{10,8},{12,... | collective-permute-start | bytes 835592 | tf_op jit(solution)/shard_map/ppermute | solution.py:219
  23.8 3.4 %collective-permute-start = (bf16[4,400,128]{2,1,0:T(8,128)(2,1)S(1)}, bf16[4,400,128]{2,1,0:T(8,128)(2,1)S(1)}, u32[]{:S(2)}, u32[]{:S(2)}) collective-permute-start(bf16[4,400,128]{2,1,0:T(8,128)(2,1)S(1)} %get-tuple-element.33), channel_id=1, source_target_pairs={{0,1},{1,0},{8,9},{9,8},{2,3},{3,2},{10,11},{11,10},{4,5},{5,4},{1... | collective-permute-start | bytes 1228808 | tf_op jit(solution)/shard_map/ppermute | solution.py:260
  27.2 4.9 %collective-permute-start.1 = (bf16[4,400,128]{2,1,0:T(8,128)(2,1)S(1)}, bf16[4,400,128]{2,1,0:T(8,128)(2,1)S(1)}, u32[]{:S(2)}, u32[]{:S(2)}) collective-permute-start(bf16[4,400,128]{2,1,0:T(8,128)(2,1)S(1)} %get-tuple-element.34), channel_id=1, source_target_pairs={{0,8},{1,9},{8,0},{9,1},{2,10},{3,11},{10,2},{11,3},{4,12},{5,13},... | collective-permute-start | bytes 1228808 | tf_op jit(solution)/shard_map/ppermute | solution.py:260
  32.1 2.4 %collective-permute-start.2 = (bf16[4,400,128]{2,1,0:T(8,128)(2,1)S(1)}, bf16[4,400,128]{2,1,0:T(8,128)(2,1)S(1)}, u32[]{:S(2)}, u32[]{:S(2)}) collective-permute-start(bf16[4,400,128]{2,1,0:T(8,128)(2,1)S(1)} %get-tuple-element.35), channel_id=1, source_target_pairs={{0,9},{1,8},{8,1},{9,0},{2,11},{3,10},{10,3},{11,2},{4,13},{5,12},... | collective-permute-start | bytes 1228808 | tf_op jit(solution)/shard_map/ppermute | solution.py:260
  34.6 0.8 collective-permute-done.4.kv3_ref
  35.4 3.2 %collective-permute-start.5 = (bf16[4,128,128]{2,1,0:T(8,128)(2,1)S(1)}, bf16[4,128,128]{2,1,0:T(8,128)(2,1)S(1)}, u32[]{:S(2)}, u32[]{:S(2)}) collective-permute-start(bf16[4,128,128]{2,1,0:T(8,128)(2,1)S(1)} %slice.8), channel_id=1, source_target_pairs={{0,2},{2,4},{4,6},{6,0},{1,3},{3,5},{5,7},{7,1},{8,10},{10,12},{12... | collective-permute-start | bytes 393224 | tf_op jit(solution)/shard_map/ppermute | solution.py:219
  38.7 4.7 %collective-permute-start.6 = (bf16[4,128,128]{2,1,0:T(8,128)(2,1)S(1)}, bf16[4,128,128]{2,1,0:T(8,128)(2,1)S(1)}, u32[]{:S(2)}, u32[]{:S(2)}) collective-permute-start(bf16[4,128,128]{2,1,0:T(8,128)(2,1)S(1)} %slice.9), channel_id=1, source_target_pairs={{0,6},{2,0},{4,2},{6,4},{1,7},{3,1},{5,3},{7,5},{8,14},{10,8},{12,... | collective-permute-start | bytes 393224 | tf_op jit(solution)/shard_map/ppermute | solution.py:219
  43.4 14.2 %collective-permute-done.5.k2_ref = bf16[4,128,128]{2,1,0:T(8,128)(2,1)S(1)} collective-permute-done((bf16[4,128,128]{2,1,0:T(8,128)(2,1)S(1)}, bf16[4,128,128]{2,1,0:T(8,128)(2,1)S(1)}, u32[]{:S(2)}, u32[]{:S(2)}) %collective-permute-start.5) | collective-permute-done | bytes 131104 | tf_op jit(solution)/shard_map/ppermute | solution.py:219
  57.6 3.8 %collective-permute-done.2.pay3_ref = bf16[4,400,128]{2,1,0:T(8,128)(2,1)S(1)} collective-permute-done((bf16[4,400,128]{2,1,0:T(8,128)(2,1)S(1)}, bf16[4,400,128]{2,1,0:T(8,128)(2,1)S(1)}, u32[]{:S(2)}, u32[]{:S(2)}) %collective-permute-start.2) | collective-permute-done | bytes 409632 | tf_op jit(solution)/shard_map/ppermute | solution.py:260
  61.3 11.6 %attend.1 = (bf16[4,128,128]{2,1,0:T(8,128)(2,1)S(1)}, bf16[4,128,128]{2,1,0:T(8,128)(2,1)S(1)}, bf16[4,128,128]{2,1,0:T(8,128)(2,1)S(1)}, bf16[4,128,128]{2,1,0...) custom-call(s32[6]{0:T(128)S(1)} %stack.27.where_ref, ...), custom_call_target="tpu_custom_call" | custom-call | tf_op jit(solution)/shard_map/attend/pallas_call | solution.py:262
  72.9 10.0 %all-to-all-start.1 = ((bf16[16,128,128]{2,1,0:T(8,128)(2,1)}), bf16[16,128,128]{2,1,0:T(8,128)(2,1)S(1)}, u32[]{:S(2)}, u32[]{:S(2)}) async-start(bf16[16,128,128]{2,1,0:T(8,128)(2,1)} %get-tuple-element.44), calls=%async_computation.1 | async-start | bytes 1048576 | tf_op jit(solution)/shard_map/all_to_all | solution.py:283
  82.9 3.5 %collective-permute-start.7 = (bf16[4,128,128]{2,1,0:T(8,128)(2,1)S(1)}, bf16[4,128,128]{2,1,0:T(8,128)(2,1)S(1)}, u32[]{:S(2)}, u32[]{:S(2)}) collective-permute-start(bf16[4,128,128]{2,1,0:T(8,128)(2,1)S(1)} %get-tuple-element.39), channel_id=1, source_target_pairs={{0,2},{2,4},{4,6},{6,0},{1,3},{3,5},{5,7},{7,1},{8,10},{10,12},{12... | collective-permute-start | bytes 393224 | tf_op jit(solution)/shard_map/ppermute | solution.py:219
  86.5 4.4 %collective-permute-start.8 = (bf16[4,128,128]{2,1,0:T(8,128)(2,1)S(1)}, bf16[4,128,128]{2,1,0:T(8,128)(2,1)S(1)}, u32[]{:S(2)}, u32[]{:S(2)}) collective-permute-start(bf16[4,128,128]{2,1,0:T(8,128)(2,1)S(1)} %get-tuple-element.41), channel_id=1, source_target_pairs={{0,6},{2,0},{4,2},{6,4},{1,7},{3,1},{5,3},{7,5},{8,14},{10,8},{12,... | collective-permute-start | bytes 393224 | tf_op jit(solution)/shard_map/ppermute | solution.py:219
  90.9 5.1 %collective-permute-start.9 = (bf16[4,128,128]{2,1,0:T(8,128)(2,1)S(1)}, bf16[4,128,128]{2,1,0:T(8,128)(2,1)S(1)}, u32[]{:S(2)}, u32[]{:S(2)}) collective-permute-start(bf16[4,128,128]{2,1,0:T(8,128)(2,1)S(1)} %get-tuple-element.46), channel_id=1, source_target_pairs={{0,1},{1,0},{8,9},{9,8},{2,3},{3,2},{10,11},{11,10},{4,5},{5,4},{1... | collective-permute-start | bytes 393224 | tf_op jit(solution)/shard_map/ppermute | solution.py:285
  96.0 4.9 %collective-permute-start.10 = (bf16[4,128,128]{2,1,0:T(8,128)(2,1)S(1)}, bf16[4,128,128]{2,1,0:T(8,128)(2,1)S(1)}, u32[]{:S(2)}, u32[]{:S(2)}) collective-permute-start(bf16[4,128,128]{2,1,0:T(8,128)(2,1)S(1)} %get-tuple-element.47), channel_id=1, source_target_pairs={{0,8},{1,9},{8,0},{9,1},{2,10},{3,11},{10,2},{11,3},{4,12},{5,13},... | collective-permute-start | bytes 393224 | tf_op jit(solution)/shard_map/ppermute | solution.py:285
  100.8 1.9 %collective-permute-start.11 = (bf16[4,128,128]{2,1,0:T(8,128)(2,1)S(1)}, bf16[4,128,128]{2,1,0:T(8,128)(2,1)S(1)}, u32[]{:S(2)}, u32[]{:S(2)}) collective-permute-start(bf16[4,128,128]{2,1,0:T(8,128)(2,1)S(1)} %get-tuple-element.48), channel_id=1, source_target_pairs={{0,9},{1,8},{8,1},{9,0},{2,11},{3,10},{10,3},{11,2},{4,13},{5,12},... | collective-permute-start | bytes 393224 | tf_op jit(solution)/shard_map/ppermute | solution.py:285
  102.9 1.5 %collective-permute-done.10.dq2_ref = bf16[4,128,128]{2,1,0:T(8,128)(2,1)S(1)} collective-permute-done((bf16[4,128,128]{2,1,0:T(8,128)(2,1)S(1)}, bf16[4,128,128]{2,1,0:T(8,128)(2,1)S(1)}, u32[]{:S(2)}, u32[]{:S(2)}) %collective-permute-start.10) | collective-permute-done | bytes 131104 | tf_op jit(solution)/shard_map/ppermute | solution.py:285
  104.3 5.8 %collective-permute-done.11.dq3_ref = bf16[4,128,128]{2,1,0:T(8,128)(2,1)S(1)} collective-permute-done((bf16[4,128,128]{2,1,0:T(8,128)(2,1)S(1)}, bf16[4,128,128]{2,1,0:T(8,128)(2,1)S(1)}, u32[]{:S(2)}, u32[]{:S(2)}) %collective-permute-start.11) | collective-permute-done | bytes 131104 | tf_op jit(solution)/shard_map/ppermute | solution.py:285
  110.1 4.2 %collective-permute-start.12 = (bf16[4,256,128]{2,1,0:T(8,128)(2,1)S(1)}, bf16[4,256,128]{2,1,0:T(8,128)(2,1)S(1)}, u32[]{:S(2)}, u32[]{:S(2)}) collective-permute-start(bf16[4,256,128]{2,1,0:T(8,128)(2,1)S(1)} %get-tuple-element.49), channel_id=1, source_target_pairs={{0,2},{2,4},{4,6},{6,0},{1,3},{3,5},{5,7},{7,1},{8,10},{10,12},{12... | collective-permute-start | bytes 786440 | tf_op jit(solution)/shard_map/ppermute | solution.py:219
  114.4 3.7 %collective-permute-start.13 = (bf16[4,256,128]{2,1,0:T(8,128)(2,1)S(1)}, bf16[4,256,128]{2,1,0:T(8,128)(2,1)S(1)}, u32[]{:S(2)}, u32[]{:S(2)}) collective-permute-start(bf16[4,256,128]{2,1,0:T(8,128)(2,1)S(1)} %get-tuple-element.50), channel_id=1, source_target_pairs={{0,6},{2,0},{4,2},{6,4},{1,7},{3,1},{5,3},{7,5},{8,14},{10,8},{12,... | collective-permute-start | bytes 786440 | tf_op jit(solution)/shard_map/ppermute | solution.py:219
  118.1 1.9 %collective-permute-start.14 = (f32[2,128,128]{2,1,0:T(8,128)S(1)}, f32[2,128,128]{2,1,0:T(8,128)S(1)}, u32[]{:S(2)}, u32[]{:S(2)}) collective-permute-start(f32[2,128,128]{2,1,0:T(8,128)S(1)} %convert_reduce_fusion), channel_id=1, source_target_pairs={{0,0},{1,32},{32,1},{33,33},{64,64},{65,96},{96,65},{97,97},{128,1... | collective-permute-start | bytes 393224 | tf_op jit(solution)/shard_map/ppermute | solution.py:289
  120.1 9.5 %collective-permute-done.14.db_ref = f32[2,128,128]{2,1,0:T(8,128)S(1)} collective-permute-done((f32[2,128,128]{2,1,0:T(8,128)S(1)}, f32[2,128,128]{2,1,0:T(8,128)S(1)}, u32[]{:S(2)}, u32[]{:S(2)}) %collective-permute-start.14) | collective-permute-done | bytes 131104 | tf_op jit(solution)/shard_map/ppermute | solution.py:289
  129.5 0.2 join.1
  129.8 11.2 %all_to_all.15.got_ref = bf16[4,512,128]{2,1,0:T(8,128)(2,1)S(1)} all-to-all(bf16[4,512,128]{2,1,0:T(8,128)(2,1)S(1)} %join.1), channel_id=1, replica_groups=mesh['xl'=2,'z'=8,'c'=2,'xh'=2,'yh'=4,'yl'=2] {'xl','c'}, dimensions={0} | all-to-all | bytes 1048576 | tf_op jit(solution)/shard_map/all_to_all | solution.py:298
  141.0 1.1 unpack.1
  (16 shorter events, 0.2 us)
Async XLA Ops:
  0.6 6.0 %copy-start = (bf16[4,128,2048]{2,1,0:T(8,128)(2,1)S(1)}, bf16[4,128,2048]{2,1,0:T(8,128)(2,1)}, u32[]{:S(2)}) copy-start(bf16[4,128,2048]{2,1,0:T(8,128)(2,1)} %bias_hbm.1) | copy-start | bytes 6291460
  3.0 12.5 %all-to-all-start = ((bf16[4,528,128]{2,1,0:T(8,128)(2,1)}), bf16[4,528,128]{2,1,0:T(8,128)(2,1)S(1)}, u32[]{:S(2)}, u32[]{:S(2)}) async-start(bf16[4,528,128]{2,1,0:T(8,128)(2,1)} %pack.1), calls=%async_computation | async-start | bytes 1081344 | tf_op jit(solution)/shard_map/all_to_all | solution.py:249
  15.7 19.7 %collective-permute-start.4 = (bf16[4,272,128]{2,1,0:T(8,128)(2,1)S(1)}, bf16[4,272,128]{2,1,0:T(8,128)(2,1)S(1)}, u32[]{:S(2)}, u32[]{:S(2)}) collective-permute-start(bf16[4,272,128]{2,1,0:T(8,128)(2,1)S(1)} %get-tuple-element.36.kv0_ref), channel_id=1, source_target_pairs={{0,2},{2,4},{4,6},{6,0},{1,3},{3,5},{5,7},{7,1},{8,10},{10,12},{12... | collective-permute-start | bytes 835592 | tf_op jit(solution)/shard_map/ppermute | solution.py:219
  20.2 18.4 %collective-permute-start.3 = (bf16[4,272,128]{2,1,0:T(8,128)(2,1)S(1)}, bf16[4,272,128]{2,1,0:T(8,128)(2,1)S(1)}, u32[]{:S(2)}, u32[]{:S(2)}) collective-permute-start(bf16[4,272,128]{2,1,0:T(8,128)(2,1)S(1)} %get-tuple-element.36.kv0_ref), channel_id=1, source_target_pairs={{0,6},{2,0},{4,2},{6,4},{1,7},{3,1},{5,3},{7,5},{8,14},{10,8},{12,... | collective-permute-start | bytes 835592 | tf_op jit(solution)/shard_map/ppermute | solution.py:219
  23.8 33.8 %collective-permute-start = (bf16[4,400,128]{2,1,0:T(8,128)(2,1)S(1)}, bf16[4,400,128]{2,1,0:T(8,128)(2,1)S(1)}, u32[]{:S(2)}, u32[]{:S(2)}) collective-permute-start(bf16[4,400,128]{2,1,0:T(8,128)(2,1)S(1)} %get-tuple-element.33), channel_id=1, source_target_pairs={{0,1},{1,0},{8,9},{9,8},{2,3},{3,2},{10,11},{11,10},{4,5},{5,4},{1... | collective-permute-start | bytes 1228808 | tf_op jit(solution)/shard_map/ppermute | solution.py:260
  27.2 30.4 %collective-permute-start.1 = (bf16[4,400,128]{2,1,0:T(8,128)(2,1)S(1)}, bf16[4,400,128]{2,1,0:T(8,128)(2,1)S(1)}, u32[]{:S(2)}, u32[]{:S(2)}) collective-permute-start(bf16[4,400,128]{2,1,0:T(8,128)(2,1)S(1)} %get-tuple-element.34), channel_id=1, source_target_pairs={{0,8},{1,9},{8,0},{9,1},{2,10},{3,11},{10,2},{11,3},{4,12},{5,13},... | collective-permute-start | bytes 1228808 | tf_op jit(solution)/shard_map/ppermute | solution.py:260
  32.1 29.2 %collective-permute-start.2 = (bf16[4,400,128]{2,1,0:T(8,128)(2,1)S(1)}, bf16[4,400,128]{2,1,0:T(8,128)(2,1)S(1)}, u32[]{:S(2)}, u32[]{:S(2)}) collective-permute-start(bf16[4,400,128]{2,1,0:T(8,128)(2,1)S(1)} %get-tuple-element.35), channel_id=1, source_target_pairs={{0,9},{1,8},{8,1},{9,0},{2,11},{3,10},{10,3},{11,2},{4,13},{5,12},... | collective-permute-start | bytes 1228808 | tf_op jit(solution)/shard_map/ppermute | solution.py:260
  35.4 22.1 %collective-permute-start.5 = (bf16[4,128,128]{2,1,0:T(8,128)(2,1)S(1)}, bf16[4,128,128]{2,1,0:T(8,128)(2,1)S(1)}, u32[]{:S(2)}, u32[]{:S(2)}) collective-permute-start(bf16[4,128,128]{2,1,0:T(8,128)(2,1)S(1)} %slice.8), channel_id=1, source_target_pairs={{0,2},{2,4},{4,6},{6,0},{1,3},{3,5},{5,7},{7,1},{8,10},{10,12},{12... | collective-permute-start | bytes 393224 | tf_op jit(solution)/shard_map/ppermute | solution.py:219
  38.7 18.9 %collective-permute-start.6 = (bf16[4,128,128]{2,1,0:T(8,128)(2,1)S(1)}, bf16[4,128,128]{2,1,0:T(8,128)(2,1)S(1)}, u32[]{:S(2)}, u32[]{:S(2)}) collective-permute-start(bf16[4,128,128]{2,1,0:T(8,128)(2,1)S(1)} %slice.9), channel_id=1, source_target_pairs={{0,6},{2,0},{4,2},{6,4},{1,7},{3,1},{5,3},{7,5},{8,14},{10,8},{12,... | collective-permute-start | bytes 393224 | tf_op jit(solution)/shard_map/ppermute | solution.py:219
  72.9 37.2 %all-to-all-start.1 = ((bf16[16,128,128]{2,1,0:T(8,128)(2,1)}), bf16[16,128,128]{2,1,0:T(8,128)(2,1)S(1)}, u32[]{:S(2)}, u32[]{:S(2)}) async-start(bf16[16,128,128]{2,1,0:T(8,128)(2,1)} %get-tuple-element.44), calls=%async_computation.1 | async-start | bytes 1048576 | tf_op jit(solution)/shard_map/all_to_all | solution.py:283
  82.9 19.8 %collective-permute-start.7 = (bf16[4,128,128]{2,1,0:T(8,128)(2,1)S(1)}, bf16[4,128,128]{2,1,0:T(8,128)(2,1)S(1)}, u32[]{:S(2)}, u32[]{:S(2)}) collective-permute-start(bf16[4,128,128]{2,1,0:T(8,128)(2,1)S(1)} %get-tuple-element.39), channel_id=1, source_target_pairs={{0,2},{2,4},{4,6},{6,0},{1,3},{3,5},{5,7},{7,1},{8,10},{10,12},{12... | collective-permute-start | bytes 393224 | tf_op jit(solution)/shard_map/ppermute | solution.py:219
  86.5 16.3 %collective-permute-start.8 = (bf16[4,128,128]{2,1,0:T(8,128)(2,1)S(1)}, bf16[4,128,128]{2,1,0:T(8,128)(2,1)S(1)}, u32[]{:S(2)}, u32[]{:S(2)}) collective-permute-start(bf16[4,128,128]{2,1,0:T(8,128)(2,1)S(1)} %get-tuple-element.41), channel_id=1, source_target_pairs={{0,6},{2,0},{4,2},{6,4},{1,7},{3,1},{5,3},{7,5},{8,14},{10,8},{12,... | collective-permute-start | bytes 393224 | tf_op jit(solution)/shard_map/ppermute | solution.py:219
  90.9 12.0 %collective-permute-start.9 = (bf16[4,128,128]{2,1,0:T(8,128)(2,1)S(1)}, bf16[4,128,128]{2,1,0:T(8,128)(2,1)S(1)}, u32[]{:S(2)}, u32[]{:S(2)}) collective-permute-start(bf16[4,128,128]{2,1,0:T(8,128)(2,1)S(1)} %get-tuple-element.46), channel_id=1, source_target_pairs={{0,1},{1,0},{8,9},{9,8},{2,3},{3,2},{10,11},{11,10},{4,5},{5,4},{1... | collective-permute-start | bytes 393224 | tf_op jit(solution)/shard_map/ppermute | solution.py:285
  96.0 8.4 %collective-permute-start.10 = (bf16[4,128,128]{2,1,0:T(8,128)(2,1)S(1)}, bf16[4,128,128]{2,1,0:T(8,128)(2,1)S(1)}, u32[]{:S(2)}, u32[]{:S(2)}) collective-permute-start(bf16[4,128,128]{2,1,0:T(8,128)(2,1)S(1)} %get-tuple-element.47), channel_id=1, source_target_pairs={{0,8},{1,9},{8,0},{9,1},{2,10},{3,11},{10,2},{11,3},{4,12},{5,13},... | collective-permute-start | bytes 393224 | tf_op jit(solution)/shard_map/ppermute | solution.py:285
  100.8 9.3 %collective-permute-start.11 = (bf16[4,128,128]{2,1,0:T(8,128)(2,1)S(1)}, bf16[4,128,128]{2,1,0:T(8,128)(2,1)S(1)}, u32[]{:S(2)}, u32[]{:S(2)}) collective-permute-start(bf16[4,128,128]{2,1,0:T(8,128)(2,1)S(1)} %get-tuple-element.48), channel_id=1, source_target_pairs={{0,9},{1,8},{8,1},{9,0},{2,11},{3,10},{10,3},{11,2},{4,13},{5,12},... | collective-permute-start | bytes 393224 | tf_op jit(solution)/shard_map/ppermute | solution.py:285
  110.1 19.4 %collective-permute-start.12 = (bf16[4,256,128]{2,1,0:T(8,128)(2,1)S(1)}, bf16[4,256,128]{2,1,0:T(8,128)(2,1)S(1)}, u32[]{:S(2)}, u32[]{:S(2)}) collective-permute-start(bf16[4,256,128]{2,1,0:T(8,128)(2,1)S(1)} %get-tuple-element.49), channel_id=1, source_target_pairs={{0,2},{2,4},{4,6},{6,0},{1,3},{3,5},{5,7},{7,1},{8,10},{10,12},{12... | collective-permute-start | bytes 786440 | tf_op jit(solution)/shard_map/ppermute | solution.py:219
  114.4 15.2 %collective-permute-start.13 = (bf16[4,256,128]{2,1,0:T(8,128)(2,1)S(1)}, bf16[4,256,128]{2,1,0:T(8,128)(2,1)S(1)}, u32[]{:S(2)}, u32[]{:S(2)}) collective-permute-start(bf16[4,256,128]{2,1,0:T(8,128)(2,1)S(1)} %get-tuple-element.50), channel_id=1, source_target_pairs={{0,6},{2,0},{4,2},{6,4},{1,7},{3,1},{5,3},{7,5},{8,14},{10,8},{12,... | collective-permute-start | bytes 786440 | tf_op jit(solution)/shard_map/ppermute | solution.py:219
  118.1 11.4 %collective-permute-start.14 = (f32[2,128,128]{2,1,0:T(8,128)S(1)}, f32[2,128,128]{2,1,0:T(8,128)S(1)}, u32[]{:S(2)}, u32[]{:S(2)}) collective-permute-start(f32[2,128,128]{2,1,0:T(8,128)S(1)} %convert_reduce_fusion), channel_id=1, source_target_pairs={{0,0},{1,32},{32,1},{33,33},{64,64},{65,96},{96,65},{97,97},{128,1... | collective-permute-start | bytes 393224 | tf_op jit(solution)/shard_map/ppermute | solution.py:289

commit v10 on v9

--- a/solution.py
+++ b/solution.py
@@ -281,9 +281,11 @@
         name="fold",
     )(up, up_more, down, down_more)
     db = lax.all_to_all(db_parts, ("z", "xh"), 0, 0)
-    for d in range(1, 4):
+    for d in (3,):
         dq_parts[d] = lax.ppermute(dq_parts[d], ("xh", "yl"), [(n, n ^ d) for n in range(4)])
     up, down, db, dq_parts = lax.optimization_barrier((up, down, db, dq_parts))
+    for d in (1, 2):
+        dq_parts[d] = lax.ppermute(dq_parts[d], ("xh", "yl"), [(n, n ^ d) for n in range(4)])
     up, down = along(up, 1), along(down, -1)
     db = jnp.sum(db.reshape(8, 2, 128, 128).astype(F32), axis=0)
     db = lax.ppermute(db, ("z", "yl"), swaps())

time: 143 us -> 142 us (level)
  the two profiles are of different devices: /device:TPU:64 before, /device:TPU:1 now
where the time goes in v10:
time: 142 us; the launch traced here: 141 us
  starting transfers between devices  74.9 us (53%)
  waiting for transfers between devices  37.6 us (26%)
  Pallas kernels  16.4 us (12%)
  blocking collectives  10.9 us (8%)
    ppermute x8, starting transfers between devices, along(): return lax.ppermute(value, 'yh', [(n, (n + steps) % 4) for n in range(4)])  29.6 us
    ppermute x3, starting transfers between devices, body(): lax.ppermute(dq_parts[d], ('xh', 'yl'), [(n, n ^ d) for n in range(4)])  16.1 us
    ppermute x8, waiting for transfers between devices, along(): return lax.ppermute(value, 'yh', [(n, (n + steps) % 4) for n in range(4)])  15.3 us
    ppermute x3, waiting for transfers between devices, body(): lax.ppermute(dq_parts[d], ('xh', 'yl'), [(n, n ^ d) for n in range(4)])  15 us
    pallas_call x1, Pallas kernels, body(): pl.pallas_call(functools.partial(attend_kernel, scale), out_shape=(shape(...  11.6 us
    all_to_all x1, blocking collectives, body(): joined = lax.all_to_all(joined, ('xl', 'c'), 0, 0)  10.9 us
    all_to_all x1, starting transfers between devices, body(): got = lax.all_to_all(packed, ('xl', 'c'), 0, 0)  10.3 us
    ppermute x3, starting transfers between devices, body(): lax.ppermute(pays[d], ('xh', 'yl'), [(n, n ^ d) for n in range(4)])  9.88 us
  transfers between devices with their start and end apart: 17, of which 4 were waited for; matrix products, arithmetic and copies ran while one was open for 0% of the time, Pallas kernels for 1%

profile of v10, /device:TPU:1, one launch (start us, length us, event | category | flops | bytes accessed | tf_op | source)
XLA Modules:
  0.0 140.9 jit_solution(913643825058205114)
XLA Ops:
  0.6 2.4 %pack.1 = bf16[4,528,128]{2,1,0:T(8,128)(2,1)} custom-call(bf16[4,128,128]{2,1,0:T(8,128)(2,1)} %k_hbm.1, bf16[4,128,128]{2,1,0:T(8,128)(2,1)} %v_hbm.1, bf16[4,128,128]{2,1,0:T(8,128)(2,1)} %q_hbm.1, bf16[4,128,128]{2,1,0:T(8,128)(2,1)} %g_hbm.1, bf16[4,128,128]{2,1,0:T(8,128)(2,1)} %o_hbm.1, f32[4,4,128]{2,1,0:T(4,128)} %l_hbm.1), custom_call_target="tpu_custom_call" | custom-call | tf_op jit(solution)/shard_map/pack/pallas_call | solution.py:230
  3.0 10.3 %all-to-all-start = ((bf16[4,528,128]{2,1,0:T(8,128)(2,1)}), bf16[4,528,128]{2,1,0:T(8,128)(2,1)S(1)}, u32[]{:S(2)}, u32[]{:S(2)}) async-start(bf16[4,528,128]{2,1,0:T(8,128)(2,1)} %pack.1), calls=%async_computation | async-start | bytes 1081344 | tf_op jit(solution)/shard_map/all_to_all | solution.py:249
  13.4 0.1 stack.27.where_ref
  13.5 0.8 bias.1.bias_ref
  14.3 7.2 %all-to-all-done.got_ref = bf16[4,528,128]{2,1,0:T(8,128)(2,1)S(1)} async-done(((bf16[4,528,128]{2,1,0:T(8,128)(2,1)}), bf16[4,528,128]{2,1,0:T(8,128)(2,1)S(1)}, u32[]{:S(2)}, u32[]{:S(2)}) %all-to-all-start) | async-done | bytes 540704 | tf_op jit(solution)/shard_map/all_to_all | solution.py:249
  21.5 0.2 assemble.1
  21.7 1.9 %collective-permute-start.4 = (bf16[4,272,128]{2,1,0:T(8,128)(2,1)S(1)}, bf16[4,272,128]{2,1,0:T(8,128)(2,1)S(1)}, u32[]{:S(2)}, u32[]{:S(2)}) collective-permute-start(bf16[4,272,128]{2,1,0:T(8,128)(2,1)S(1)} %get-tuple-element.36.kv0_ref), channel_id=1, source_target_pairs={{0,2},{2,4},{4,6},{6,0},{1,3},{3,5},{5,7},{7,1},{8,10},{10,12},{12... | collective-permute-start | bytes 835592 | tf_op jit(solution)/shard_map/ppermute | solution.py:219
  23.6 5.5 %collective-permute-start.3 = (bf16[4,272,128]{2,1,0:T(8,128)(2,1)S(1)}, bf16[4,272,128]{2,1,0:T(8,128)(2,1)S(1)}, u32[]{:S(2)}, u32[]{:S(2)}) collective-permute-start(bf16[4,272,128]{2,1,0:T(8,128)(2,1)S(1)} %get-tuple-element.36.kv0_ref), channel_id=1, source_target_pairs={{0,6},{2,0},{4,2},{6,4},{1,7},{3,1},{5,3},{7,5},{8,14},{10,8},{12,... | collective-permute-start | bytes 835592 | tf_op jit(solution)/shard_map/ppermute | solution.py:219
  29.1 1.9 %collective-permute-start = (bf16[4,400,128]{2,1,0:T(8,128)(2,1)S(1)}, bf16[4,400,128]{2,1,0:T(8,128)(2,1)S(1)}, u32[]{:S(2)}, u32[]{:S(2)}) collective-permute-start(bf16[4,400,128]{2,1,0:T(8,128)(2,1)S(1)} %get-tuple-element.33), channel_id=1, source_target_pairs={{0,1},{1,0},{8,9},{9,8},{2,3},{3,2},{10,11},{11,10},{4,5},{5,4},{1... | collective-permute-start | bytes 1228808 | tf_op jit(solution)/shard_map/ppermute | solution.py:260
  31.1 1.9 %collective-permute-start.1 = (bf16[4,400,128]{2,1,0:T(8,128)(2,1)S(1)}, bf16[4,400,128]{2,1,0:T(8,128)(2,1)S(1)}, u32[]{:S(2)}, u32[]{:S(2)}) collective-permute-start(bf16[4,400,128]{2,1,0:T(8,128)(2,1)S(1)} %get-tuple-element.34), channel_id=1, source_target_pairs={{0,8},{1,9},{8,0},{9,1},{2,10},{3,11},{10,2},{11,3},{4,12},{5,13},... | collective-permute-start | bytes 1228808 | tf_op jit(solution)/shard_map/ppermute | solution.py:260
  33.0 6.0 %collective-permute-start.2 = (bf16[4,400,128]{2,1,0:T(8,128)(2,1)S(1)}, bf16[4,400,128]{2,1,0:T(8,128)(2,1)S(1)}, u32[]{:S(2)}, u32[]{:S(2)}) collective-permute-start(bf16[4,400,128]{2,1,0:T(8,128)(2,1)S(1)} %get-tuple-element.35), channel_id=1, source_target_pairs={{0,9},{1,8},{8,1},{9,0},{2,11},{3,10},{10,3},{11,2},{4,13},{5,12},... | collective-permute-start | bytes 1228808 | tf_op jit(solution)/shard_map/ppermute | solution.py:260
  39.0 0.0 collective-permute-done.4.kv3_ref
  39.1 1.9 %collective-permute-start.5 = (bf16[4,128,128]{2,1,0:T(8,128)(2,1)S(1)}, bf16[4,128,128]{2,1,0:T(8,128)(2,1)S(1)}, u32[]{:S(2)}, u32[]{:S(2)}) collective-permute-start(bf16[4,128,128]{2,1,0:T(8,128)(2,1)S(1)} %slice.8), channel_id=1, source_target_pairs={{0,2},{2,4},{4,6},{6,0},{1,3},{3,5},{5,7},{7,1},{8,10},{10,12},{12... | collective-permute-start | bytes 393224 | tf_op jit(solution)/shard_map/ppermute | solution.py:219
  41.0 5.5 %collective-permute-start.6 = (bf16[4,128,128]{2,1,0:T(8,128)(2,1)S(1)}, bf16[4,128,128]{2,1,0:T(8,128)(2,1)S(1)}, u32[]{:S(2)}, u32[]{:S(2)}) collective-permute-start(bf16[4,128,128]{2,1,0:T(8,128)(2,1)S(1)} %slice.9), channel_id=1, source_target_pairs={{0,6},{2,0},{4,2},{6,4},{1,7},{3,1},{5,3},{7,5},{8,14},{10,8},{12,... | collective-permute-start | bytes 393224 | tf_op jit(solution)/shard_map/ppermute | solution.py:219
  46.5 15.3 %collective-permute-done.5.k2_ref = bf16[4,128,128]{2,1,0:T(8,128)(2,1)S(1)} collective-permute-done((bf16[4,128,128]{2,1,0:T(8,128)(2,1)S(1)}, bf16[4,128,128]{2,1,0:T(8,128)(2,1)S(1)}, u32[]{:S(2)}, u32[]{:S(2)}) %collective-permute-start.5) | collective-permute-done | bytes 131104 | tf_op jit(solution)/shard_map/ppermute | solution.py:219
  61.8 11.6 %attend.1 = (bf16[4,128,128]{2,1,0:T(8,128)(2,1)S(1)}, bf16[4,128,128]{2,1,0:T(8,128)(2,1)S(1)}, bf16[4,128,128]{2,1,0:T(8,128)(2,1)S(1)}, bf16[4,128,128]{2,1,0...) custom-call(s32[6]{0:T(128)S(1)} %stack.27.where_ref, ...), custom_call_target="tpu_custom_call" | custom-call | tf_op jit(solution)/shard_map/attend/pallas_call | solution.py:262
  73.5 8.4 %all-to-all-start.1 = ((bf16[16,128,128]{2,1,0:T(8,128)(2,1)}), bf16[16,128,128]{2,1,0:T(8,128)(2,1)S(1)}, u32[]{:S(2)}, u32[]{:S(2)}) async-start(bf16[16,128,128]{2,1,0:T(8,128)(2,1)} %get-tuple-element.44), calls=%async_computation.1 | async-start | bytes 1048576 | tf_op jit(solution)/shard_map/all_to_all | solution.py:283
  81.9 2.9 %collective-permute-start.7 = (bf16[4,128,128]{2,1,0:T(8,128)(2,1)S(1)}, bf16[4,128,128]{2,1,0:T(8,128)(2,1)S(1)}, u32[]{:S(2)}, u32[]{:S(2)}) collective-permute-start(bf16[4,128,128]{2,1,0:T(8,128)(2,1)S(1)} %get-tuple-element.39), channel_id=1, source_target_pairs={{0,2},{2,4},{4,6},{6,0},{1,3},{3,5},{5,7},{7,1},{8,10},{10,12},{12... | collective-permute-start | bytes 393224 | tf_op jit(solution)/shard_map/ppermute | solution.py:219
  84.8 4.5 %collective-permute-start.8 = (bf16[4,128,128]{2,1,0:T(8,128)(2,1)S(1)}, bf16[4,128,128]{2,1,0:T(8,128)(2,1)S(1)}, u32[]{:S(2)}, u32[]{:S(2)}) collective-permute-start(bf16[4,128,128]{2,1,0:T(8,128)(2,1)S(1)} %get-tuple-element.41), channel_id=1, source_target_pairs={{0,6},{2,0},{4,2},{6,4},{1,7},{3,1},{5,3},{7,5},{8,14},{10,8},{12,... | collective-permute-start | bytes 393224 | tf_op jit(solution)/shard_map/ppermute | solution.py:219
  89.3 8.4 %collective-permute-start.9 = (bf16[4,128,128]{2,1,0:T(8,128)(2,1)S(1)}, bf16[4,128,128]{2,1,0:T(8,128)(2,1)S(1)}, u32[]{:S(2)}, u32[]{:S(2)}) collective-permute-start(bf16[4,128,128]{2,1,0:T(8,128)(2,1)S(1)} %get-tuple-element.48), channel_id=1, source_target_pairs={{0,9},{1,8},{8,1},{9,0},{2,11},{3,10},{10,3},{11,2},{4,13},{5,12},... | collective-permute-start | bytes 393224 | tf_op jit(solution)/shard_map/ppermute | solution.py:285
  97.7 0.1 fold.1
  97.8 4.3 %collective-permute-done.9.dq3_ref = bf16[4,128,128]{2,1,0:T(8,128)(2,1)S(1)} collective-permute-done((bf16[4,128,128]{2,1,0:T(8,128)(2,1)S(1)}, bf16[4,128,128]{2,1,0:T(8,128)(2,1)S(1)}, u32[]{:S(2)}, u32[]{:S(2)}) %collective-permute-start.9) | collective-permute-done | bytes 131104 | tf_op jit(solution)/shard_map/ppermute | solution.py:285
  102.1 4.8 %collective-permute-start.10 = (bf16[4,256,128]{2,1,0:T(8,128)(2,1)S(1)}, bf16[4,256,128]{2,1,0:T(8,128)(2,1)S(1)}, u32[]{:S(2)}, u32[]{:S(2)}) collective-permute-start(bf16[4,256,128]{2,1,0:T(8,128)(2,1)S(1)} %get-tuple-element.49), channel_id=1, source_target_pairs={{0,2},{2,4},{4,6},{6,0},{1,3},{3,5},{5,7},{7,1},{8,10},{10,12},{12... | collective-permute-start | bytes 786440 | tf_op jit(solution)/shard_map/ppermute | solution.py:219
  106.9 2.6 %collective-permute-start.11 = (bf16[4,256,128]{2,1,0:T(8,128)(2,1)S(1)}, bf16[4,256,128]{2,1,0:T(8,128)(2,1)S(1)}, u32[]{:S(2)}, u32[]{:S(2)}) collective-permute-start(bf16[4,256,128]{2,1,0:T(8,128)(2,1)S(1)} %get-tuple-element.50), channel_id=1, source_target_pairs={{0,6},{2,0},{4,2},{6,4},{1,7},{3,1},{5,3},{7,5},{8,14},{10,8},{12,... | collective-permute-start | bytes 786440 | tf_op jit(solution)/shard_map/ppermute | solution.py:219
  109.5 0.1 convert_reduce_fusion
  109.6 0.7 collective-permute-start.12
  110.3 5.5 %collective-permute-start.13 = (bf16[4,128,128]{2,1,0:T(8,128)(2,1)S(1)}, bf16[4,128,128]{2,1,0:T(8,128)(2,1)S(1)}, u32[]{:S(2)}, u32[]{:S(2)}) collective-permute-start(bf16[4,128,128]{2,1,0:T(8,128)(2,1)S(1)} %get-tuple-element.53), channel_id=1, source_target_pairs={{0,1},{1,0},{8,9},{9,8},{2,3},{3,2},{10,11},{11,10},{4,5},{5,4},{1... | collective-permute-start | bytes 393224 | tf_op jit(solution)/shard_map/ppermute | solution.py:288
  115.8 2.2 %collective-permute-start.14 = (bf16[4,128,128]{2,1,0:T(8,128)(2,1)S(1)}, bf16[4,128,128]{2,1,0:T(8,128)(2,1)S(1)}, u32[]{:S(2)}, u32[]{:S(2)}) collective-permute-start(bf16[4,128,128]{2,1,0:T(8,128)(2,1)S(1)} %get-tuple-element.54), channel_id=1, source_target_pairs={{0,8},{1,9},{8,0},{9,1},{2,10},{3,11},{10,2},{11,3},{4,12},{5,13},... | collective-permute-start | bytes 393224 | tf_op jit(solution)/shard_map/ppermute | solution.py:288
  118.0 10.7 %collective-permute-done.13.dq1_ref = bf16[4,128,128]{2,1,0:T(8,128)(2,1)S(1)} collective-permute-done((bf16[4,128,128]{2,1,0:T(8,128)(2,1)S(1)}, bf16[4,128,128]{2,1,0:T(8,128)(2,1)S(1)}, u32[]{:S(2)}, u32[]{:S(2)}) %collective-permute-start.13) | collective-permute-done | bytes 131104 | tf_op jit(solution)/shard_map/ppermute | solution.py:288
  128.7 0.2 join.1
  128.9 10.9 %all_to_all.15.got_ref = bf16[4,512,128]{2,1,0:T(8,128)(2,1)S(1)} all-to-all(bf16[4,512,128]{2,1,0:T(8,128)(2,1)S(1)} %join.1), channel_id=1, replica_groups=mesh['xl'=2,'z'=8,'c'=2,'xh'=2,'yh'=4,'yl'=2] {'xl','c'}, dimensions={0} | all-to-all | bytes 1048576 | tf_op jit(solution)/shard_map/all_to_all | solution.py:300
  139.9 1.1 unpack.1
  (16 shorter events, 0.1 us)
Async XLA Ops:
  0.6 12.8 %copy-start = (bf16[4,128,2048]{2,1,0:T(8,128)(2,1)S(1)}, bf16[4,128,2048]{2,1,0:T(8,128)(2,1)}, u32[]{:S(2)}) copy-start(bf16[4,128,2048]{2,1,0:T(8,128)(2,1)} %bias_hbm.1) | copy-start | bytes 6291460
  3.0 18.5 %all-to-all-start = ((bf16[4,528,128]{2,1,0:T(8,128)(2,1)}), bf16[4,528,128]{2,1,0:T(8,128)(2,1)S(1)}, u32[]{:S(2)}, u32[]{:S(2)}) async-start(bf16[4,528,128]{2,1,0:T(8,128)(2,1)} %pack.1), calls=%async_computation | async-start | bytes 1081344 | tf_op jit(solution)/shard_map/all_to_all | solution.py:249
  21.7 17.3 %collective-permute-start.4 = (bf16[4,272,128]{2,1,0:T(8,128)(2,1)S(1)}, bf16[4,272,128]{2,1,0:T(8,128)(2,1)S(1)}, u32[]{:S(2)}, u32[]{:S(2)}) collective-permute-start(bf16[4,272,128]{2,1,0:T(8,128)(2,1)S(1)} %get-tuple-element.36.kv0_ref), channel_id=1, source_target_pairs={{0,2},{2,4},{4,6},{6,0},{1,3},{3,5},{5,7},{7,1},{8,10},{10,12},{12... | collective-permute-start | bytes 835592 | tf_op jit(solution)/shard_map/ppermute | solution.py:219
  23.6 17.3 %collective-permute-start.3 = (bf16[4,272,128]{2,1,0:T(8,128)(2,1)S(1)}, bf16[4,272,128]{2,1,0:T(8,128)(2,1)S(1)}, u32[]{:S(2)}, u32[]{:S(2)}) collective-permute-start(bf16[4,272,128]{2,1,0:T(8,128)(2,1)S(1)} %get-tuple-element.36.kv0_ref), channel_id=1, source_target_pairs={{0,6},{2,0},{4,2},{6,4},{1,7},{3,1},{5,3},{7,5},{8,14},{10,8},{12,... | collective-permute-start | bytes 835592 | tf_op jit(solution)/shard_map/ppermute | solution.py:219
  29.1 32.7 %collective-permute-start = (bf16[4,400,128]{2,1,0:T(8,128)(2,1)S(1)}, bf16[4,400,128]{2,1,0:T(8,128)(2,1)S(1)}, u32[]{:S(2)}, u32[]{:S(2)}) collective-permute-start(bf16[4,400,128]{2,1,0:T(8,128)(2,1)S(1)} %get-tuple-element.33), channel_id=1, source_target_pairs={{0,1},{1,0},{8,9},{9,8},{2,3},{3,2},{10,11},{11,10},{4,5},{5,4},{1... | collective-permute-start | bytes 1228808 | tf_op jit(solution)/shard_map/ppermute | solution.py:260
  31.1 30.8 %collective-permute-start.1 = (bf16[4,400,128]{2,1,0:T(8,128)(2,1)S(1)}, bf16[4,400,128]{2,1,0:T(8,128)(2,1)S(1)}, u32[]{:S(2)}, u32[]{:S(2)}) collective-permute-start(bf16[4,400,128]{2,1,0:T(8,128)(2,1)S(1)} %get-tuple-element.34), channel_id=1, source_target_pairs={{0,8},{1,9},{8,0},{9,1},{2,10},{3,11},{10,2},{11,3},{4,12},{5,13},... | collective-permute-start | bytes 1228808 | tf_op jit(solution)/shard_map/ppermute | solution.py:260
  33.0 28.8 %collective-permute-start.2 = (bf16[4,400,128]{2,1,0:T(8,128)(2,1)S(1)}, bf16[4,400,128]{2,1,0:T(8,128)(2,1)S(1)}, u32[]{:S(2)}, u32[]{:S(2)}) collective-permute-start(bf16[4,400,128]{2,1,0:T(8,128)(2,1)S(1)} %get-tuple-element.35), channel_id=1, source_target_pairs={{0,9},{1,8},{8,1},{9,0},{2,11},{3,10},{10,3},{11,2},{4,13},{5,12},... | collective-permute-start | bytes 1228808 | tf_op jit(solution)/shard_map/ppermute | solution.py:260
  39.1 22.8 %collective-permute-start.5 = (bf16[4,128,128]{2,1,0:T(8,128)(2,1)S(1)}, bf16[4,128,128]{2,1,0:T(8,128)(2,1)S(1)}, u32[]{:S(2)}, u32[]{:S(2)}) collective-permute-start(bf16[4,128,128]{2,1,0:T(8,128)(2,1)S(1)} %slice.8), channel_id=1, source_target_pairs={{0,2},{2,4},{4,6},{6,0},{1,3},{3,5},{5,7},{7,1},{8,10},{10,12},{12... | collective-permute-start | bytes 393224 | tf_op jit(solution)/shard_map/ppermute | solution.py:219
  41.0 20.8 %collective-permute-start.6 = (bf16[4,128,128]{2,1,0:T(8,128)(2,1)S(1)}, bf16[4,128,128]{2,1,0:T(8,128)(2,1)S(1)}, u32[]{:S(2)}, u32[]{:S(2)}) collective-permute-start(bf16[4,128,128]{2,1,0:T(8,128)(2,1)S(1)} %slice.9), channel_id=1, source_target_pairs={{0,6},{2,0},{4,2},{6,4},{1,7},{3,1},{5,3},{7,5},{8,14},{10,8},{12,... | collective-permute-start | bytes 393224 | tf_op jit(solution)/shard_map/ppermute | solution.py:219
  73.5 28.6 %all-to-all-start.1 = ((bf16[16,128,128]{2,1,0:T(8,128)(2,1)}), bf16[16,128,128]{2,1,0:T(8,128)(2,1)S(1)}, u32[]{:S(2)}, u32[]{:S(2)}) async-start(bf16[16,128,128]{2,1,0:T(8,128)(2,1)} %get-tuple-element.44), calls=%async_computation.1 | async-start | bytes 1048576 | tf_op jit(solution)/shard_map/all_to_all | solution.py:283
  81.9 15.8 %collective-permute-start.7 = (bf16[4,128,128]{2,1,0:T(8,128)(2,1)S(1)}, bf16[4,128,128]{2,1,0:T(8,128)(2,1)S(1)}, u32[]{:S(2)}, u32[]{:S(2)}) collective-permute-start(bf16[4,128,128]{2,1,0:T(8,128)(2,1)S(1)} %get-tuple-element.39), channel_id=1, source_target_pairs={{0,2},{2,4},{4,6},{6,0},{1,3},{3,5},{5,7},{7,1},{8,10},{10,12},{12... | collective-permute-start | bytes 393224 | tf_op jit(solution)/shard_map/ppermute | solution.py:219
  84.8 12.9 %collective-permute-start.8 = (bf16[4,128,128]{2,1,0:T(8,128)(2,1)S(1)}, bf16[4,128,128]{2,1,0:T(8,128)(2,1)S(1)}, u32[]{:S(2)}, u32[]{:S(2)}) collective-permute-start(bf16[4,128,128]{2,1,0:T(8,128)(2,1)S(1)} %get-tuple-element.41), channel_id=1, source_target_pairs={{0,6},{2,0},{4,2},{6,4},{1,7},{3,1},{5,3},{7,5},{8,14},{10,8},{12,... | collective-permute-start | bytes 393224 | tf_op jit(solution)/shard_map/ppermute | solution.py:219
  89.3 12.8 %collective-permute-start.9 = (bf16[4,128,128]{2,1,0:T(8,128)(2,1)S(1)}, bf16[4,128,128]{2,1,0:T(8,128)(2,1)S(1)}, u32[]{:S(2)}, u32[]{:S(2)}) collective-permute-start(bf16[4,128,128]{2,1,0:T(8,128)(2,1)S(1)} %get-tuple-element.48), channel_id=1, source_target_pairs={{0,9},{1,8},{8,1},{9,0},{2,11},{3,10},{10,3},{11,2},{4,13},{5,12},... | collective-permute-start | bytes 393224 | tf_op jit(solution)/shard_map/ppermute | solution.py:285
  102.1 26.6 %collective-permute-start.10 = (bf16[4,256,128]{2,1,0:T(8,128)(2,1)S(1)}, bf16[4,256,128]{2,1,0:T(8,128)(2,1)S(1)}, u32[]{:S(2)}, u32[]{:S(2)}) collective-permute-start(bf16[4,256,128]{2,1,0:T(8,128)(2,1)S(1)} %get-tuple-element.49), channel_id=1, source_target_pairs={{0,2},{2,4},{4,6},{6,0},{1,3},{3,5},{5,7},{7,1},{8,10},{10,12},{12... | collective-permute-start | bytes 786440 | tf_op jit(solution)/shard_map/ppermute | solution.py:219
  106.9 21.8 %collective-permute-start.11 = (bf16[4,256,128]{2,1,0:T(8,128)(2,1)S(1)}, bf16[4,256,128]{2,1,0:T(8,128)(2,1)S(1)}, u32[]{:S(2)}, u32[]{:S(2)}) collective-permute-start(bf16[4,256,128]{2,1,0:T(8,128)(2,1)S(1)} %get-tuple-element.50), channel_id=1, source_target_pairs={{0,6},{2,0},{4,2},{6,4},{1,7},{3,1},{5,3},{7,5},{8,14},{10,8},{12,... | collective-permute-start | bytes 786440 | tf_op jit(solution)/shard_map/ppermute | solution.py:219
  109.6 8.4 %collective-permute-start.12 = (f32[2,128,128]{2,1,0:T(8,128)S(1)}, f32[2,128,128]{2,1,0:T(8,128)S(1)}, u32[]{:S(2)}, u32[]{:S(2)}) collective-permute-start(f32[2,128,128]{2,1,0:T(8,128)S(1)} %convert_reduce_fusion), channel_id=1, source_target_pairs={{0,0},{1,32},{32,1},{33,33},{64,64},{65,96},{96,65},{97,97},{128,1... | collective-permute-start | bytes 393224 | tf_op jit(solution)/shard_map/ppermute | solution.py:291
  110.3 18.4 %collective-permute-start.13 = (bf16[4,128,128]{2,1,0:T(8,128)(2,1)S(1)}, bf16[4,128,128]{2,1,0:T(8,128)(2,1)S(1)}, u32[]{:S(2)}, u32[]{:S(2)}) collective-permute-start(bf16[4,128,128]{2,1,0:T(8,128)(2,1)S(1)} %get-tuple-element.53), channel_id=1, source_target_pairs={{0,1},{1,0},{8,9},{9,8},{2,3},{3,2},{10,11},{11,10},{4,5},{5,4},{1... | collective-permute-start | bytes 393224 | tf_op jit(solution)/shard_map/ppermute | solution.py:288
  115.8 12.9 %collective-permute-start.14 = (bf16[4,128,128]{2,1,0:T(8,128)(2,1)S(1)}, bf16[4,128,128]{2,1,0:T(8,128)(2,1)S(1)}, u32[]{:S(2)}, u32[]{:S(2)}) collective-permute-start(bf16[4,128,128]{2,1,0:T(8,128)(2,1)S(1)} %get-tuple-element.54), channel_id=1, source_target_pairs={{0,8},{1,9},{8,0},{9,1},{2,10},{3,11},{10,2},{11,3},{4,12},{5,13},... | collective-permute-start | bytes 393224 | tf_op jit(solution)/shard_map/ppermute | solution.py:288

commit v11 on v9

--- a/solution.py
+++ b/solution.py
@@ -12,6 +12,7 @@
 BLK = ("xh", "yh", "yl")
 LOG2E = 1.4426950408889634
 AUG = 16
+FLIPS = (0, 3, 2, 1)
 F32, BF16 = jnp.float32, jnp.bfloat16
 
 
@@ -224,7 +225,7 @@
     shape = lambda *s: jax.ShapeDtypeStruct(s, BF16)
     head = lax.axis_index("xl") * 2 + lax.axis_index("c")
     mine = lax.axis_index("xh") * 2 + lax.axis_index("yl")
-    where = jnp.stack([head] + [mine ^ d for d in range(4)] + [lax.axis_index("yh")]).astype(jnp.int32)
+    where = jnp.stack([head] + [mine ^ d for d in FLIPS] + [lax.axis_index("yh")]).astype(jnp.int32)
     hbm = pl.BlockSpec(memory_space=pltpu.HBM)
     smem = pl.BlockSpec(memory_space=pltpu.SMEM)
     packed = pl.pallas_call(
@@ -257,7 +258,7 @@
     )(got, bias_out)
     after, before = along(own, -1), along(own, 1)
     for d in range(1, 4):
-        pays[d] = lax.ppermute(pays[d], ("xh", "yl"), [(n, n ^ d) for n in range(4)])
+        pays[d] = lax.ppermute(pays[d], ("xh", "yl"), [(n, n ^ FLIPS[d]) for n in range(4)])
     k_far, v_far = along(before[:, :128], 1), along(after[:, 128:256], -1)
     *dq_parts, own, up, dk_far, dv_far, down, db_parts = pl.pallas_call(
         functools.partial(attend_kernel, scale),
@@ -281,9 +282,9 @@
         name="fold",
     )(up, up_more, down, down_more)
     db = lax.all_to_all(db_parts, ("z", "xh"), 0, 0)
+    up, down, db, dq_parts = lax.optimization_barrier((up, down, db, dq_parts))
     for d in range(1, 4):
-        dq_parts[d] = lax.ppermute(dq_parts[d], ("xh", "yl"), [(n, n ^ d) for n in range(4)])
-    up, down, db, dq_parts = lax.optimization_barrier((up, down, db, dq_parts))
+        dq_parts[d] = lax.ppermute(dq_parts[d], ("xh", "yl"), [(n, n ^ FLIPS[d]) for n in range(4)])
     up, down = along(up, 1), along(down, -1)
     db = jnp.sum(db.reshape(8, 2, 128, 128).astype(F32), axis=0)
     db = lax.ppermute(db, ("z", "yl"), swaps())

time: 143 us -> 142 us (level)
  the two profiles are of different devices: /device:TPU:64 before, /device:TPU:1 now
where the time goes in v11:
time: 142 us; the launch traced here: 141 us
  starting transfers between devices  74.2 us (52%)
  waiting for transfers between devices  35.4 us (25%)
  Pallas kernels  16.4 us (12%)
  blocking collectives  14.2 us (10%)
    ppermute x8, starting transfers between devices, along(): return lax.ppermute(value, 'yh', [(n, (n + steps) % 4) for n in range(4)])  30.2 us
    ppermute x8, waiting for transfers between devices, along(): return lax.ppermute(value, 'yh', [(n, (n + steps) % 4) for n in range(4)])  19.5 us
    ppermute x3, starting transfers between devices, body(): lax.ppermute(dq_parts[d], ('xh', 'yl'), [(n, n ^ FLIPS[d]) for n in range...  14.8 us
    all_to_all x1, blocking collectives, body(): joined = lax.all_to_all(joined, ('xl', 'c'), 0, 0)  14.2 us
    pallas_call x1, Pallas kernels, body(): pl.pallas_call(functools.partial(attend_kernel, scale), out_shape=(shape(...  11.6 us
    all_to_all x1, starting transfers between devices, body(): got = lax.all_to_all(packed, ('xl', 'c'), 0, 0)  10.3 us
    ppermute x3, starting transfers between devices, body(): lax.ppermute(pays[d], ('xh', 'yl'), [(n, n ^ FLIPS[d]) for n in range(4)])  9.88 us
    all_to_all x1, starting transfers between devices, body(): db = lax.all_to_all(db_parts, ('z', 'xh'), 0, 0)  8.4 us
  transfers between devices with their start and end apart: 17, of which 8 were waited for; matrix products, arithmetic and copies ran while one was open for 0% of the time, Pallas kernels for 1%

profile of v11, /device:TPU:1, one launch (start us, length us, event | category | flops | bytes accessed | tf_op | source)
XLA Modules:
  0.0 141.2 jit_solution(15005651551714776372)
XLA Ops:
  0.6 2.4 %pack.1 = bf16[4,528,128]{2,1,0:T(8,128)(2,1)} custom-call(bf16[4,128,128]{2,1,0:T(8,128)(2,1)} %k_hbm.1, bf16[4,128,128]{2,1,0:T(8,128)(2,1)} %v_hbm.1, bf16[4,128,128]{2,1,0:T(8,128)(2,1)} %q_hbm.1, bf16[4,128,128]{2,1,0:T(8,128)(2,1)} %g_hbm.1, bf16[4,128,128]{2,1,0:T(8,128)(2,1)} %o_hbm.1, f32[4,4,128]{2,1,0:T(4,128)} %l_hbm.1), custom_call_target="tpu_custom_call" | custom-call | tf_op jit(solution)/shard_map/pack/pallas_call | solution.py:231
  3.0 10.3 %all-to-all-start = ((bf16[4,528,128]{2,1,0:T(8,128)(2,1)}), bf16[4,528,128]{2,1,0:T(8,128)(2,1)S(1)}, u32[]{:S(2)}, u32[]{:S(2)}) async-start(bf16[4,528,128]{2,1,0:T(8,128)(2,1)} %pack.1), calls=%async_computation | async-start | bytes 1081344 | tf_op jit(solution)/shard_map/all_to_all | solution.py:250
  13.5 0.8 bias.1.bias_ref
  14.3 7.2 %all-to-all-done.got_ref = bf16[4,528,128]{2,1,0:T(8,128)(2,1)S(1)} async-done(((bf16[4,528,128]{2,1,0:T(8,128)(2,1)}), bf16[4,528,128]{2,1,0:T(8,128)(2,1)S(1)}, u32[]{:S(2)}, u32[]{:S(2)}) %all-to-all-start) | async-done | bytes 540704 | tf_op jit(solution)/shard_map/all_to_all | solution.py:250
  21.5 0.2 assemble.1
  21.7 1.9 %collective-permute-start.4 = (bf16[4,272,128]{2,1,0:T(8,128)(2,1)S(1)}, bf16[4,272,128]{2,1,0:T(8,128)(2,1)S(1)}, u32[]{:S(2)}, u32[]{:S(2)}) collective-permute-start(bf16[4,272,128]{2,1,0:T(8,128)(2,1)S(1)} %get-tuple-element.36.kv0_ref), channel_id=1, source_target_pairs={{0,2},{2,4},{4,6},{6,0},{1,3},{3,5},{5,7},{7,1},{8,10},{10,12},{12... | collective-permute-start | bytes 835592 | tf_op jit(solution)/shard_map/ppermute | solution.py:220
  23.6 5.5 %collective-permute-start.3 = (bf16[4,272,128]{2,1,0:T(8,128)(2,1)S(1)}, bf16[4,272,128]{2,1,0:T(8,128)(2,1)S(1)}, u32[]{:S(2)}, u32[]{:S(2)}) collective-permute-start(bf16[4,272,128]{2,1,0:T(8,128)(2,1)S(1)} %get-tuple-element.36.kv0_ref), channel_id=1, source_target_pairs={{0,6},{2,0},{4,2},{6,4},{1,7},{3,1},{5,3},{7,5},{8,14},{10,8},{12,... | collective-permute-start | bytes 835592 | tf_op jit(solution)/shard_map/ppermute | solution.py:220
  29.1 1.9 %collective-permute-start = (bf16[4,400,128]{2,1,0:T(8,128)(2,1)S(1)}, bf16[4,400,128]{2,1,0:T(8,128)(2,1)S(1)}, u32[]{:S(2)}, u32[]{:S(2)}) collective-permute-start(bf16[4,400,128]{2,1,0:T(8,128)(2,1)S(1)} %get-tuple-element.33), channel_id=1, source_target_pairs={{0,9},{1,8},{8,1},{9,0},{2,11},{3,10},{10,3},{11,2},{4,13},{5,12},... | collective-permute-start | bytes 1228808 | tf_op jit(solution)/shard_map/ppermute | solution.py:261
  31.1 1.9 %collective-permute-start.1 = (bf16[4,400,128]{2,1,0:T(8,128)(2,1)S(1)}, bf16[4,400,128]{2,1,0:T(8,128)(2,1)S(1)}, u32[]{:S(2)}, u32[]{:S(2)}) collective-permute-start(bf16[4,400,128]{2,1,0:T(8,128)(2,1)S(1)} %get-tuple-element.34), channel_id=1, source_target_pairs={{0,8},{1,9},{8,0},{9,1},{2,10},{3,11},{10,2},{11,3},{4,12},{5,13},... | collective-permute-start | bytes 1228808 | tf_op jit(solution)/shard_map/ppermute | solution.py:261
  33.0 6.0 %collective-permute-start.2 = (bf16[4,400,128]{2,1,0:T(8,128)(2,1)S(1)}, bf16[4,400,128]{2,1,0:T(8,128)(2,1)S(1)}, u32[]{:S(2)}, u32[]{:S(2)}) collective-permute-start(bf16[4,400,128]{2,1,0:T(8,128)(2,1)S(1)} %get-tuple-element.35), channel_id=1, source_target_pairs={{0,1},{1,0},{8,9},{9,8},{2,3},{3,2},{10,11},{11,10},{4,5},{5,4},{1... | collective-permute-start | bytes 1228808 | tf_op jit(solution)/shard_map/ppermute | solution.py:261
  39.1 1.9 %collective-permute-start.5 = (bf16[4,128,128]{2,1,0:T(8,128)(2,1)S(1)}, bf16[4,128,128]{2,1,0:T(8,128)(2,1)S(1)}, u32[]{:S(2)}, u32[]{:S(2)}) collective-permute-start(bf16[4,128,128]{2,1,0:T(8,128)(2,1)S(1)} %slice.8), channel_id=1, source_target_pairs={{0,2},{2,4},{4,6},{6,0},{1,3},{3,5},{5,7},{7,1},{8,10},{10,12},{12... | collective-permute-start | bytes 393224 | tf_op jit(solution)/shard_map/ppermute | solution.py:220
  41.0 5.5 %collective-permute-start.6 = (bf16[4,128,128]{2,1,0:T(8,128)(2,1)S(1)}, bf16[4,128,128]{2,1,0:T(8,128)(2,1)S(1)}, u32[]{:S(2)}, u32[]{:S(2)}) collective-permute-start(bf16[4,128,128]{2,1,0:T(8,128)(2,1)S(1)} %slice.9), channel_id=1, source_target_pairs={{0,6},{2,0},{4,2},{6,4},{1,7},{3,1},{5,3},{7,5},{8,14},{10,8},{12,... | collective-permute-start | bytes 393224 | tf_op jit(solution)/shard_map/ppermute | solution.py:220
  46.5 15.4 %collective-permute-done.5.k2_ref = bf16[4,128,128]{2,1,0:T(8,128)(2,1)S(1)} collective-permute-done((bf16[4,128,128]{2,1,0:T(8,128)(2,1)S(1)}, bf16[4,128,128]{2,1,0:T(8,128)(2,1)S(1)}, u32[]{:S(2)}, u32[]{:S(2)}) %collective-permute-start.5) | collective-permute-done | bytes 131104 | tf_op jit(solution)/shard_map/ppermute | solution.py:220
  61.9 11.6 %attend.1 = (bf16[4,128,128]{2,1,0:T(8,128)(2,1)S(1)}, bf16[4,128,128]{2,1,0:T(8,128)(2,1)S(1)}, bf16[4,128,128]{2,1,0:T(8,128)(2,1)S(1)}, bf16[4,128,128]{2,1,0...) custom-call(s32[6]{0:T(128)S(1)} %stack.27.where_ref, ...), custom_call_target="tpu_custom_call" | custom-call | tf_op jit(solution)/shard_map/attend/pallas_call | solution.py:263
  73.6 8.4 %all-to-all-start.1 = ((bf16[16,128,128]{2,1,0:T(8,128)(2,1)}), bf16[16,128,128]{2,1,0:T(8,128)(2,1)S(1)}, u32[]{:S(2)}, u32[]{:S(2)}) async-start(bf16[16,128,128]{2,1,0:T(8,128)(2,1)} %get-tuple-element.44), calls=%async_computation.1 | async-start | bytes 1048576 | tf_op jit(solution)/shard_map/all_to_all | solution.py:284
  82.0 2.8 %collective-permute-start.7 = (bf16[4,128,128]{2,1,0:T(8,128)(2,1)S(1)}, bf16[4,128,128]{2,1,0:T(8,128)(2,1)S(1)}, u32[]{:S(2)}, u32[]{:S(2)}) collective-permute-start(bf16[4,128,128]{2,1,0:T(8,128)(2,1)S(1)} %get-tuple-element.39), channel_id=1, source_target_pairs={{0,2},{2,4},{4,6},{6,0},{1,3},{3,5},{5,7},{7,1},{8,10},{10,12},{12... | collective-permute-start | bytes 393224 | tf_op jit(solution)/shard_map/ppermute | solution.py:220
  84.8 4.6 %collective-permute-start.8 = (bf16[4,128,128]{2,1,0:T(8,128)(2,1)S(1)}, bf16[4,128,128]{2,1,0:T(8,128)(2,1)S(1)}, u32[]{:S(2)}, u32[]{:S(2)}) collective-permute-start(bf16[4,128,128]{2,1,0:T(8,128)(2,1)S(1)} %get-tuple-element.41), channel_id=1, source_target_pairs={{0,6},{2,0},{4,2},{6,4},{1,7},{3,1},{5,3},{7,5},{8,14},{10,8},{12,... | collective-permute-start | bytes 393224 | tf_op jit(solution)/shard_map/ppermute | solution.py:220
  89.4 0.7 collective-permute-done.7.up_more_ref
  90.1 3.4 %collective-permute-done.8.down_more_ref = bf16[4,128,128]{2,1,0:T(8,128)(2,1)S(1)} collective-permute-done((bf16[4,128,128]{2,1,0:T(8,128)(2,1)S(1)}, bf16[4,128,128]{2,1,0:T(8,128)(2,1)S(1)}, u32[]{:S(2)}, u32[]{:S(2)}) %collective-permute-start.8) | collective-permute-done | bytes 131104 | tf_op jit(solution)/shard_map/ppermute | solution.py:220
  93.5 3.4 %all-to-all-done.1 = bf16[16,128,128]{2,1,0:T(8,128)(2,1)S(1)} async-done(((bf16[16,128,128]{2,1,0:T(8,128)(2,1)}), bf16[16,128,128]{2,1,0:T(8,128)(2,1)S(1)}, u32[]{:S(2)}, u32[]{:S(2)}) %all-to-all-start.1) | async-done | bytes 524320 | tf_op jit(solution)/shard_map/all_to_all | solution.py:284
  97.0 0.7 collective-permute-start.11
  97.7 2.5 %collective-permute-start.9 = (bf16[4,256,128]{2,1,0:T(8,128)(2,1)S(1)}, bf16[4,256,128]{2,1,0:T(8,128)(2,1)S(1)}, u32[]{:S(2)}, u32[]{:S(2)}) collective-permute-start(bf16[4,256,128]{2,1,0:T(8,128)(2,1)S(1)} %get-tuple-element.49), channel_id=1, source_target_pairs={{0,2},{2,4},{4,6},{6,0},{1,3},{3,5},{5,7},{7,1},{8,10},{10,12},{12... | collective-permute-start | bytes 786440 | tf_op jit(solution)/shard_map/ppermute | solution.py:220
  100.2 5.5 %collective-permute-start.10 = (bf16[4,256,128]{2,1,0:T(8,128)(2,1)S(1)}, bf16[4,256,128]{2,1,0:T(8,128)(2,1)S(1)}, u32[]{:S(2)}, u32[]{:S(2)}) collective-permute-start(bf16[4,256,128]{2,1,0:T(8,128)(2,1)S(1)} %get-tuple-element.50), channel_id=1, source_target_pairs={{0,6},{2,0},{4,2},{6,4},{1,7},{3,1},{5,3},{7,5},{8,14},{10,8},{12,... | collective-permute-start | bytes 786440 | tf_op jit(solution)/shard_map/ppermute | solution.py:220
  105.7 8.1 %collective-permute-start.12 = (bf16[4,128,128]{2,1,0:T(8,128)(2,1)S(1)}, bf16[4,128,128]{2,1,0:T(8,128)(2,1)S(1)}, u32[]{:S(2)}, u32[]{:S(2)}) collective-permute-start(bf16[4,128,128]{2,1,0:T(8,128)(2,1)S(1)} %get-tuple-element.53), channel_id=1, source_target_pairs={{0,9},{1,8},{8,1},{9,0},{2,11},{3,10},{10,3},{11,2},{4,13},{5,12},... | collective-permute-start | bytes 393224 | tf_op jit(solution)/shard_map/ppermute | solution.py:287
  113.9 4.7 %collective-permute-start.13 = (bf16[4,128,128]{2,1,0:T(8,128)(2,1)S(1)}, bf16[4,128,128]{2,1,0:T(8,128)(2,1)S(1)}, u32[]{:S(2)}, u32[]{:S(2)}) collective-permute-start(bf16[4,128,128]{2,1,0:T(8,128)(2,1)S(1)} %get-tuple-element.54), channel_id=1, source_target_pairs={{0,8},{1,9},{8,0},{9,1},{2,10},{3,11},{10,2},{11,3},{4,12},{5,13},... | collective-permute-start | bytes 393224 | tf_op jit(solution)/shard_map/ppermute | solution.py:287
  118.6 1.9 %collective-permute-start.14 = (bf16[4,128,128]{2,1,0:T(8,128)(2,1)S(1)}, bf16[4,128,128]{2,1,0:T(8,128)(2,1)S(1)}, u32[]{:S(2)}, u32[]{:S(2)}) collective-permute-start(bf16[4,128,128]{2,1,0:T(8,128)(2,1)S(1)} %get-tuple-element.55), channel_id=1, source_target_pairs={{0,1},{1,0},{8,9},{9,8},{2,3},{3,2},{10,11},{11,10},{4,5},{5,4},{1... | collective-permute-start | bytes 393224 | tf_op jit(solution)/shard_map/ppermute | solution.py:287
  120.5 1.5 %collective-permute-done.12.dq1_ref = bf16[4,128,128]{2,1,0:T(8,128)(2,1)S(1)} collective-permute-done((bf16[4,128,128]{2,1,0:T(8,128)(2,1)S(1)}, bf16[4,128,128]{2,1,0:T(8,128)(2,1)S(1)}, u32[]{:S(2)}, u32[]{:S(2)}) %collective-permute-start.12) | collective-permute-done | bytes 131104 | tf_op jit(solution)/shard_map/ppermute | solution.py:287
  122.0 0.2 collective-permute-done.13.dq2_ref
  122.3 3.5 %collective-permute-done.14.dq3_ref = bf16[4,128,128]{2,1,0:T(8,128)(2,1)S(1)} collective-permute-done((bf16[4,128,128]{2,1,0:T(8,128)(2,1)S(1)}, bf16[4,128,128]{2,1,0:T(8,128)(2,1)S(1)}, u32[]{:S(2)}, u32[]{:S(2)}) %collective-permute-start.14) | collective-permute-done | bytes 131104 | tf_op jit(solution)/shard_map/ppermute | solution.py:287
  125.8 0.2 join.1
  126.0 14.2 %all_to_all.15.got_ref = bf16[4,512,128]{2,1,0:T(8,128)(2,1)S(1)} all-to-all(bf16[4,512,128]{2,1,0:T(8,128)(2,1)S(1)} %join.1), channel_id=1, replica_groups=mesh['xl'=2,'z'=8,'c'=2,'xh'=2,'yh'=4,'yl'=2] {'xl','c'}, dimensions={0} | all-to-all | bytes 1048576 | tf_op jit(solution)/shard_map/all_to_all | solution.py:299
  140.2 1.1 unpack.1
  (16 shorter events, 0.3 us)
Async XLA Ops:
  0.6 12.8 %copy-start = (bf16[4,128,2048]{2,1,0:T(8,128)(2,1)S(1)}, bf16[4,128,2048]{2,1,0:T(8,128)(2,1)}, u32[]{:S(2)}) copy-start(bf16[4,128,2048]{2,1,0:T(8,128)(2,1)} %bias_hbm.1) | copy-start | bytes 6291460
  3.0 18.5 %all-to-all-start = ((bf16[4,528,128]{2,1,0:T(8,128)(2,1)}), bf16[4,528,128]{2,1,0:T(8,128)(2,1)S(1)}, u32[]{:S(2)}, u32[]{:S(2)}) async-start(bf16[4,528,128]{2,1,0:T(8,128)(2,1)} %pack.1), calls=%async_computation | async-start | bytes 1081344 | tf_op jit(solution)/shard_map/all_to_all | solution.py:250
  21.7 17.3 %collective-permute-start.4 = (bf16[4,272,128]{2,1,0:T(8,128)(2,1)S(1)}, bf16[4,272,128]{2,1,0:T(8,128)(2,1)S(1)}, u32[]{:S(2)}, u32[]{:S(2)}) collective-permute-start(bf16[4,272,128]{2,1,0:T(8,128)(2,1)S(1)} %get-tuple-element.36.kv0_ref), channel_id=1, source_target_pairs={{0,2},{2,4},{4,6},{6,0},{1,3},{3,5},{5,7},{7,1},{8,10},{10,12},{12... | collective-permute-start | bytes 835592 | tf_op jit(solution)/shard_map/ppermute | solution.py:220
  23.6 17.3 %collective-permute-start.3 = (bf16[4,272,128]{2,1,0:T(8,128)(2,1)S(1)}, bf16[4,272,128]{2,1,0:T(8,128)(2,1)S(1)}, u32[]{:S(2)}, u32[]{:S(2)}) collective-permute-start(bf16[4,272,128]{2,1,0:T(8,128)(2,1)S(1)} %get-tuple-element.36.kv0_ref), channel_id=1, source_target_pairs={{0,6},{2,0},{4,2},{6,4},{1,7},{3,1},{5,3},{7,5},{8,14},{10,8},{12,... | collective-permute-start | bytes 835592 | tf_op jit(solution)/shard_map/ppermute | solution.py:220
  29.1 32.8 %collective-permute-start = (bf16[4,400,128]{2,1,0:T(8,128)(2,1)S(1)}, bf16[4,400,128]{2,1,0:T(8,128)(2,1)S(1)}, u32[]{:S(2)}, u32[]{:S(2)}) collective-permute-start(bf16[4,400,128]{2,1,0:T(8,128)(2,1)S(1)} %get-tuple-element.33), channel_id=1, source_target_pairs={{0,9},{1,8},{8,1},{9,0},{2,11},{3,10},{10,3},{11,2},{4,13},{5,12},... | collective-permute-start | bytes 1228808 | tf_op jit(solution)/shard_map/ppermute | solution.py:261
  31.1 30.9 %collective-permute-start.1 = (bf16[4,400,128]{2,1,0:T(8,128)(2,1)S(1)}, bf16[4,400,128]{2,1,0:T(8,128)(2,1)S(1)}, u32[]{:S(2)}, u32[]{:S(2)}) collective-permute-start(bf16[4,400,128]{2,1,0:T(8,128)(2,1)S(1)} %get-tuple-element.34), channel_id=1, source_target_pairs={{0,8},{1,9},{8,0},{9,1},{2,10},{3,11},{10,2},{11,3},{4,12},{5,13},... | collective-permute-start | bytes 1228808 | tf_op jit(solution)/shard_map/ppermute | solution.py:261
  33.0 28.9 %collective-permute-start.2 = (bf16[4,400,128]{2,1,0:T(8,128)(2,1)S(1)}, bf16[4,400,128]{2,1,0:T(8,128)(2,1)S(1)}, u32[]{:S(2)}, u32[]{:S(2)}) collective-permute-start(bf16[4,400,128]{2,1,0:T(8,128)(2,1)S(1)} %get-tuple-element.35), channel_id=1, source_target_pairs={{0,1},{1,0},{8,9},{9,8},{2,3},{3,2},{10,11},{11,10},{4,5},{5,4},{1... | collective-permute-start | bytes 1228808 | tf_op jit(solution)/shard_map/ppermute | solution.py:261
  39.1 22.8 %collective-permute-start.5 = (bf16[4,128,128]{2,1,0:T(8,128)(2,1)S(1)}, bf16[4,128,128]{2,1,0:T(8,128)(2,1)S(1)}, u32[]{:S(2)}, u32[]{:S(2)}) collective-permute-start(bf16[4,128,128]{2,1,0:T(8,128)(2,1)S(1)} %slice.8), channel_id=1, source_target_pairs={{0,2},{2,4},{4,6},{6,0},{1,3},{3,5},{5,7},{7,1},{8,10},{10,12},{12... | collective-permute-start | bytes 393224 | tf_op jit(solution)/shard_map/ppermute | solution.py:220
  41.0 20.9 %collective-permute-start.6 = (bf16[4,128,128]{2,1,0:T(8,128)(2,1)S(1)}, bf16[4,128,128]{2,1,0:T(8,128)(2,1)S(1)}, u32[]{:S(2)}, u32[]{:S(2)}) collective-permute-start(bf16[4,128,128]{2,1,0:T(8,128)(2,1)S(1)} %slice.9), channel_id=1, source_target_pairs={{0,6},{2,0},{4,2},{6,4},{1,7},{3,1},{5,3},{7,5},{8,14},{10,8},{12,... | collective-permute-start | bytes 393224 | tf_op jit(solution)/shard_map/ppermute | solution.py:220
  73.6 23.4 %all-to-all-start.1 = ((bf16[16,128,128]{2,1,0:T(8,128)(2,1)}), bf16[16,128,128]{2,1,0:T(8,128)(2,1)S(1)}, u32[]{:S(2)}, u32[]{:S(2)}) async-start(bf16[16,128,128]{2,1,0:T(8,128)(2,1)} %get-tuple-element.44), calls=%async_computation.1 | async-start | bytes 1048576 | tf_op jit(solution)/shard_map/all_to_all | solution.py:284
  82.0 8.1 %collective-permute-start.7 = (bf16[4,128,128]{2,1,0:T(8,128)(2,1)S(1)}, bf16[4,128,128]{2,1,0:T(8,128)(2,1)S(1)}, u32[]{:S(2)}, u32[]{:S(2)}) collective-permute-start(bf16[4,128,128]{2,1,0:T(8,128)(2,1)S(1)} %get-tuple-element.39), channel_id=1, source_target_pairs={{0,2},{2,4},{4,6},{6,0},{1,3},{3,5},{5,7},{7,1},{8,10},{10,12},{12... | collective-permute-start | bytes 393224 | tf_op jit(solution)/shard_map/ppermute | solution.py:220
  84.8 8.6 %collective-permute-start.8 = (bf16[4,128,128]{2,1,0:T(8,128)(2,1)S(1)}, bf16[4,128,128]{2,1,0:T(8,128)(2,1)S(1)}, u32[]{:S(2)}, u32[]{:S(2)}) collective-permute-start(bf16[4,128,128]{2,1,0:T(8,128)(2,1)S(1)} %get-tuple-element.41), channel_id=1, source_target_pairs={{0,6},{2,0},{4,2},{6,4},{1,7},{3,1},{5,3},{7,5},{8,14},{10,8},{12,... | collective-permute-start | bytes 393224 | tf_op jit(solution)/shard_map/ppermute | solution.py:220
  97.0 21.6 %collective-permute-start.11 = (f32[2,128,128]{2,1,0:T(8,128)S(1)}, f32[2,128,128]{2,1,0:T(8,128)S(1)}, u32[]{:S(2)}, u32[]{:S(2)}) collective-permute-start(f32[2,128,128]{2,1,0:T(8,128)S(1)} %convert_reduce_fusion), channel_id=1, source_target_pairs={{0,0},{1,32},{32,1},{33,33},{64,64},{65,96},{96,65},{97,97},{128,1... | collective-permute-start | bytes 393224 | tf_op jit(solution)/shard_map/ppermute | solution.py:290
  97.7 28.1 %collective-permute-start.9 = (bf16[4,256,128]{2,1,0:T(8,128)(2,1)S(1)}, bf16[4,256,128]{2,1,0:T(8,128)(2,1)S(1)}, u32[]{:S(2)}, u32[]{:S(2)}) collective-permute-start(bf16[4,256,128]{2,1,0:T(8,128)(2,1)S(1)} %get-tuple-element.49), channel_id=1, source_target_pairs={{0,2},{2,4},{4,6},{6,0},{1,3},{3,5},{5,7},{7,1},{8,10},{10,12},{12... | collective-permute-start | bytes 786440 | tf_op jit(solution)/shard_map/ppermute | solution.py:220
  100.2 25.5 %collective-permute-start.10 = (bf16[4,256,128]{2,1,0:T(8,128)(2,1)S(1)}, bf16[4,256,128]{2,1,0:T(8,128)(2,1)S(1)}, u32[]{:S(2)}, u32[]{:S(2)}) collective-permute-start(bf16[4,256,128]{2,1,0:T(8,128)(2,1)S(1)} %get-tuple-element.50), channel_id=1, source_target_pairs={{0,6},{2,0},{4,2},{6,4},{1,7},{3,1},{5,3},{7,5},{8,14},{10,8},{12,... | collective-permute-start | bytes 786440 | tf_op jit(solution)/shard_map/ppermute | solution.py:220
  105.7 16.3 %collective-permute-start.12 = (bf16[4,128,128]{2,1,0:T(8,128)(2,1)S(1)}, bf16[4,128,128]{2,1,0:T(8,128)(2,1)S(1)}, u32[]{:S(2)}, u32[]{:S(2)}) collective-permute-start(bf16[4,128,128]{2,1,0:T(8,128)(2,1)S(1)} %get-tuple-element.53), channel_id=1, source_target_pairs={{0,9},{1,8},{8,1},{9,0},{2,11},{3,10},{10,3},{11,2},{4,13},{5,12},... | collective-permute-start | bytes 393224 | tf_op jit(solution)/shard_map/ppermute | solution.py:287
  113.9 8.4 %collective-permute-start.13 = (bf16[4,128,128]{2,1,0:T(8,128)(2,1)S(1)}, bf16[4,128,128]{2,1,0:T(8,128)(2,1)S(1)}, u32[]{:S(2)}, u32[]{:S(2)}) collective-permute-start(bf16[4,128,128]{2,1,0:T(8,128)(2,1)S(1)} %get-tuple-element.54), channel_id=1, source_target_pairs={{0,8},{1,9},{8,0},{9,1},{2,10},{3,11},{10,2},{11,3},{4,12},{5,13},... | collective-permute-start | bytes 393224 | tf_op jit(solution)/shard_map/ppermute | solution.py:287
  118.6 7.2 %collective-permute-start.14 = (bf16[4,128,128]{2,1,0:T(8,128)(2,1)S(1)}, bf16[4,128,128]{2,1,0:T(8,128)(2,1)S(1)}, u32[]{:S(2)}, u32[]{:S(2)}) collective-permute-start(bf16[4,128,128]{2,1,0:T(8,128)(2,1)S(1)} %get-tuple-element.55), channel_id=1, source_target_pairs={{0,1},{1,0},{8,9},{9,8},{2,3},{3,2},{10,11},{11,10},{4,5},{5,4},{1... | collective-permute-start | bytes 393224 | tf_op jit(solution)/shard_map/ppermute | solution.py:287

commit v12 on v11

--- a/solution.py
+++ b/solution.py
@@ -282,8 +282,10 @@
         name="fold",
     )(up, up_more, down, down_more)
     db = lax.all_to_all(db_parts, ("z", "xh"), 0, 0)
-    up, down, db, dq_parts = lax.optimization_barrier((up, down, db, dq_parts))
-    for d in range(1, 4):
+    for d in (1,):
+        dq_parts[d] = lax.ppermute(dq_parts[d], ("xh", "yl"), [(n, n ^ FLIPS[d]) for n in range(4)])
+    up, down, dq_parts = lax.optimization_barrier((up, down, dq_parts))
+    for d in (2, 3):
         dq_parts[d] = lax.ppermute(dq_parts[d], ("xh", "yl"), [(n, n ^ FLIPS[d]) for n in range(4)])
     up, down = along(up, 1), along(down, -1)
     db = jnp.sum(db.reshape(8, 2, 128, 128).astype(F32), axis=0)

time: 142 us -> 144 us (1.014)
  the two profiles are of different devices: /device:TPU:1 before, /device:TPU:64 now
where the time goes in v12:
time: 144 us; the launch traced here: 143 us
  starting transfers between devices  75.8 us (53%)
  waiting for transfers between devices  38.7 us (27%)
  Pallas kernels  16.4 us (11%)
  blocking collectives  11.2 us (8%)
    ppermute x8, starting transfers between devices, along(): return lax.ppermute(value, 'yh', [(n, (n + steps) % 4) for n in range(4)])  31.9 us
    ppermute x8, waiting for transfers between devices, along(): return lax.ppermute(value, 'yh', [(n, (n + steps) % 4) for n in range(4)])  22.6 us
    ppermute x3, starting transfers between devices, body(): lax.ppermute(dq_parts[d], ('xh', 'yl'), [(n, n ^ FLIPS[d]) for n in range...  15.3 us
    all_to_all x1, starting transfers between devices, body(): db = lax.all_to_all(db_parts, ('z', 'xh'), 0, 0)  12.4 us
    pallas_call x1, Pallas kernels, body(): pl.pallas_call(functools.partial(attend_kernel, scale), out_shape=(shape(...  11.6 us
    all_to_all x1, blocking collectives, body(): joined = lax.all_to_all(joined, ('xl', 'c'), 0, 0)  11.2 us
    ppermute x3, starting transfers between devices, body(): lax.ppermute(pays[d], ('xh', 'yl'), [(n, n ^ FLIPS[d]) for n in range(4)])  10.7 us
    all_to_all x1, waiting for transfers between devices, body(): got = lax.all_to_all(packed, ('xl', 'c'), 0, 0)  8.06 us
  transfers between devices with their start and end apart: 17, of which 7 were waited for; matrix products, arithmetic and copies ran while one was open for 0% of the time, Pallas kernels for 1%

profile of v12, /device:TPU:64, one launch (start us, length us, event | category | flops | bytes accessed | tf_op | source)
XLA Modules:
  0.0 143.2 jit_solution(8434731411406372176)
XLA Ops:
  0.6 2.4 %pack.1 = bf16[4,528,128]{2,1,0:T(8,128)(2,1)} custom-call(bf16[4,128,128]{2,1,0:T(8,128)(2,1)} %k_hbm.1, bf16[4,128,128]{2,1,0:T(8,128)(2,1)} %v_hbm.1, bf16[4,128,128]{2,1,0:T(8,128)(2,1)} %q_hbm.1, bf16[4,128,128]{2,1,0:T(8,128)(2,1)} %g_hbm.1, bf16[4,128,128]{2,1,0:T(8,128)(2,1)} %o_hbm.1, f32[4,4,128]{2,1,0:T(4,128)} %l_hbm.1), custom_call_target="tpu_custom_call" | custom-call | tf_op jit(solution)/shard_map/pack/pallas_call | solution.py:231
  3.0 3.5 %all-to-all-start = ((bf16[4,528,128]{2,1,0:T(8,128)(2,1)}), bf16[4,528,128]{2,1,0:T(8,128)(2,1)S(1)}, u32[]{:S(2)}, u32[]{:S(2)}) async-start(bf16[4,528,128]{2,1,0:T(8,128)(2,1)} %pack.1), calls=%async_computation | async-start | bytes 1081344 | tf_op jit(solution)/shard_map/all_to_all | solution.py:250
  6.5 0.1 stack.27.where_ref
  6.6 0.8 bias.1.bias_ref
  7.5 8.1 %all-to-all-done.got_ref = bf16[4,528,128]{2,1,0:T(8,128)(2,1)S(1)} async-done(((bf16[4,528,128]{2,1,0:T(8,128)(2,1)}), bf16[4,528,128]{2,1,0:T(8,128)(2,1)S(1)}, u32[]{:S(2)}, u32[]{:S(2)}) %all-to-all-start) | async-done | bytes 540704 | tf_op jit(solution)/shard_map/all_to_all | solution.py:250
  15.5 0.2 assemble.1
  15.7 4.5 %collective-permute-start.4 = (bf16[4,272,128]{2,1,0:T(8,128)(2,1)S(1)}, bf16[4,272,128]{2,1,0:T(8,128)(2,1)S(1)}, u32[]{:S(2)}, u32[]{:S(2)}) collective-permute-start(bf16[4,272,128]{2,1,0:T(8,128)(2,1)S(1)} %get-tuple-element.35.kv0_ref), channel_id=1, source_target_pairs={{0,2},{2,4},{4,6},{6,0},{1,3},{3,5},{5,7},{7,1},{8,10},{10,12},{12... | collective-permute-start | bytes 835592 | tf_op jit(solution)/shard_map/ppermute | solution.py:220
  20.2 3.6 %collective-permute-start.3 = (bf16[4,272,128]{2,1,0:T(8,128)(2,1)S(1)}, bf16[4,272,128]{2,1,0:T(8,128)(2,1)S(1)}, u32[]{:S(2)}, u32[]{:S(2)}) collective-permute-start(bf16[4,272,128]{2,1,0:T(8,128)(2,1)S(1)} %get-tuple-element.35.kv0_ref), channel_id=1, source_target_pairs={{0,6},{2,0},{4,2},{6,4},{1,7},{3,1},{5,3},{7,5},{8,14},{10,8},{12,... | collective-permute-start | bytes 835592 | tf_op jit(solution)/shard_map/ppermute | solution.py:220
  23.8 5.8 %collective-permute-start = (bf16[4,400,128]{2,1,0:T(8,128)(2,1)S(1)}, bf16[4,400,128]{2,1,0:T(8,128)(2,1)S(1)}, u32[]{:S(2)}, u32[]{:S(2)}) collective-permute-start(bf16[4,400,128]{2,1,0:T(8,128)(2,1)S(1)} %get-tuple-element.32), channel_id=1, source_target_pairs={{0,9},{1,8},{8,1},{9,0},{2,11},{3,10},{10,3},{11,2},{4,13},{5,12},... | collective-permute-start | bytes 1228808 | tf_op jit(solution)/shard_map/ppermute | solution.py:261
  29.6 2.4 %collective-permute-start.1 = (bf16[4,400,128]{2,1,0:T(8,128)(2,1)S(1)}, bf16[4,400,128]{2,1,0:T(8,128)(2,1)S(1)}, u32[]{:S(2)}, u32[]{:S(2)}) collective-permute-start(bf16[4,400,128]{2,1,0:T(8,128)(2,1)S(1)} %get-tuple-element.33), channel_id=1, source_target_pairs={{0,8},{1,9},{8,0},{9,1},{2,10},{3,11},{10,2},{11,3},{4,12},{5,13},... | collective-permute-start | bytes 1228808 | tf_op jit(solution)/shard_map/ppermute | solution.py:261
  32.1 2.5 %collective-permute-start.2 = (bf16[4,400,128]{2,1,0:T(8,128)(2,1)S(1)}, bf16[4,400,128]{2,1,0:T(8,128)(2,1)S(1)}, u32[]{:S(2)}, u32[]{:S(2)}) collective-permute-start(bf16[4,400,128]{2,1,0:T(8,128)(2,1)S(1)} %get-tuple-element.34), channel_id=1, source_target_pairs={{0,1},{1,0},{8,9},{9,8},{2,3},{3,2},{10,11},{11,10},{4,5},{5,4},{1... | collective-permute-start | bytes 1228808 | tf_op jit(solution)/shard_map/ppermute | solution.py:261
  34.6 4.0 %collective-permute-start.5 = (bf16[4,128,128]{2,1,0:T(8,128)(2,1)S(1)}, bf16[4,128,128]{2,1,0:T(8,128)(2,1)S(1)}, u32[]{:S(2)}, u32[]{:S(2)}) collective-permute-start(bf16[4,128,128]{2,1,0:T(8,128)(2,1)S(1)} %slice.8), channel_id=1, source_target_pairs={{0,2},{2,4},{4,6},{6,0},{1,3},{3,5},{5,7},{7,1},{8,10},{10,12},{12... | collective-permute-start | bytes 393224 | tf_op jit(solution)/shard_map/ppermute | solution.py:220
  38.7 3.9 %collective-permute-start.6 = (bf16[4,128,128]{2,1,0:T(8,128)(2,1)S(1)}, bf16[4,128,128]{2,1,0:T(8,128)(2,1)S(1)}, u32[]{:S(2)}, u32[]{:S(2)}) collective-permute-start(bf16[4,128,128]{2,1,0:T(8,128)(2,1)S(1)} %slice.9), channel_id=1, source_target_pairs={{0,6},{2,0},{4,2},{6,4},{1,7},{3,1},{5,3},{7,5},{8,14},{10,8},{12,... | collective-permute-start | bytes 393224 | tf_op jit(solution)/shard_map/ppermute | solution.py:220
  42.6 15.1 %collective-permute-done.5.k2_ref = bf16[4,128,128]{2,1,0:T(8,128)(2,1)S(1)} collective-permute-done((bf16[4,128,128]{2,1,0:T(8,128)(2,1)S(1)}, bf16[4,128,128]{2,1,0:T(8,128)(2,1)S(1)}, u32[]{:S(2)}, u32[]{:S(2)}) %collective-permute-start.5) | collective-permute-done | bytes 131104 | tf_op jit(solution)/shard_map/ppermute | solution.py:220
  57.7 1.2 collective-permute-done.2.pay3_ref
  58.9 11.6 %attend.1 = (bf16[4,128,128]{2,1,0:T(8,128)(2,1)S(1)}, bf16[4,128,128]{2,1,0:T(8,128)(2,1)S(1)}, bf16[4,128,128]{2,1,0:T(8,128)(2,1)S(1)}, bf16[4,128,128]{2,1,0...) custom-call(s32[6]{0:T(128)S(1)} %stack.27.where_ref, ...), custom_call_target="tpu_custom_call" | custom-call | tf_op jit(solution)/shard_map/attend/pallas_call | solution.py:263
  70.5 12.4 %all-to-all-start.1 = ((bf16[16,128,128]{2,1,0:T(8,128)(2,1)}), bf16[16,128,128]{2,1,0:T(8,128)(2,1)S(1)}, u32[]{:S(2)}, u32[]{:S(2)}) async-start(bf16[16,128,128]{2,1,0:T(8,128)(2,1)} %get-tuple-element.49), calls=%async_computation.1 | async-start | bytes 1048576 | tf_op jit(solution)/shard_map/all_to_all | solution.py:284
  83.0 3.5 %collective-permute-start.7 = (bf16[4,128,128]{2,1,0:T(8,128)(2,1)S(1)}, bf16[4,128,128]{2,1,0:T(8,128)(2,1)S(1)}, u32[]{:S(2)}, u32[]{:S(2)}) collective-permute-start(bf16[4,128,128]{2,1,0:T(8,128)(2,1)S(1)} %get-tuple-element.38), channel_id=1, source_target_pairs={{0,2},{2,4},{4,6},{6,0},{1,3},{3,5},{5,7},{7,1},{8,10},{10,12},{12... | collective-permute-start | bytes 393224 | tf_op jit(solution)/shard_map/ppermute | solution.py:220
  86.5 4.4 %collective-permute-start.8 = (bf16[4,128,128]{2,1,0:T(8,128)(2,1)S(1)}, bf16[4,128,128]{2,1,0:T(8,128)(2,1)S(1)}, u32[]{:S(2)}, u32[]{:S(2)}) collective-permute-start(bf16[4,128,128]{2,1,0:T(8,128)(2,1)S(1)} %get-tuple-element.40), channel_id=1, source_target_pairs={{0,6},{2,0},{4,2},{6,4},{1,7},{3,1},{5,3},{7,5},{8,14},{10,8},{12,... | collective-permute-start | bytes 393224 | tf_op jit(solution)/shard_map/ppermute | solution.py:220
  90.9 7.4 %collective-permute-start.9 = (bf16[4,128,128]{2,1,0:T(8,128)(2,1)S(1)}, bf16[4,128,128]{2,1,0:T(8,128)(2,1)S(1)}, u32[]{:S(2)}, u32[]{:S(2)}) collective-permute-start(bf16[4,128,128]{2,1,0:T(8,128)(2,1)S(1)} %get-tuple-element.44), channel_id=1, source_target_pairs={{0,9},{1,8},{8,1},{9,0},{2,11},{3,10},{10,3},{11,2},{4,13},{5,12},... | collective-permute-start | bytes 393224 | tf_op jit(solution)/shard_map/ppermute | solution.py:286
  98.4 3.7 %collective-permute-done.9.dq1_ref = bf16[4,128,128]{2,1,0:T(8,128)(2,1)S(1)} collective-permute-done((bf16[4,128,128]{2,1,0:T(8,128)(2,1)S(1)}, bf16[4,128,128]{2,1,0:T(8,128)(2,1)S(1)}, u32[]{:S(2)}, u32[]{:S(2)}) %collective-permute-start.9) | collective-permute-done | bytes 131104 | tf_op jit(solution)/shard_map/ppermute | solution.py:286
  102.2 2.9 %collective-permute-start.13 = (bf16[4,128,128]{2,1,0:T(8,128)(2,1)S(1)}, bf16[4,128,128]{2,1,0:T(8,128)(2,1)S(1)}, u32[]{:S(2)}, u32[]{:S(2)}) collective-permute-start(bf16[4,128,128]{2,1,0:T(8,128)(2,1)S(1)} %get-tuple-element.52), channel_id=1, source_target_pairs={{0,8},{1,9},{8,0},{9,1},{2,10},{3,11},{10,2},{11,3},{4,12},{5,13},... | collective-permute-start | bytes 393224 | tf_op jit(solution)/shard_map/ppermute | solution.py:289
  105.1 5.0 %collective-permute-start.14 = (bf16[4,128,128]{2,1,0:T(8,128)(2,1)S(1)}, bf16[4,128,128]{2,1,0:T(8,128)(2,1)S(1)}, u32[]{:S(2)}, u32[]{:S(2)}) collective-permute-start(bf16[4,128,128]{2,1,0:T(8,128)(2,1)S(1)} %get-tuple-element.53), channel_id=1, source_target_pairs={{0,1},{1,0},{8,9},{9,8},{2,3},{3,2},{10,11},{11,10},{4,5},{5,4},{1... | collective-permute-start | bytes 393224 | tf_op jit(solution)/shard_map/ppermute | solution.py:289
  110.1 4.4 %collective-permute-start.10 = (bf16[4,256,128]{2,1,0:T(8,128)(2,1)S(1)}, bf16[4,256,128]{2,1,0:T(8,128)(2,1)S(1)}, u32[]{:S(2)}, u32[]{:S(2)}) collective-permute-start(bf16[4,256,128]{2,1,0:T(8,128)(2,1)S(1)} %get-tuple-element.47), channel_id=1, source_target_pairs={{0,2},{2,4},{4,6},{6,0},{1,3},{3,5},{5,7},{7,1},{8,10},{10,12},{12... | collective-permute-start | bytes 786440 | tf_op jit(solution)/shard_map/ppermute | solution.py:220
  114.5 3.6 %collective-permute-start.11 = (bf16[4,256,128]{2,1,0:T(8,128)(2,1)S(1)}, bf16[4,256,128]{2,1,0:T(8,128)(2,1)S(1)}, u32[]{:S(2)}, u32[]{:S(2)}) collective-permute-start(bf16[4,256,128]{2,1,0:T(8,128)(2,1)S(1)} %get-tuple-element.48), channel_id=1, source_target_pairs={{0,6},{2,0},{4,2},{6,4},{1,7},{3,1},{5,3},{7,5},{8,14},{10,8},{12,... | collective-permute-start | bytes 786440 | tf_op jit(solution)/shard_map/ppermute | solution.py:220
  118.1 1.9 %collective-permute-start.12 = (f32[2,128,128]{2,1,0:T(8,128)S(1)}, f32[2,128,128]{2,1,0:T(8,128)S(1)}, u32[]{:S(2)}, u32[]{:S(2)}) collective-permute-start(f32[2,128,128]{2,1,0:T(8,128)S(1)} %convert_reduce_fusion), channel_id=1, source_target_pairs={{0,0},{1,32},{32,1},{33,33},{64,64},{65,96},{96,65},{97,97},{128,1... | collective-permute-start | bytes 393224 | tf_op jit(solution)/shard_map/ppermute | solution.py:292
  120.1 5.3 %collective-permute-done.10.up_ref = bf16[4,256,128]{2,1,0:T(8,128)(2,1)S(1)} collective-permute-done((bf16[4,256,128]{2,1,0:T(8,128)(2,1)S(1)}, bf16[4,256,128]{2,1,0:T(8,128)(2,1)S(1)}, u32[]{:S(2)}, u32[]{:S(2)}) %collective-permute-start.10) | collective-permute-done | bytes 262176 | tf_op jit(solution)/shard_map/ppermute | solution.py:220
  125.4 2.2 %collective-permute-done.11.down_ref = bf16[4,256,128]{2,1,0:T(8,128)(2,1)S(1)} collective-permute-done((bf16[4,256,128]{2,1,0:T(8,128)(2,1)S(1)}, bf16[4,256,128]{2,1,0:T(8,128)(2,1)S(1)}, u32[]{:S(2)}, u32[]{:S(2)}) %collective-permute-start.11) | collective-permute-done | bytes 262176 | tf_op jit(solution)/shard_map/ppermute | solution.py:220
  127.6 3.1 %collective-permute-done.12.db_ref = f32[2,128,128]{2,1,0:T(8,128)S(1)} collective-permute-done((f32[2,128,128]{2,1,0:T(8,128)S(1)}, f32[2,128,128]{2,1,0:T(8,128)S(1)}, u32[]{:S(2)}, u32[]{:S(2)}) %collective-permute-start.12) | collective-permute-done | bytes 131104 | tf_op jit(solution)/shard_map/ppermute | solution.py:292
  130.7 0.2 join.1
  130.9 11.2 %all_to_all.15.got_ref = bf16[4,512,128]{2,1,0:T(8,128)(2,1)S(1)} all-to-all(bf16[4,512,128]{2,1,0:T(8,128)(2,1)S(1)} %join.1), channel_id=1, replica_groups=mesh['xl'=2,'z'=8,'c'=2,'xh'=2,'yh'=4,'yl'=2] {'xl','c'}, dimensions={0} | all-to-all | bytes 1048576 | tf_op jit(solution)/shard_map/all_to_all | solution.py:301
  142.2 1.1 unpack.1
  (16 shorter events, 0.2 us)
Async XLA Ops:
  0.6 6.0 %copy-start = (bf16[4,128,2048]{2,1,0:T(8,128)(2,1)S(1)}, bf16[4,128,2048]{2,1,0:T(8,128)(2,1)}, u32[]{:S(2)}) copy-start(bf16[4,128,2048]{2,1,0:T(8,128)(2,1)} %bias_hbm.1) | copy-start | bytes 6291460
  3.0 12.5 %all-to-all-start = ((bf16[4,528,128]{2,1,0:T(8,128)(2,1)}), bf16[4,528,128]{2,1,0:T(8,128)(2,1)S(1)}, u32[]{:S(2)}, u32[]{:S(2)}) async-start(bf16[4,528,128]{2,1,0:T(8,128)(2,1)} %pack.1), calls=%async_computation | async-start | bytes 1081344 | tf_op jit(solution)/shard_map/all_to_all | solution.py:250
  15.7 18.8 %collective-permute-start.4 = (bf16[4,272,128]{2,1,0:T(8,128)(2,1)S(1)}, bf16[4,272,128]{2,1,0:T(8,128)(2,1)S(1)}, u32[]{:S(2)}, u32[]{:S(2)}) collective-permute-start(bf16[4,272,128]{2,1,0:T(8,128)(2,1)S(1)} %get-tuple-element.35.kv0_ref), channel_id=1, source_target_pairs={{0,2},{2,4},{4,6},{6,0},{1,3},{3,5},{5,7},{7,1},{8,10},{10,12},{12... | collective-permute-start | bytes 835592 | tf_op jit(solution)/shard_map/ppermute | solution.py:220
  20.2 18.4 %collective-permute-start.3 = (bf16[4,272,128]{2,1,0:T(8,128)(2,1)S(1)}, bf16[4,272,128]{2,1,0:T(8,128)(2,1)S(1)}, u32[]{:S(2)}, u32[]{:S(2)}) collective-permute-start(bf16[4,272,128]{2,1,0:T(8,128)(2,1)S(1)} %get-tuple-element.35.kv0_ref), channel_id=1, source_target_pairs={{0,6},{2,0},{4,2},{6,4},{1,7},{3,1},{5,3},{7,5},{8,14},{10,8},{12,... | collective-permute-start | bytes 835592 | tf_op jit(solution)/shard_map/ppermute | solution.py:220
  23.8 33.9 %collective-permute-start = (bf16[4,400,128]{2,1,0:T(8,128)(2,1)S(1)}, bf16[4,400,128]{2,1,0:T(8,128)(2,1)S(1)}, u32[]{:S(2)}, u32[]{:S(2)}) collective-permute-start(bf16[4,400,128]{2,1,0:T(8,128)(2,1)S(1)} %get-tuple-element.32), channel_id=1, source_target_pairs={{0,9},{1,8},{8,1},{9,0},{2,11},{3,10},{10,3},{11,2},{4,13},{5,12},... | collective-permute-start | bytes 1228808 | tf_op jit(solution)/shard_map/ppermute | solution.py:261
  29.6 28.1 %collective-permute-start.1 = (bf16[4,400,128]{2,1,0:T(8,128)(2,1)S(1)}, bf16[4,400,128]{2,1,0:T(8,128)(2,1)S(1)}, u32[]{:S(2)}, u32[]{:S(2)}) collective-permute-start(bf16[4,400,128]{2,1,0:T(8,128)(2,1)S(1)} %get-tuple-element.33), channel_id=1, source_target_pairs={{0,8},{1,9},{8,0},{9,1},{2,10},{3,11},{10,2},{11,3},{4,12},{5,13},... | collective-permute-start | bytes 1228808 | tf_op jit(solution)/shard_map/ppermute | solution.py:261
  32.1 26.9 %collective-permute-start.2 = (bf16[4,400,128]{2,1,0:T(8,128)(2,1)S(1)}, bf16[4,400,128]{2,1,0:T(8,128)(2,1)S(1)}, u32[]{:S(2)}, u32[]{:S(2)}) collective-permute-start(bf16[4,400,128]{2,1,0:T(8,128)(2,1)S(1)} %get-tuple-element.34), channel_id=1, source_target_pairs={{0,1},{1,0},{8,9},{9,8},{2,3},{3,2},{10,11},{11,10},{4,5},{5,4},{1... | collective-permute-start | bytes 1228808 | tf_op jit(solution)/shard_map/ppermute | solution.py:261
  34.6 23.1 %collective-permute-start.5 = (bf16[4,128,128]{2,1,0:T(8,128)(2,1)S(1)}, bf16[4,128,128]{2,1,0:T(8,128)(2,1)S(1)}, u32[]{:S(2)}, u32[]{:S(2)}) collective-permute-start(bf16[4,128,128]{2,1,0:T(8,128)(2,1)S(1)} %slice.8), channel_id=1, source_target_pairs={{0,2},{2,4},{4,6},{6,0},{1,3},{3,5},{5,7},{7,1},{8,10},{10,12},{12... | collective-permute-start | bytes 393224 | tf_op jit(solution)/shard_map/ppermute | solution.py:220
  38.7 19.1 %collective-permute-start.6 = (bf16[4,128,128]{2,1,0:T(8,128)(2,1)S(1)}, bf16[4,128,128]{2,1,0:T(8,128)(2,1)S(1)}, u32[]{:S(2)}, u32[]{:S(2)}) collective-permute-start(bf16[4,128,128]{2,1,0:T(8,128)(2,1)S(1)} %slice.9), channel_id=1, source_target_pairs={{0,6},{2,0},{4,2},{6,4},{1,7},{3,1},{5,3},{7,5},{8,14},{10,8},{12,... | collective-permute-start | bytes 393224 | tf_op jit(solution)/shard_map/ppermute | solution.py:220
  70.5 47.5 %all-to-all-start.1 = ((bf16[16,128,128]{2,1,0:T(8,128)(2,1)}), bf16[16,128,128]{2,1,0:T(8,128)(2,1)S(1)}, u32[]{:S(2)}, u32[]{:S(2)}) async-start(bf16[16,128,128]{2,1,0:T(8,128)(2,1)} %get-tuple-element.49), calls=%async_computation.1 | async-start | bytes 1048576 | tf_op jit(solution)/shard_map/all_to_all | solution.py:284
  83.0 15.4 %collective-permute-start.7 = (bf16[4,128,128]{2,1,0:T(8,128)(2,1)S(1)}, bf16[4,128,128]{2,1,0:T(8,128)(2,1)S(1)}, u32[]{:S(2)}, u32[]{:S(2)}) collective-permute-start(bf16[4,128,128]{2,1,0:T(8,128)(2,1)S(1)} %get-tuple-element.38), channel_id=1, source_target_pairs={{0,2},{2,4},{4,6},{6,0},{1,3},{3,5},{5,7},{7,1},{8,10},{10,12},{12... | collective-permute-start | bytes 393224 | tf_op jit(solution)/shard_map/ppermute | solution.py:220
  86.5 11.9 %collective-permute-start.8 = (bf16[4,128,128]{2,1,0:T(8,128)(2,1)S(1)}, bf16[4,128,128]{2,1,0:T(8,128)(2,1)S(1)}, u32[]{:S(2)}, u32[]{:S(2)}) collective-permute-start(bf16[4,128,128]{2,1,0:T(8,128)(2,1)S(1)} %get-tuple-element.40), channel_id=1, source_target_pairs={{0,6},{2,0},{4,2},{6,4},{1,7},{3,1},{5,3},{7,5},{8,14},{10,8},{12,... | collective-permute-start | bytes 393224 | tf_op jit(solution)/shard_map/ppermute | solution.py:220
  90.9 11.2 %collective-permute-start.9 = (bf16[4,128,128]{2,1,0:T(8,128)(2,1)S(1)}, bf16[4,128,128]{2,1,0:T(8,128)(2,1)S(1)}, u32[]{:S(2)}, u32[]{:S(2)}) collective-permute-start(bf16[4,128,128]{2,1,0:T(8,128)(2,1)S(1)} %get-tuple-element.44), channel_id=1, source_target_pairs={{0,9},{1,8},{8,1},{9,0},{2,11},{3,10},{10,3},{11,2},{4,13},{5,12},... | collective-permute-start | bytes 393224 | tf_op jit(solution)/shard_map/ppermute | solution.py:286
  102.2 17.9 %collective-permute-start.13 = (bf16[4,128,128]{2,1,0:T(8,128)(2,1)S(1)}, bf16[4,128,128]{2,1,0:T(8,128)(2,1)S(1)}, u32[]{:S(2)}, u32[]{:S(2)}) collective-permute-start(bf16[4,128,128]{2,1,0:T(8,128)(2,1)S(1)} %get-tuple-element.52), channel_id=1, source_target_pairs={{0,8},{1,9},{8,0},{9,1},{2,10},{3,11},{10,2},{11,3},{4,12},{5,13},... | collective-permute-start | bytes 393224 | tf_op jit(solution)/shard_map/ppermute | solution.py:289
  105.1 15.0 %collective-permute-start.14 = (bf16[4,128,128]{2,1,0:T(8,128)(2,1)S(1)}, bf16[4,128,128]{2,1,0:T(8,128)(2,1)S(1)}, u32[]{:S(2)}, u32[]{:S(2)}) collective-permute-start(bf16[4,128,128]{2,1,0:T(8,128)(2,1)S(1)} %get-tuple-element.53), channel_id=1, source_target_pairs={{0,1},{1,0},{8,9},{9,8},{2,3},{3,2},{10,11},{11,10},{4,5},{5,4},{1... | collective-permute-start | bytes 393224 | tf_op jit(solution)/shard_map/ppermute | solution.py:289
  110.1 15.3 %collective-permute-start.10 = (bf16[4,256,128]{2,1,0:T(8,128)(2,1)S(1)}, bf16[4,256,128]{2,1,0:T(8,128)(2,1)S(1)}, u32[]{:S(2)}, u32[]{:S(2)}) collective-permute-start(bf16[4,256,128]{2,1,0:T(8,128)(2,1)S(1)} %get-tuple-element.47), channel_id=1, source_target_pairs={{0,2},{2,4},{4,6},{6,0},{1,3},{3,5},{5,7},{7,1},{8,10},{10,12},{12... | collective-permute-start | bytes 786440 | tf_op jit(solution)/shard_map/ppermute | solution.py:220
  114.5 13.1 %collective-permute-start.11 = (bf16[4,256,128]{2,1,0:T(8,128)(2,1)S(1)}, bf16[4,256,128]{2,1,0:T(8,128)(2,1)S(1)}, u32[]{:S(2)}, u32[]{:S(2)}) collective-permute-start(bf16[4,256,128]{2,1,0:T(8,128)(2,1)S(1)} %get-tuple-element.48), channel_id=1, source_target_pairs={{0,6},{2,0},{4,2},{6,4},{1,7},{3,1},{5,3},{7,5},{8,14},{10,8},{12,... | collective-permute-start | bytes 786440 | tf_op jit(solution)/shard_map/ppermute | solution.py:220
  118.1 12.6 %collective-permute-start.12 = (f32[2,128,128]{2,1,0:T(8,128)S(1)}, f32[2,128,128]{2,1,0:T(8,128)S(1)}, u32[]{:S(2)}, u32[]{:S(2)}) collective-permute-start(f32[2,128,128]{2,1,0:T(8,128)S(1)} %convert_reduce_fusion), channel_id=1, source_target_pairs={{0,0},{1,32},{32,1},{33,33},{64,64},{65,96},{96,65},{97,97},{128,1... | collective-permute-start | bytes 393224 | tf_op jit(solution)/shard_map/ppermute | solution.py:292
